TPU v7x, 32 devices: a whole 2x2x4 slice. The times are simulated.
32 devices in a mesh: fsdp: 4 (over z), win: 8 (over y, x, core).
Axes of the slice: x: 2, y: 2, z: 4, core: 2. Of those that a mesh axis runs over, the one named last changes fastest.
Arguments:
- tokens: bfloat16 [512, 100, 512], P(('fsdp', 'win')), may hold values from -6 to 6
- live: int32 [32], P(('fsdp', 'win')), may hold values from 8 to 16, as said below
- vectors: float32 [8, 512], P(None, ('fsdp', 'win'))
- fc1_bias: float32 [2048], P(('fsdp', 'win')), may hold values from -1.8 to 1.8
- w_qkv: bfloat16 [512, 1536], P('win', 'fsdp'), may hold values from -0.25 to 0.25
- w_proj: bfloat16 [512, 512], P('win', 'fsdp'), may hold values from -0.5 to 0.5
- w_fc1: bfloat16 [512, 2048], P('win', 'fsdp'), may hold values from -0.25 to 0.25
- w_fc2: bfloat16 [2048, 512], P('win', 'fsdp'), may hold values from -0.125 to 0.125
- rel_table: float32 [361, 16], replicated, may hold values from -5 to 5
- cotangent: bfloat16 [512, 100, 512], P(('fsdp', 'win')), may hold values from -6 to 6
Outputs:
- block_out: bfloat16 [512, 100, 512], P(('fsdp', 'win'))
- grad_tokens: bfloat16 [512, 100, 512], P(('fsdp', 'win'))
- grad_vectors: float32 [8, 512], P(None, ('fsdp', 'win'))
- grad_fc1_bias: float32 [2048], P(('fsdp', 'win'))
- grad_qkv: float32 [512, 1536], P('win', 'fsdp')
- grad_proj: float32 [512, 512], P('win', 'fsdp')
- grad_fc1: float32 [512, 2048], P('win', 'fsdp')
- grad_fc2: float32 [2048, 512], P('win', 'fsdp')
- grad_table: float32 [361, 16], replicated
Inputs may be any that keep to these rules, and one draw needn't show every extreme that they name: Every device has at least half of its 16 slots live, and some device has all of them live.
All inputs are finite; a program needn't handle non-finite values.
Results may differ from a plain program's by a relative error of at most 0.017.
Values may be sent and summed in bfloat16 or wider, within the bound.
No kernel may reach another device: no remote copies, remote signals or barrier semaphores. Data moves between devices by JAX's collectives and lax.ppermute only.
A program may use at most 192 MiB of HBM per device.

v0:
```python
import jax
import jax.numpy as jnp
from jax import lax
from jax.sharding import PartitionSpec as P

HEADS = 16
HD = 32
WS = 10


NORM_EPS = 1e-05
HIGH = lax.Precision.HIGHEST


def layer_norm(values, gain, shift):
    centre = values - jnp.mean(values, -1, keepdims=True)
    spread = jnp.mean(centre * centre, -1, keepdims=True)
    return centre * lax.rsqrt(spread + NORM_EPS) * gain + shift


def offset_onehot(side):
    place = jnp.arange(side)
    offset = place[:, None] - place[None, :] + side - 1
    return (offset[:, :, None] == jnp.arange(2 * side - 1)[None, None, :]).astype(jnp.float32)


def gather_weights(pieces):
    section = (
        lax.all_gather(pieces[0], "fsdp", axis=1, tiled=True),
        lax.all_gather(pieces[1], "fsdp", axis=1, tiled=True),
        lax.all_gather(pieces[2], "fsdp", axis=1, tiled=True),
        lax.all_gather(pieces[3], "fsdp", axis=1, tiled=True),
    )
    return (
        lax.all_gather(section[0], "win", axis=0, tiled=True),
        lax.all_gather(section[1], "win", axis=0, tiled=True),
        lax.all_gather(section[2], "win", axis=0, tiled=True),
        lax.all_gather(section[3], "win", axis=0, tiled=True),
    )


def body(tokens, live, vectors, fc1_bias, w_qkv, w_proj, w_fc1, w_fc2, rel_table, cotangent):
    f32 = jnp.float32
    bf16 = jnp.bfloat16
    win_count, win_tokens, width = tokens.shape
    tok_rows = win_count * win_tokens
    q_scale = HD ** (-0.5)
    full_qkv, full_proj, full_one, full_two = gather_weights((w_qkv, w_proj, w_fc1, w_fc2))
    vec_all, bias_one = (
        lax.all_gather(vectors, ("fsdp", "win"), axis=1, tiled=True),
        lax.all_gather(fc1_bias, ("fsdp", "win"), axis=0, tiled=True),
    )
    slot_live = (jnp.arange(win_count) < live[0]).astype(f32)
    row_mask = (slot_live[:, None] * jnp.ones((1, win_tokens), f32)).reshape(tok_rows, 1)
    inputs = tokens.astype(f32).reshape(tok_rows, width)
    norm_one, pull_one = jax.vjp(layer_norm, inputs, vec_all[0], vec_all[1])
    norm_one_low = norm_one.astype(bf16)
    mixed = jnp.dot(norm_one_low, full_qkv, preferred_element_type=f32)
    query_low = (
        ((mixed[:, :width] + vec_all[2]) * q_scale)
        .astype(bf16)
        .reshape(win_count, win_tokens, HEADS, HD)
    )
    key_low = mixed[:, width : 2 * width].astype(bf16).reshape(win_count, win_tokens, HEADS, HD)
    value_low = (
        (mixed[:, 2 * width :] + vec_all[3]).astype(bf16).reshape(win_count, win_tokens, HEADS, HD)
    )
    onehot_side = offset_onehot(WS)
    table_grid = rel_table.reshape(2 * WS - 1, 2 * WS - 1, HEADS)
    pos_bias = jnp.einsum(
        "ija,klb,abh->hikjl", onehot_side, onehot_side, table_grid, precision=HIGH
    ).reshape(HEADS, win_tokens, win_tokens)
    scores = (
        jnp.einsum("cqhd,ckhd->chqk", query_low, key_low, preferred_element_type=f32)
        + pos_bias[None]
    )
    probs = jax.nn.softmax(scores, axis=-1)
    probs_low = probs.astype(bf16)
    attended = jnp.einsum("chqk,ckhd->cqhd", probs_low, value_low, preferred_element_type=f32)
    attended_low = attended.reshape(tok_rows, width).astype(bf16)
    after_att = inputs + jnp.dot(attended_low, full_proj, preferred_element_type=f32) + vec_all[4]
    norm_two, pull_two = jax.vjp(layer_norm, after_att, vec_all[5], vec_all[6])
    norm_two_low = norm_two.astype(bf16)
    upper = jnp.dot(norm_two_low, full_one, preferred_element_type=f32) + bias_one
    activated, pull_act = jax.vjp(jax.nn.gelu, upper)
    act_low = activated.astype(bf16)
    result = after_att + jnp.dot(act_low, full_two, preferred_element_type=f32) + vec_all[7]
    block_out = (result * row_mask).astype(bf16).reshape(tokens.shape)
    section_again = (
        lax.all_gather(w_qkv, "fsdp", axis=1, tiled=True),
        lax.all_gather(w_proj, "fsdp", axis=1, tiled=True),
        lax.all_gather(w_fc1, "fsdp", axis=1, tiled=True),
        lax.all_gather(w_fc2, "fsdp", axis=1, tiled=True),
    )
    back_qkv, back_proj, back_one, back_two = (
        lax.all_gather(section_again[0], "win", axis=0, tiled=True),
        lax.all_gather(section_again[1], "win", axis=0, tiled=True),
        lax.all_gather(section_again[2], "win", axis=0, tiled=True),
        lax.all_gather(section_again[3], "win", axis=0, tiled=True),
    )
    grad_out = cotangent.astype(f32).reshape(tok_rows, width) * row_mask
    grad_out_low = grad_out.astype(bf16)
    grad_two = jnp.einsum("rf,rd->fd", act_low, grad_out_low, preferred_element_type=f32)
    grad_bias_two = jnp.sum(grad_out_low.astype(f32), 0)
    grad_act = jnp.einsum("rd,fd->rf", grad_out_low, back_two, preferred_element_type=f32)
    (grad_upper,) = pull_act(grad_act)
    grad_upper_low = grad_upper.astype(bf16)
    grad_one = jnp.einsum("rd,rf->df", norm_two_low, grad_upper_low, preferred_element_type=f32)
    grad_bias_one = jnp.sum(grad_upper_low.astype(f32), 0)
    grad_norm_two = jnp.einsum("rf,df->rd", grad_upper_low, back_one, preferred_element_type=f32)
    grad_after_norm, grad_gain_two, grad_shift_two = pull_two(grad_norm_two)
    grad_after = grad_out + grad_after_norm
    grad_after_low = grad_after.astype(bf16)
    grad_proj = jnp.einsum("rd,re->de", attended_low, grad_after_low, preferred_element_type=f32)
    grad_bias_proj = jnp.sum(grad_after_low.astype(f32), 0)
    grad_att = jnp.einsum("re,de->rd", grad_after_low, back_proj, preferred_element_type=f32)
    grad_att_low = grad_att.astype(bf16).reshape(win_count, win_tokens, HEADS, HD)
    grad_probs = jnp.einsum("cqhd,ckhd->chqk", grad_att_low, value_low, preferred_element_type=f32)
    grad_value = jnp.einsum("chqk,cqhd->ckhd", probs_low, grad_att_low, preferred_element_type=f32)
    grad_scores = probs * (grad_probs - jnp.sum(probs * grad_probs, -1, keepdims=True))
    grad_scores_low = grad_scores.astype(bf16)
    grad_query = jnp.einsum("chqk,ckhd->cqhd", grad_scores_low, key_low, preferred_element_type=f32)
    grad_key = jnp.einsum("chqk,cqhd->ckhd", grad_scores_low, query_low, preferred_element_type=f32)
    score_total = jnp.sum(grad_scores_low.astype(f32), 0).reshape(HEADS, WS, WS, WS, WS)
    grad_grid = jnp.einsum(
        "ija,klb,hikjl->abh", onehot_side, onehot_side, score_total, precision=HIGH
    )
    grad_table = grad_grid.reshape((2 * WS - 1) * (2 * WS - 1), HEADS)
    grad_mixed = jnp.concatenate(
        [
            grad_query.reshape(tok_rows, width).astype(bf16),
            grad_key.reshape(tok_rows, width).astype(bf16),
            grad_value.reshape(tok_rows, width).astype(bf16),
        ],
        axis=1,
    )
    column_scale = jnp.concatenate([jnp.full((width,), q_scale, f32), jnp.ones((2 * width,), f32)])
    grad_qkv = (
        jnp.einsum("rd,re->de", norm_one_low, grad_mixed, preferred_element_type=f32) * column_scale
    )
    grad_bias_query = jnp.sum(grad_mixed[:, :width].astype(f32), 0) * q_scale
    grad_bias_value = jnp.sum(grad_mixed[:, 2 * width :].astype(f32), 0)
    grad_norm_one = jnp.einsum(
        "re,de->rd", grad_mixed[:, :width], back_qkv[:, :width], preferred_element_type=f32
    ) * q_scale + jnp.einsum(
        "re,de->rd", grad_mixed[:, width:], back_qkv[:, width:], preferred_element_type=f32
    )
    grad_in_norm, grad_gain_one, grad_shift_one = pull_one(grad_norm_one)
    grad_tokens = (grad_after + grad_in_norm).astype(bf16).reshape(tokens.shape)
    grad_vec_local = jnp.stack(
        [
            grad_gain_one,
            grad_shift_one,
            grad_bias_query,
            grad_bias_value,
            grad_bias_proj,
            grad_gain_two,
            grad_shift_two,
            grad_bias_two,
        ]
    )
    weight_grads = (grad_qkv, grad_proj, grad_one, grad_two)
    row_parts = (
        lax.psum_scatter(
            weight_grads[0].astype(jnp.bfloat16), "win", scatter_dimension=0, tiled=True
        ).astype(jnp.float32),
        lax.psum_scatter(
            weight_grads[1].astype(jnp.bfloat16), "win", scatter_dimension=0, tiled=True
        ).astype(jnp.float32),
        lax.psum_scatter(
            weight_grads[2].astype(jnp.bfloat16), "win", scatter_dimension=0, tiled=True
        ).astype(jnp.float32),
        lax.psum_scatter(
            weight_grads[3].astype(jnp.bfloat16), "win", scatter_dimension=0, tiled=True
        ).astype(jnp.float32),
    )
    owned = (
        lax.psum_scatter(
            row_parts[0].astype(jnp.bfloat16), "fsdp", scatter_dimension=1, tiled=True
        ).astype(jnp.float32),
        lax.psum_scatter(
            row_parts[1].astype(jnp.bfloat16), "fsdp", scatter_dimension=1, tiled=True
        ).astype(jnp.float32),
        lax.psum_scatter(
            row_parts[2].astype(jnp.bfloat16), "fsdp", scatter_dimension=1, tiled=True
        ).astype(jnp.float32),
        lax.psum_scatter(
            row_parts[3].astype(jnp.bfloat16), "fsdp", scatter_dimension=1, tiled=True
        ).astype(jnp.float32),
    )
    grad_vectors, grad_fc1_bias = (
        lax.psum_scatter(grad_vec_local, ("fsdp", "win"), scatter_dimension=1, tiled=True),
        lax.psum_scatter(grad_bias_one, ("fsdp", "win"), scatter_dimension=0, tiled=True),
    )
    grad_table_all = lax.psum(grad_table, ("fsdp", "win"))
    return (
        block_out,
        grad_tokens,
        grad_vectors,
        grad_fc1_bias,
        owned[0],
        owned[1],
        owned[2],
        owned[3],
        grad_table_all,
    )


def solution(mesh):
    return jax.shard_map(
        body,
        mesh=mesh,
        in_specs=(
            P(("fsdp", "win"), None, None),
            P(("fsdp", "win")),
            P(None, ("fsdp", "win")),
            P(("fsdp", "win")),
            P("win", "fsdp"),
            P("win", "fsdp"),
            P("win", "fsdp"),
            P("win", "fsdp"),
            P(),
            P(("fsdp", "win"), None, None),
        ),
        out_specs=(
            P(("fsdp", "win"), None, None),
            P(("fsdp", "win"), None, None),
            P(None, ("fsdp", "win")),
            P(("fsdp", "win")),
            P("win", "fsdp"),
            P("win", "fsdp"),
            P("win", "fsdp"),
            P("win", "fsdp"),
            P(),
        ),
        check_vma=False,
    )
```

profile of v0, /device:TPU:0, one launch (start us, length us, event | category | flops | bytes accessed | tf_op | source)
XLA Modules:
  0.0 775.6 jit_solution(15727152391180003152)
XLA Ops:
  7.2 17.4 %all_gather.39 = bf16[64,1536]{1,0:T(8,128)(2,1)} all-gather(bf16[64,384]{1,0:T(8,128)(2,1)} %param.14), channel_id=1, replica_groups=mesh['fsdp'=4,'win'=8] {'fsdp'}, dimensions={1}, use_global_device_ids=true | all-gather | bytes 245760 | tf_op jit(solution)/shard_map/all_gather | solution.py:29
  24.7 15.3 %all_gather.43 = bf16[64,2048]{1,0:T(8,128)(2,1)} all-gather(bf16[64,512]{1,0:T(8,128)(2,1)} %param.16), channel_id=1, replica_groups=mesh['fsdp'=4,'win'=8] {'fsdp'}, dimensions={1}, use_global_device_ids=true | all-gather | bytes 327680 | tf_op jit(solution)/shard_map/all_gather | solution.py:31
  40.1 13.8 %all_gather.46 = bf16[256,512]{1,0:T(8,128)(2,1)} all-gather(bf16[256,128]{1,0:T(8,128)(2,1)} %param.17), channel_id=1, replica_groups=mesh['fsdp'=4,'win'=8] {'fsdp'}, dimensions={1}, use_global_device_ids=true | all-gather | bytes 327680 | tf_op jit(solution)/shard_map/all_gather | solution.py:32
  59.9 39.3 %all-reduce = f32[2048]{0:T(1024)S(1)} all-reduce(f32[2048]{0:T(1024)S(1)} %dynamic-update-slice), channel_id=1, replica_groups=mesh['fsdp'=4,'win'=8] {'fsdp','win'}, use_global_device_ids=true, to_apply=%add | all-reduce | flops 2048 | bytes 16384
  100.3 12.0 %all_gather.41 = bf16[64,512]{1,0:T(8,128)(2,1)S(1)} all-gather(bf16[64,128]{1,0:T(8,128)(2,1)S(1)} %copy-done.25), channel_id=1, replica_groups=mesh['fsdp'=4,'win'=8] {'fsdp'}, dimensions={1}, use_global_device_ids=true | all-gather | bytes 81920 | tf_op jit(solution)/shard_map/all_gather | solution.py:30
  112.3 39.0 %all-gather = f32[32,16,8]{1,2,0:T(8,128)S(1)} all-gather(f32[1,16,8]{1,2,0:T(8,128)S(1)} %bitcast.140), channel_id=1, replica_groups=mesh['fsdp'=4,'win'=8] {'fsdp','win'}, dimensions={0}, use_global_device_ids=true | all-gather | bytes 16896 | tf_op jit(solution)/shard_map/all_gather | solution.py:50
  152.3 9.9 %all_gather.42 = bf16[512,512]{1,0:T(8,128)(2,1)} all-gather(bf16[64,512]{1,0:T(8,128)(2,1)S(1)} %all_gather.41), channel_id=1, replica_groups=mesh['fsdp'=4,'win'=8] {'win'}, dimensions={0}, use_global_device_ids=true | all-gather | bytes 589824 | tf_op jit(solution)/shard_map/all_gather | solution.py:36
  178.6 18.5 %copy.139 = f32[16,10,10,10,10]{2,1,4,3,0:T(8,128)} copy(f32[16,10,10,10,10]{4,0,2,3,1:T(8,128)} %convolution_bitcast_fusion) | data formatting | bytes 1280000 | tf_op jit(solution)/shard_map/add | solution.py:74
  244.2 10.9 %fusion.48 = f32[16,16,100,100]{2,3,1,0:T(8,128)} fusion(bf16[16,100,16,32]{1,0,3,2:T(8,128)(2,1)} %reshape.195, bf16[16,100,16,32]{1,0,3,2:T(8,128)(2,1)} %reshape.194), kind=kOutput, calls=%fused_computation.79 | convolution fusion | flops 163840000 | bytes 13516800 | tf_op jit(solution)/shard_map/cqhd,ckhd->chqk/dot_general | solution.py:74
  255.1 18.2 %fusion.76 = (f32[16,16,100]{2,1,0:T(8,128)S(1)}, f32[16,16,100,100]{2,3,1,0:T(8,128)}) fusion(f32[16,16,100,100]{2,3,1,0:T(8,128)} %fusion.48, f32[16,100,100]{1,2,0:T(8,128)} %reshape.218), kind=kOutput, calls=%fused_computation.120 | output fusion | flops 10240099 | bytes 21222400 | tf_op jit(solution)/shard_map/sub | solution.py:77
  293.7 12.6 %multiply_convert_fusion.1 = (bf16[1600,2048]{1,0:T(8,128)(2,1)}, f32[1600,2048]{1,0:T(8,128)}) fusion(f32[2048]{0:T(1024)S(1)} %all-reduce, bf16[512,2048]{1,0:T(8,128)(2,1)} %all-gather.7.cloned.1.call-done, f32[1600,512]{1,0:T(8,128)} %copy-done, f32[512]{0:T(512)S(1)} %bitcast.142, f32[512]{0:T(512)S(1)} %bitcast.133, f32[1600]{0:T(1024)S(1)} %fusion.66, ...), kind=kOutput, calls=%fused_computation.15 | convolution fusion | flops 3392307200 | bytes 25059840 | tf_op jit(solution)/shard_map/dot_general | solution.py:84
  306.3 15.7 %convert_reduce_fusion.1 = (f32[2048]{0:T(1024)S(1)}, bf16[1600,2048]{1,0:T(8,128)(2,1)S(1)}) fusion(f32[1600,2048]{1,0:T(8,128)} %get-tuple-element.76, f32[2048]{0:T(1024)S(1)} %all-reduce, bf16[2048,512]{1,0:T(8,128)(2,1)} %all-gather.9.cloned.1.call-done, f32[1600,512]{1,0:T(8,128)} %reshape.198, f32[1600]{0:T(1024)S(1)} %mul.235), kind=kOutput, calls=%fused_computation.14 | convolution fusion | flops 3432445952 | bytes 25057536 | tf_op jit(solution)/shard_map/rd,fd->rf/dot_general | solution.py:105
  347.9 10.7 %convert_reduce_fusion.2 = (f32[16,32]{1,0:T(8,128)S(1)}, bf16[16,16,32,100]{3,2,1,0:T(8,128)(2,1)}) fusion(f32[16,16,100,100]{2,3,1,0:T(8,128)} %get-tuple-element.72, f32[16,16,100]{2,1,0:T(8,128)S(1)} %get-tuple-element.71, bf16[16,100,16,32]{1,0,3,2:T(8,128)(2,1)} %reshape.199), kind=kOutput, calls=%fused_computation.28 | convolution fusion | flops 171417088 | bytes 13621248 | tf_op jit(solution)/shard_map/chqk,cqhd->ckhd/dot_general | solution.py:119
  358.6 9.9 %multiply_reduce_fusion = (f32[16,16,100]{2,1,0:T(8,128)S(1)}, f32[16,16,100,100]{2,3,1,0:T(8,128)}) fusion(f32[16,16,100,100]{2,3,1,0:T(8,128)} %get-tuple-element.72, f32[16,16,100]{2,1,0:T(8,128)S(1)} %get-tuple-element.71, bf16[16,100,16,32]{1,0,3,2:T(8,128)(2,1)S(1)} %copy-done.12, bf16[16,100,16,32]{1,0,3,2:T(8,128)(2,1)S(1)} %copy-done.13), kind=kOutput, calls=%fused_computation.5 | convolution fusion | flops 171494400 | bytes 23961600 | tf_op jit(solution)/shard_map/cqhd,ckhd->chqk/dot_general | solution.py:118
  368.5 11.4 %convert_reduce_fusion = (f32[16,100,100]{1,2,0:T(8,128)}, bf16[16,16,100,100]{2,3,1,0:T(8,128)(2,1)S(1)}) fusion(f32[16,16,100,100]{2,3,1,0:T(8,128)} %get-tuple-element.79, f32[16,16,100]{2,1,0:T(8,128)S(1)} %get-tuple-element.78, f32[16,16,100,100]{2,3,1,0:T(8,128)} %get-tuple-element.72, f32[16,16,100]{2,1,0:T(8,128)S(1)} %get-tuple-element.71), kind=kLoop, calls=%fused_computation.3 | loop fusion | flops 15200000 | bytes 26444800 | tf_op jit(solution)/shard_map/reduce_sum | solution.py:124
  432.3 9.8 %convolution_convert_fusion.2 = bf16[512,2048]{1,0:T(8,128)(2,1)} fusion(bf16[1600,2048]{1,0:T(8,128)(2,1)} %copy-done.37, f32[1600,512]{1,0:T(8,128)} %copy-done, f32[512]{0:T(512)S(1)} %bitcast.143, f32[512]{0:T(512)S(1)} %bitcast.136, f32[1600]{0:T(1024)S(1)} %fusion.66, f32[1600]{0:T(1024)S(1)} %broadcast_multiply_fusion.1), kind=kOutput, calls=%fused_computation.68 | convolution fusion | flops 3360587776 | bytes 11944448 | tf_op jit(solution)/shard_map/rd,rf->df/dot_general | solution.py:108
  479.9 27.1 %reduce-scatter.26.cloned.1.call-done = bf16[256,512]{1,0:T(8,128)(2,1)} async-done(((bf16[2048,512]{1,0:T(8,128)(2,1)}), bf16[256,512]{1,0:T(8,128)(2,1)}) %reduce-scatter.26.cloned.1.call-update) | async-done | bytes 262160 | tf_op jit(solution)/shard_map/reduce_scatter | solution.py:173
  523.5 22.8 %copy.125 = f32[16,10,10,10,10]{3,4,1,2,0:T(8,128)} copy(f32[16,10,10,10,10]{2,1,4,3,0:T(8,128)} %reshape.219) | data formatting | bytes 1280000 | tf_op jit(solution)/shard_map/reshape | solution.py:124
  560.8 40.0 %all-reduce.2 = (f32[2048]{0:T(1024)S(1)}, f32[361,16]{0,1:T(8,128)}) all-reduce(f32[2048]{0:T(1024)S(1)} %get-tuple-element.85, f32[361,16]{0,1:T(8,128)S(1)} %reshape.206), channel_id=3, replica_groups=mesh['fsdp'=4,'win'=8] {'fsdp','win'}, use_global_device_ids=true, to_apply=%region_21.0.clone | all-reduce | flops 7824 | bytes 62592
  601.3 86.1 %reduce-scatter.28.cloned.1.call-done = f32[16,8]{1,0:T(8,128)} async-done(((f32[512,8]{1,0:T(8,128)}), f32[16,8]{1,0:T(8,128)}) %reduce-scatter.28.cloned.1.call-update) | async-done | bytes 528
  688.8 16.6 %reduce-scatter.32.cloned.1.call-done = bf16[128,64]{1,0:T(8,128)(2,1)} async-done(((bf16[512,64]{1,0:T(8,128)(2,1)}), bf16[128,64]{1,0:T(8,128)(2,1)}) %reduce-scatter.32.cloned.1.call-update) | async-done | bytes 16400
  706.8 19.6 %reduce-scatter.30.cloned.1.call-done = bf16[384,64]{1,0:T(8,128)(2,1)} async-done(((bf16[1536,64]{1,0:T(8,128)(2,1)}), bf16[384,64]{1,0:T(8,128)(2,1)}) %reduce-scatter.30.cloned.1.call-update) | async-done | bytes 49168
  728.1 18.6 %reduce-scatter.34.cloned.1.call-done = bf16[128,256]{1,0:T(8,128)(2,1)} async-done(((bf16[512,256]{1,0:T(8,128)(2,1)}), bf16[128,256]{1,0:T(8,128)(2,1)}) %reduce-scatter.34.cloned.1.call-update) | async-done | bytes 65552
  748.3 18.4 %reduce-scatter.24.cloned.1.call-done = bf16[64,512]{1,0:T(8,128)(2,1)} async-done(((bf16[64,2048]{1,0:T(8,128)(2,1)}), bf16[64,512]{1,0:T(8,128)(2,1)}) %reduce-scatter.24.cloned.1.call-update) | async-done | bytes 65552 | tf_op jit(solution)/shard_map/reduce_scatter | solution.py:184
  (201 shorter events, 245.9 us)
Async XLA Ops:
  7.2 48.8 %copy-start.6 = (bf16[16,100,512]{2,0,1:T(8,128)(2,1)S(1)}, bf16[16,100,512]{2,0,1:T(8,128)(2,1)}, u32[]{:S(2)}) copy-start(bf16[16,100,512]{2,0,1:T(8,128)(2,1)} %param.10) | copy-start | bytes 4915204
  7.2 198.4 %all-gather.5.cloned.1.call-start = ((), (), s32[]{:S(2)}) async-start(), calls=%async_computation.9 | async-start | bytes 1769472 | tf_op jit(solution)/shard_map/all_gather | solution.py:35
  24.6 269.0 %all-gather.7.cloned.1.call-start = ((), (), s32[]{:S(2)}) async-start(), calls=%async_computation.10 | async-start | bytes 2359296 | tf_op jit(solution)/shard_map/all_gather | solution.py:37
  40.0 266.3 %all-gather.9.cloned.1.call-start = ((), (), s32[]{:S(2)}) async-start(), calls=%async_computation.11 | async-start | bytes 2359296 | tf_op jit(solution)/shard_map/all_gather | solution.py:38
  53.9 410.4 %reduce-scatter.20.cloned.1.call-start = ((), (), s32[]{:S(2)}) async-start(), calls=%async_computation.13 | async-start | bytes 589824 | tf_op jit(solution)/shard_map/reduce_scatter | solution.py:167
  54.0 118.9 %copy-start.14 = (s32[10,10]{1,0:T(8,128)}, s32[10,10]{1,0:T(8,128)S(1)}, u32[]{:S(2)}) copy-start(s32[10,10]{1,0:T(8,128)S(1)} %subtract_add_fusion) | copy-start | bytes 1204
  55.9 149.7 %copy-start.18 = (f32[1600]{0:T(1024)}, f32[1600]{0:T(1024)S(1)}, u32[]{:S(2)}) copy-start(f32[1600]{0:T(1024)S(1)} %div.47) | copy-start | bytes 19204
  56.0 44.3 %copy-start.25 = (bf16[64,128]{1,0:T(8,128)(2,1)S(1)}, bf16[64,128]{1,0:T(8,128)(2,1)}, u32[]{:S(2)}) copy-start(bf16[64,128]{1,0:T(8,128)(2,1)} %param.15) | copy-start | bytes 49156
  56.0 56.3 %copy-start.27 = (f32[8,16]{1,0:T(8,128)S(1)}, f32[8,16]{1,0:T(8,128)}, u32[]{:S(2)}) copy-start(f32[8,16]{1,0:T(8,128)} %param.12) | copy-start | bytes 1540
  56.0 96.1 %copy-start.22 = (f32[361,16]{0,1:T(8,128)S(1)}, f32[361,16]{0,1:T(8,128)}, u32[]{:S(2)}) copy-start(f32[361,16]{0,1:T(8,128)} %param.18) | copy-start | bytes 69316
  56.1 106.1 %copy-start.10 = (bf16[16,100,512]{2,0,1:T(8,128)(2,1)S(1)}, bf16[16,100,512]{2,0,1:T(8,128)(2,1)}, u32[]{:S(2)}) copy-start(bf16[16,100,512]{2,0,1:T(8,128)(2,1)} %param.19) | copy-start | bytes 4915204
  59.4 40.8 %copy-start.28 = (f32[16]{0:T(128)}, f32[16]{0:T(128)S(1)}, u32[]{:S(2)}) copy-start(f32[16]{0:T(128)S(1)} %compare_convert_fusion) | copy-start | bytes 196
  100.3 51.3 %copy-start.16 = (f32[1600]{0:T(1024)}, f32[1600]{0:T(1024)S(1)}, u32[]{:S(2)}) copy-start(f32[1600]{0:T(1024)S(1)} %add.156) | copy-start | bytes 19204
  100.3 105.3 %copy-start.20 = (f32[1600]{0:T(1024)}, f32[1600]{0:T(1024)S(1)}, u32[]{:S(2)}) copy-start(f32[1600]{0:T(1024)S(1)} %rsqrt.20) | copy-start | bytes 19204
  152.1 53.4 %copy-start.23 = (f32[1,512]{1,0:T(1,128)}, f32[1,512]{1,0:T(1,128)S(1)}, u32[]{:S(2)}) copy-start(f32[1,512]{1,0:T(1,128)S(1)} %get-tuple-element.70) | copy-start | bytes 6148
  388.2 77.9 %reduce-scatter.18.cloned.1.call-start = ((), (), s32[]{:S(2)}) async-start(), calls=%async_computation.12 | async-start | bytes 1769472 | tf_op jit(solution)/shard_map/reduce_scatter | solution.py:164
  422.7 84.4 %reduce-scatter.26.cloned.1.call-start = ((), (), s32[]{:S(2)}) async-start(), calls=%async_computation.16 | async-start | bytes 2359296 | tf_op jit(solution)/shard_map/reduce_scatter | solution.py:173
  432.2 119.4 %reduce-scatter.22.cloned.1.call-start = ((), (), s32[]{:S(2)}) async-start(), calls=%async_computation.14 | async-start | bytes 2359296 | tf_op jit(solution)/shard_map/reduce_scatter | solution.py:170
  442.1 245.3 %reduce-scatter.28.cloned.1.call-start = ((), (), s32[]{:S(2)}) async-start(), calls=%async_computation.17 | async-start | bytes 270336
  454.8 250.6 %reduce-scatter.32.cloned.1.call-start = ((), (), s32[]{:S(2)}) async-start(), calls=%async_computation.19 | async-start | bytes 163840
  465.9 260.5 %reduce-scatter.30.cloned.1.call-start = ((), (), s32[]{:S(2)}) async-start(), calls=%async_computation.18 | async-start | bytes 491520
  467.9 278.7 %reduce-scatter.34.cloned.1.call-start = ((), (), s32[]{:S(2)}) async-start(), calls=%async_computation.20 | async-start | bytes 327680
  472.7 36.5 %copy-start.4 = (f32[1600,512]{1,0:T(8,128)S(1)}, f32[1600,512]{1,0:T(8,128)}, u32[]{:S(2)}) copy-start(f32[1600,512]{1,0:T(8,128)} %copy-done.3) | copy-start | bytes 9830404
  508.9 257.9 %reduce-scatter.24.cloned.1.call-start = ((), (), s32[]{:S(2)}) async-start(), calls=%async_computation.15 | async-start | bytes 327680 | tf_op jit(solution)/shard_map/reduce_scatter | solution.py:184
  (26 other events, 209.5 us)
Sparse Core Ops, SparseCore 0:
  24.7 25.8 all-gather.4
  52.5 28.4 all-gather.6
  82.9 28.3 all-gather.8
  388.3 31.3 reduce-scatter.19
  423.8 38.4 reduce-scatter.17
  465.7 41.2 reduce-scatter.25
  510.3 41.2 reduce-scatter.21
  553.9 133.4 reduce-scatter.27
  690.2 15.0 reduce-scatter.31
  707.6 18.7 reduce-scatter.29
  728.7 17.9 reduce-scatter.33
  748.9 17.7 reduce-scatter.23
where the time goes:
time: 783 us; the launch traced here: 776 us
  waiting for transfers between devices  192 us (25%)
  blocking collectives  187 us (24%)
  local copies, waits for them, and re-layouts  174 us (22%)
  matrix products  154 us (20%)
  other arithmetic  51.6 us (7%)
  between operations  16 us (2%)
    unnamed x16, waiting for transfers between devices  141 us
    unnamed x2, blocking collectives  79.3 us
    all_gather x1, blocking collectives, body(): lax.all_gather(vectors, ('fsdp', 'win'), axis=1, tiled=True)  39 us
    reshape x2, local copies, waits for them, and re-layouts, body(): jnp.sum(grad_scores_low.astype(f32), 0).reshape(HEADS, WS, WS, WS, WS)  29.6 us
    reduce_scatter x1, waiting for transfers between devices, body(): lax.psum_scatter(weight_grads[3].astype(jnp.bfloat16), 'win', scatter_dim...  27.1 us
    add x2, local copies, waits for them, and re-layouts, body(): jnp.einsum('cqhd,ckhd->chqk', query_low, key_low, preferred_element_type=...  27 us
    unnamed x90, local copies, waits for them, and re-layouts  20.1 us
    reduce_scatter x1, waiting for transfers between devices, body(): lax.psum_scatter(row_parts[2].astype(jnp.bfloat16), 'fsdp', scatter_dimen...  18.4 us
  transfers between devices with their start and end apart: 12, of which 7 were waited for; matrix products, arithmetic and copies ran while one was open for 38% of the time, Pallas kernels for 0%

commit v1 on v0

v1 whole, which is shorter than its diff:
```python
import functools

import jax
import jax.numpy as jnp
import numpy as np
from jax import lax
from jax.experimental import pallas as pl
from jax.experimental.pallas import tpu as pltpu
from jax.sharding import PartitionSpec as P

f32 = jnp.float32
bf16 = jnp.bfloat16
HEADS = 16
HD = 32
WS = 10
WT = WS * WS
D = HEADS * HD
FF = 4 * D
SIDE = 2 * WS - 1
TABLE = SIDE * SIDE
TP = 112
TL = 128
TT = 384
GH = 4
NG = HEADS // GH
EPS = 1e-5
SCALE = HD**-0.5
EXTRA = 32
NN = (((1,), (0,)), ((), ()))
NT = (((1,), (1,)), ((), ()))
TN = (((0,), (0,)), ((), ()))


def dot(a, b, dims=NN):
    return lax.dot_general(a, b, dims, preferred_element_type=f32)


def params(n=1):
    return pltpu.CompilerParams(dimension_semantics=("arbitrary",) * n, vmem_limit_bytes=60 * 2**20)


def cost(us):
    return pl.CostEstimate(flops=int(us * 1.1e9), bytes_accessed=int(us * 1e6), transcendentals=0)


def whole(shape):
    n = len(shape)
    return pl.BlockSpec(shape, lambda *a: (0,) * n, pipeline_mode=pl.Buffered(1))


def smem():
    return pl.BlockSpec(memory_space=pltpu.SMEM)


def anyspace():
    return pl.BlockSpec(memory_space=pl.ANY)


def three(x):
    hi = x.astype(bf16)
    rest = x - hi.astype(f32)
    mid = rest.astype(bf16)
    return hi, mid, (rest - mid.astype(f32)).astype(bf16)


def offset_place():
    cj = np.arange(WS)[:, None, None]
    r = np.arange(TT)[None, :, None]
    l = np.arange(256)[None, None, :]
    hit = (l < SIDE * WS) & (r == (l // WS) * SIDE + (l % WS) - cj + WS - 1)
    return jnp.asarray(hit, bf16)


class Geometry:
    def __init__(self, nw, nz):
        self.nw, self.nz = nw, nz
        self.r = D // nw
        self.cq, self.cp, self.c1 = 3 * D // nz // TL, D // nz // TL, FF // nz // TL
        self.r2 = FF // nw
        self.rows_a = self.cq * self.r
        self.rows_b = self.cp * self.r + self.c1 * self.r + self.cp * self.r2


def slabs(x):
    return jnp.concatenate([x[:, i : i + TL] for i in range(0, x.shape[1], TL)], 0)


def pack_body(wq, wp, w1, w2, vec, b1, a_o, b_o):
    ra = 0
    for i in range(0, wq.shape[1], TL):
        a_o[ra : ra + wq.shape[0], :] = wq[:, i : i + TL]
        ra += wq.shape[0]
    buf = jnp.zeros((EXTRA, TL), f32)
    own = vec.shape[1]
    pieces = [p.astype(f32) for p in three(vec[...])] + [p.astype(f32) for p in three(b1[...])]
    rows = [jnp.concatenate([p, jnp.zeros((8, TL - own), f32)], 1) for p in pieces[:3]]
    tail = [jnp.concatenate([p, jnp.zeros((1, TL - b1.shape[1]), f32)], 1) for p in pieces[3:]]
    tail = jnp.concatenate(tail + [jnp.zeros((5, TL), f32)], 0)
    a_o[ra : ra + EXTRA, :] = jnp.concatenate(rows + [tail], 0).astype(bf16)
    rb = 0
    for w in (wp, w1, w2):
        for i in range(0, w.shape[1], TL):
            b_o[rb : rb + w.shape[0], :] = w[:, i : i + TL]
            rb += w.shape[0]


def pack(geo, wq, wp, w1, w2, vec, b1):
    S = jax.ShapeDtypeStruct
    return pl.pallas_call(
        pack_body,
        out_shape=[S((geo.rows_a + EXTRA, TL), bf16), S((geo.rows_b, TL), bf16)],
        compiler_params=pltpu.CompilerParams(vmem_limit_bytes=16 * 2**20),
        cost_estimate=cost(1),
        name="pack",
    )(wq, wp, w1, w2, vec, b1)


def copies_a(geo, bufs, me, wq, sem):
    out = []
    for d in range(geo.nw):
        row = pl.multiple_of((me[0] ^ d) * geo.r, geo.r)
        for e in range(geo.nz):
            col = (me[1] ^ e) * geo.cq
            for i in range(geo.cq):
                out.append(
                    pltpu.make_async_copy(
                        bufs[d].at[e, pl.ds(i * geo.r, geo.r), :],
                        wq.at[col + i, pl.ds(row, geo.r), :],
                        sem,
                    )
                )
    return out


def copies_b(geo, bufs, me, wp, w1, w2, sem):
    out = []
    for d in range(geo.nw):
        row = pl.multiple_of((me[0] ^ d) * geo.r, geo.r)
        row2 = pl.multiple_of((me[0] ^ d) * geo.r2, geo.r2)
        for e in range(geo.nz):
            z = me[1] ^ e
            at = 0
            for w, n, r, to in ((wp, geo.cp, geo.r, row), (w1, geo.c1, geo.r, row), (w2, geo.cp, geo.r2, row2)):
                for i in range(n):
                    out.append(
                        pltpu.make_async_copy(
                            bufs[d].at[e, pl.ds(at, r), :], w.at[z * n + i, pl.ds(to, r), :], sem
                        )
                    )
                    at += r
    return out


def wide(ref, lo, n):
    return jnp.concatenate([ref[lo + i] for i in range(n)], 1)


def strided(ref, first, count, step):
    return jnp.concatenate([ref[half, pl.ds(first, count, stride=step), :] for half in range(2)], 1)


def bias_body(table, place, pb_o, zs):
    parts = jnp.concatenate([p for p in three(table[...])], 0)
    for cj in range(WS):
        z = dot(parts, place[cj])
        z = z[:HEADS] + z[HEADS : 2 * HEADS] + z[2 * HEADS :]
        for half in range(2):
            zs[half, cj * HEADS : (cj + 1) * HEADS, :] = z[:, half * TL : (half + 1) * TL]
    for j in range(NG):
        pb_o[j, WT:TP, :] = jnp.full((TP - WT, GH * TL), -1e30, f32)
        for h in range(GH):
            zh = strided(zs, j * GH + h, WS, HEADS)
            for rj in range(WS):
                off = (WS - 1 - rj) * WS
                part = zh if off == 0 else pltpu.roll(zh, 256 - off, 1)
                pb_o[j, rj * WS : (rj + 1) * WS, h * TL : (h + 1) * TL] = part[:, :TL]


def bias(table, place):
    return pl.pallas_call(
        bias_body,
        out_shape=jax.ShapeDtypeStruct((NG, TP, GH * TL), f32),
        scratch_shapes=[pltpu.VMEM((2, WS * HEADS, TL), f32)],
        compiler_params=pltpu.CompilerParams(vmem_limit_bytes=24 * 2**20),
        cost_estimate=cost(4),
        name="position_bias",
    )(table, place)


def table_sum(gt, place, rs):
    for j in range(NG):
        for h in range(GH):
            total = None
            for rj in range(WS):
                part = gt[j, rj * WS : (rj + 1) * WS, h * TL : (h + 1) * TL]
                part = jnp.concatenate([part, jnp.zeros((WS, TL), f32)], 1)
                off = (WS - 1 - rj) * WS
                part = part if off == 0 else pltpu.roll(part, off, 1)
                total = part if total is None else total + part
            base = (j * GH + h) * 16
            for half in range(2):
                rs[half, base : base + WS, :] = total[:, half * TL : (half + 1) * TL]
    out = jnp.zeros((HEADS, TT), f32)
    for cj in range(WS):
        parts = jnp.concatenate([p for p in three(strided(rs, cj, HEADS, 16))], 0)
        z = dot(parts, place[cj], NT)
        out = out + (z[:HEADS] + z[HEADS : 2 * HEADS] + z[2 * HEADS :])
    return out


def norm(x):
    mean = jnp.sum(x, -1, keepdims=True) * (1.0 / D)
    c = x - mean
    var = jnp.sum(c * c, -1, keepdims=True) * (1.0 / D)
    r = lax.rsqrt(var + EPS)
    return c * r, r


def norm_back(dn, xhat, r, gain):
    t = dn * gain
    m1 = jnp.sum(t, -1, keepdims=True) * (1.0 / D)
    m2 = jnp.sum(t * xhat, -1, keepdims=True) * (1.0 / D)
    return (t - m1 - xhat * m2) * r


def fill_blocks(bd, part):
    lane = lax.broadcasted_iota(jnp.int32, (1, TL), 1) // HD
    for h in range(GH):
        bd[h * TL : h * TL + TP, :] = jnp.where(lane == h, part, jnp.zeros_like(part))


def diag_t(full):
    return jnp.concatenate([full[h * HD : (h + 1) * HD, h * TL : (h + 1) * TL] for h in range(GH)], 0)


def gather_vectors(bufs, geo, me, vec_o, b1_o, tmp):
    own = D // (geo.nw * geo.nz)
    own1 = FF // (geo.nw * geo.nz)
    i32 = jnp.int32
    pick = (lax.broadcasted_iota(i32, (TL, D), 0) == lax.broadcasted_iota(i32, (TL, D), 1) % own).astype(bf16)
    pick1 = (lax.broadcasted_iota(i32, (TL, FF), 0) == lax.broadcasted_iota(i32, (TL, FF), 1) % own1).astype(bf16)
    slot = lax.broadcasted_iota(i32, (1, D), 1) // own
    slot1 = lax.broadcasted_iota(i32, (1, FF), 1) // own1
    vec = jnp.zeros((8, D), f32)
    b1 = jnp.zeros((8, FF), f32)
    for d in range(geo.nw):
        for e in range(geo.nz):
            dev = (me[1] ^ e) * geo.nw + (me[0] ^ d)
            x = tmp[d, e]
            y = dot(x[:24], pick)
            vec = vec + jnp.where(slot == dev, y[:8] + y[8:16] + y[16:24], 0.0)
            y1 = dot(x[24:], pick1)
            b1 = b1 + jnp.where(slot1 == dev, y1, 0.0)
    vec_o[...] = vec
    b1_o[...] = b1[0:1] + b1[1:2] + b1[2:3]


def attn_fwd_body(geo, G, vectors_in, *refs):
    nb = geo.nw
    me, tok, pb = refs[:3]
    bufs = refs[3 : 3 + nb]
    refs = refs[3 + nb :]
    if vectors_in:
        vec, refs = refs[0], refs[1:]
    n1_o, q_o, k_o, v_o, p_o, a_o = refs[:6]
    refs = refs[6:]
    if not vectors_in:
        vec, b1_o = refs[:2]
        refs = refs[2:]
    xs, bd, wq, tmp, sem, sem2 = refs

    @pl.when(pl.program_id(0) == 0)
    def _():
        moves = copies_a(geo, bufs, me, wq, sem)
        for m in moves:
            m.start()
        if not vectors_in:
            small = [
                pltpu.make_async_copy(bufs[d].at[:, pl.ds(geo.rows_a, EXTRA), :], tmp.at[d], sem2)
                for d in range(geo.nw)
            ]
            for m in small:
                m.start()
        xs[...] = jnp.zeros_like(xs)
        bd[...] = jnp.zeros_like(bd)
        if not vectors_in:
            for m in small:
                m.wait()
            gather_vectors(bufs, geo, me, vec, b1_o, tmp)
        for m in moves:
            m.wait()

    for g in range(G):
        xs[g * TP : g * TP + WT, :] = tok[g].astype(f32)
    xhat, _ = norm(xs[...])
    n1 = (xhat * vec[0:1, :] + vec[1:2, :]).astype(bf16)
    n1_o[...] = n1
    q_o[...] = ((dot(n1, wide(wq, 0, NG)) + vec[2:3, :]) * SCALE).astype(bf16)
    k_o[...] = dot(n1, wide(wq, NG, NG)).astype(bf16)
    v_o[...] = (dot(n1, wide(wq, 2 * NG, NG)) + vec[3:4, :]).astype(bf16)

    def window(g, carry):
        rows = pl.ds(pl.multiple_of(g * TP, 16), TP)
        for j in range(NG):
            cols = slice(j * TL, (j + 1) * TL)
            qg = q_o[rows, cols]
            kg = k_o[rows, cols]
            vg = v_o[rows, cols]
            b = bd.at[j]
            fill_blocks(b, qg)
            s = dot(kg, b[...], NT) + pb[j]
            m = jnp.max(s, 0, keepdims=True)
            e = jnp.exp(s - m)
            l = jnp.sum(e, 0, keepdims=True)
            p = (e * (1.0 / l)).astype(bf16)
            p_o[g, j] = p
            at = diag_t(dot(vg, p, TN))
            a_o[rows, cols] = at.T[:TP].astype(bf16)
        return carry

    lax.fori_loop(0, G, window, 0)


def attn_fwd(geo, me, tok, pb, bufs, vec=None, G=4):
    B = tok.shape[0]
    R = B * TP
    S = jax.ShapeDtypeStruct
    act = S((R, D), bf16)
    blk = pl.BlockSpec((G * TP, D), lambda i: (i, 0))
    given = [] if vec is None else [vec]
    out_specs = [blk, blk, blk, blk, pl.BlockSpec((G, NG, TP, GH * TL), lambda i: (i, 0, 0, 0)), blk]
    out_shape = [act, act, act, act, S((B, NG, TP, GH * TL), bf16), act]
    if vec is None:
        out_specs += [whole((8, D)), whole((1, FF))]
        out_shape += [S((8, D), f32), S((1, FF), f32)]
    return pl.pallas_call(
        functools.partial(attn_fwd_body, geo, G, vec is not None),
        grid=(B // G,),
        in_specs=[smem(), pl.BlockSpec((G, WT, D), lambda i: (i, 0, 0)), whole(pb.shape)]
        + [anyspace()] * len(bufs)
        + [whole(g.shape) for g in given],
        out_specs=out_specs,
        out_shape=out_shape,
        scratch_shapes=[
            pltpu.VMEM((G * TP, D), f32),
            pltpu.VMEM((NG, GH * TL, TL), bf16),
            pltpu.VMEM((3 * NG, D, TL), bf16),
            pltpu.VMEM((geo.nw, geo.nz, EXTRA, TL), bf16),
            pltpu.SemaphoreType.DMA,
            pltpu.SemaphoreType.DMA,
        ],
        compiler_params=params(),
        cost_estimate=cost(30),
        name="attn_fwd",
    )(me, tok, pb, *bufs, *given)


GC = 0.7978845608028654
GA = 0.044715


def gelu_both(u):
    u2 = u * u
    t = jnp.tanh(u * (GC + (GC * GA) * u2))
    h = 0.5 + 0.5 * t
    act = u * h
    slope = h + (act * (2.0 - 2.0 * h)) * (GC + (3.0 * GC * GA) * u2)
    return act, slope


def scatter_out(geo, me, blocks, outs):
    cores = len(outs)
    for c in range(cores):
        for xy in range(geo.nw // cores):
            w = me[0] ^ (xy * cores + c)
            for e in range(geo.nz):
                z = me[1] ^ e
                at = 0
                for ref, pick in blocks:
                    for part in pick(ref, w, z):
                        outs[c][xy, e, at : at + part.shape[0], :] = part.astype(bf16)
                        at += part.shape[0]


def mlp_body(geo, G, FC, *refs):
    nb = geo.nw
    me, live, tok, cot, attn = refs[:5]
    bufs = refs[5 : 5 + nb]
    vec, b1 = refs[5 + nb : 7 + nb]
    refs = refs[7 + nb :]
    out_o, dx1_o, da_o, gv_o, gb1_o = refs[:5]
    cores = 2 if nb > 1 else 1
    outs = refs[5 : 5 + cores]
    xs, dys, gp, g1, g2, gv, gb1, acc, dn2, wp, w1, w2, sem = refs[5 + cores :]
    i = pl.program_id(0)
    n = pl.num_programs(0)

    @pl.when(i == 0)
    def _():
        moves = copies_b(geo, bufs, me, wp, w1, w2, sem)
        for m in moves:
            m.start()
        for ref in (xs, dys, gp, g1, g2, gv, gb1):
            ref[...] = jnp.zeros_like(ref)
        for m in moves:
            m.wait()

    for g in range(G):
        xs[g * TP : g * TP + WT, :] = tok[g].astype(f32)
        mask = (i * G + g < live[0]).astype(f32)
        dys[g * TP : g * TP + WT, :] = cot[g].astype(f32) * mask
    at = attn[...]
    wpv = wide(wp, 0, NG)
    x1 = xs[...] + dot(at, wpv) + vec[4:5, :]
    acc[...] = x1 + vec[7:8, :]
    xhat, r = norm(x1)
    n2 = (xhat * vec[5:6, :] + vec[6:7, :]).astype(bf16)
    n2t = n2.T
    dyf = dys[...]
    dy = dyf.astype(bf16)
    dyt = dy.T
    ns = FC // TL
    for c in range(FF // FC):
        cols = slice(c * FC, (c + 1) * FC)
        w1c = wide(w1, c * ns, ns)
        w2c = jnp.concatenate([w2[z, cols, :] for z in range(NG)], 1)
        u = dot(n2, w1c) + b1[:, cols]
        a, ga = gelu_both(u)
        a = a.astype(bf16)
        acc[...] += dot(a, w2c)
        du = (dot(dy, w2c, NT) * ga).astype(bf16)
        t2 = dot(dyt, a)
        t1 = dot(n2t, du)
        for k in range(ns):
            g2[c * ns + k] += t2[:, k * TL : (k + 1) * TL]
            g1[c * ns + k] += t1[:, k * TL : (k + 1) * TL]
        gb1[:, cols] += jnp.sum(du.astype(f32), 0, keepdims=True)
        d = dot(du, w1c, NT)
        if c == 0:
            dn2[...] = d
        else:
            dn2[...] += d
    for g in range(G):
        mask = (i * G + g < live[0]).astype(f32)
        out_o[g] = (acc[g * TP : g * TP + WT, :] * mask).astype(bf16)
    dn = dn2[...]
    gv[7:8, :] += jnp.sum(dyf, 0, keepdims=True)
    gv[5:6, :] += jnp.sum(dn * xhat, 0, keepdims=True)
    gv[6:7, :] += jnp.sum(dn, 0, keepdims=True)
    dx1 = dyf + norm_back(dn, xhat, r, vec[5:6, :])
    dx1_o[...] = dx1
    dl = dx1.astype(bf16)
    gv[4:5, :] += jnp.sum(dl.astype(f32), 0, keepdims=True)
    tp = dot(at.T, dl)
    for k in range(NG):
        gp[k] += tp[:, k * TL : (k + 1) * TL]
    da_o[...] = dot(dl, wpv, NT).astype(bf16)

    @pl.when(i == n - 1)
    def _():
        gv_o[...] = gv[...]
        gb1_o[...] = gb1[...]

        def rows(ref, n):
            def pick(ref, w, z):
                at = pl.multiple_of(w * geo.r, geo.r)
                return [ref[z * n + k, pl.ds(at, geo.r), :] for k in range(n)]

            return ref, pick

        def turned(ref, w, z):
            n, r = geo.r2 // TL, D // geo.nz
            at = pl.multiple_of(z * r, r)
            return [ref[w * n + k, pl.ds(at, r), :] for k in range(n)]

        scatter_out(geo, me, [rows(gp, geo.cp), rows(g1, geo.c1), (g2, turned)], outs)


def mlp(geo, me, live, tok, cot, attn, bufs, vec, b1, G=4, FC=512):
    B = tok.shape[0]
    R = B * TP
    M = G * TP
    blk = pl.BlockSpec((M, D), lambda i: (i, 0))
    win = pl.BlockSpec((G, WT, D), lambda i: (i, 0, 0))
    S = jax.ShapeDtypeStruct
    cores = 2 if geo.nw > 1 else 1
    gshape = (geo.nw // cores, geo.nz, geo.rows_b, TL)
    V = pltpu.VMEM
    return pl.pallas_call(
        functools.partial(mlp_body, geo, G, FC),
        grid=(B // G,),
        in_specs=[smem(), smem(), win, win, blk] + [anyspace()] * len(bufs) + [whole(vec.shape), whole(b1.shape)],
        out_specs=[win, blk, blk, whole((8, D)), whole((1, FF))] + [whole(gshape)] * cores,
        out_shape=[S(tok.shape, bf16), S((R, D), f32), S((R, D), bf16), S((8, D), f32), S((1, FF), f32)]
        + [S(gshape, bf16)] * cores,
        scratch_shapes=[
            V((M, D), f32),
            V((M, D), f32),
            V((NG, D, TL), f32),
            V((FF // TL, D, TL), f32),
            V((FF // TL, D, TL), f32),
            V((8, D), f32),
            V((1, FF), f32),
            V((M, D), f32),
            V((M, D), f32),
            V((NG, D, TL), bf16),
            V((FF // TL, D, TL), bf16),
            V((NG, FF, TL), bf16),
            pltpu.SemaphoreType.DMA,
        ],
        compiler_params=params(),
        cost_estimate=cost(44),
        name="mlp",
    )(me, live, tok, cot, attn, *bufs, vec, b1)


def attn_bwd_body(geo, G, *refs):
    me, q, k, v, p, da, n1, dc_o, gb_o, gt_o = refs[:10]
    cores = 2 if geo.nw > 1 else 1
    outs = refs[10 : 10 + cores]
    bdq, bda, gq, gb, gt = refs[10 + cores :]
    i = pl.program_id(0)
    n = pl.num_programs(0)

    @pl.when(i == 0)
    def _():
        for ref in (bdq, bda, gq, gb, gt):
            ref[...] = jnp.zeros_like(ref)

    def window(g, carry):
        rows = pl.ds(pl.multiple_of(g * TP, 16), TP)
        for j in range(NG):
            cols = slice(j * TL, (j + 1) * TL)
            qg, kg, vg, dg = q[rows, cols], k[rows, cols], v[rows, cols], da[rows, cols]
            bq, ba = bdq.at[j], bda.at[j]
            fill_blocks(bq, qg)
            fill_blocks(ba, dg)
            pt = p[g, j]
            pf = pt.astype(f32)
            dp = dot(vg, ba[...], NT)
            t = pf * dp
            ds = (t - pf * jnp.sum(t, 0, keepdims=True)).astype(bf16)
            gt[j] += ds.astype(f32)
            dv = dot(pt, ba[...])
            dk = dot(ds, bq[...])
            dq = diag_t(dot(kg, ds, TN)).T[:TP] * SCALE
            dc_o[rows, j * TL : (j + 1) * TL] = dq.astype(bf16)
            dc_o[rows, D + j * TL : D + (j + 1) * TL] = dk.astype(bf16)
            dc_o[rows, 2 * D + j * TL : 2 * D + (j + 1) * TL] = dv.astype(bf16)
        return carry

    lax.fori_loop(0, G, window, 0)
    n1t = n1[...].T
    for c in range(3):
        cols = slice(c * D, (c + 1) * D)
        dc = dc_o[:, cols]
        t = dot(n1t, dc)
        for s in range(NG):
            gq[c * NG + s] += t[:, s * TL : (s + 1) * TL]
        gb[:, cols] += jnp.sum(dc.astype(f32), 0, keepdims=True)

    @pl.when(i == n - 1)
    def _():
        gb_o[...] = gb[...]
        gt_o[...] = gt[...]

        def rows(ref, w, z):
            at = pl.multiple_of(w * geo.r, geo.r)
            return [ref[z * geo.cq + s, pl.ds(at, geo.r), :] for s in range(geo.cq)]

        scatter_out(geo, me, [(gq, rows)], outs)


def attn_bwd(geo, me, q, k, v, p, da, n1, G=4):
    R = q.shape[0]
    B = R // TP
    blk = pl.BlockSpec((G * TP, D), lambda i: (i, 0))
    S = jax.ShapeDtypeStruct
    V = pltpu.VMEM
    cores = 2 if geo.nw > 1 else 1
    gshape = (geo.nw // cores, geo.nz, geo.rows_a, TL)
    return pl.pallas_call(
        functools.partial(attn_bwd_body, geo, G),
        grid=(B // G,),
        in_specs=[smem(), blk, blk, blk, pl.BlockSpec((G, NG, TP, GH * TL), lambda i: (i, 0, 0, 0)), blk, blk],
        out_specs=[pl.BlockSpec((G * TP, 3 * D), lambda i: (i, 0)), whole((1, 3 * D)), whole((NG, TP, GH * TL))]
        + [whole(gshape)] * cores,
        out_shape=[S((R, 3 * D), bf16), S((1, 3 * D), f32), S((NG, TP, GH * TL), f32)] + [S(gshape, bf16)] * cores,
        scratch_shapes=[
            V((NG, GH * TL, TL), bf16),
            V((NG, GH * TL, TL), bf16),
            V((3 * NG, D, TL), f32),
            V((1, 3 * D), f32),
            V((NG, TP, GH * TL), f32),
        ],
        compiler_params=params(),
        cost_estimate=cost(30),
        name="attn_bwd",
    )(me, q, k, v, p, da, n1)


def input_bwd_body(geo, G, *refs):
    nb = geo.nw
    me, tok, dc, dx1, vec, gv2, gb, gb1, gt, place = refs[:10]
    bufs = refs[10 : 10 + nb]
    gt_o, small_o, xs, gv, rs, wq, sem = refs[10 + nb :]
    i = pl.program_id(0)
    n = pl.num_programs(0)

    @pl.when(i == 0)
    def _():
        moves = copies_a(geo, bufs, me, wq, sem)
        for m in moves:
            m.start()
        xs[...] = jnp.zeros_like(xs)
        gv[...] = jnp.zeros_like(gv)
        small_o[8:24, :TT] = table_sum(gt, place, rs)
        for k in range(FF // TL):
            small_o[8 + k : 9 + k, TT:] = gb1[:, k * TL : (k + 1) * TL]
        for m in moves:
            m.wait()

    for g in range(G):
        xs[g * TP : g * TP + WT, :] = tok[g].astype(f32)
    dn = dot(dc[...], wide(wq, 0, 3 * NG), NT)
    xhat, r = norm(xs[...])
    gv[0:1, :] += jnp.sum(dn * xhat, 0, keepdims=True)
    gv[1:2, :] += jnp.sum(dn, 0, keepdims=True)
    dx = dx1[...] + norm_back(dn, xhat, r, vec[0:1, :])
    for g in range(G):
        gt_o[g] = dx[g * TP : g * TP + WT].astype(bf16)

    @pl.when(i == n - 1)
    def _():
        small_o[0:2, :] = gv[0:2, :]
        small_o[2:3, :] = gb[:, :D]
        small_o[3:4, :] = gb[:, 2 * D :]
        small_o[4:8, :] = gv2[4:8, :]


def input_bwd(geo, me, tok, dc, dx1, vec, gv2, gb, gb1, gt, place, bufs, G=4):
    B = tok.shape[0]
    blk = pl.BlockSpec((G * TP, D), lambda i: (i, 0))
    win = pl.BlockSpec((G, WT, D), lambda i: (i, 0, 0))
    S = jax.ShapeDtypeStruct
    V = pltpu.VMEM
    return pl.pallas_call(
        functools.partial(input_bwd_body, geo, G),
        grid=(B // G,),
        in_specs=[smem(), win, pl.BlockSpec((G * TP, 3 * D), lambda i: (i, 0)), blk]
        + [whole(x.shape) for x in (vec, gv2, gb, gb1, gt, place)]
        + [anyspace()] * len(bufs),
        out_specs=[win, whole((24, D))],
        out_shape=[S(tok.shape, bf16), S((24, D), f32)],
        scratch_shapes=[
            V((G * TP, D), f32),
            V((8, D), f32),
            V((2, HEADS * 16, TL), f32),
            V((3 * NG, D, TL), bf16),
            pltpu.SemaphoreType.DMA,
        ],
        compiler_params=params(),
        cost_estimate=cost(11),
        name="input_bwd",
    )(me, tok, dc, dx1, vec, gv2, gb, gb1, gt, place, *bufs)


def swap(x, axis, size, d):
    return lax.ppermute(x, axis, [(i, i ^ d) for i in range(size)])


def gather_pieces(buf, nw, nz):
    mine = jnp.stack([buf] + [swap(buf, "fsdp", nz, e) for e in range(1, nz)])
    planes = [mine] + [swap(mine, "win", nw, 2 * d) for d in range(1, nw // 2)]
    out = []
    for x in planes:
        out += [x, swap(x, "win", nw, 1)]
    return out


def scatter_sum(keep, send, nw, nz):
    got = swap(send, "win", nw, 1)
    sums = [(keep[d].astype(f32) + got[d].astype(f32)).astype(bf16) for d in range(nw // 2)]
    total = sums[0].astype(f32)
    for d in range(1, nw // 2):
        total = total + swap(sums[d], "win", nw, 2 * d).astype(f32)
    low = total.astype(bf16)
    own = total[0]
    for e in range(1, nz):
        own = own + swap(low[e], "fsdp", nz, e).astype(f32)
    return own


def sum_all(x, nw, nz):
    x = x + swap(x, "win", nw, 1)
    x = x + functools.reduce(jnp.add, [swap(x, "win", nw, 2 * d) for d in range(1, nw // 2)])
    return x + functools.reduce(jnp.add, [swap(x, "fsdp", nz, e) for e in range(1, nz)])


def unslab(x, n):
    r = x.shape[0] // n
    return jnp.concatenate([x[i * r : (i + 1) * r] for i in range(n)], 1)


def split_b(geo, x):
    a, b = geo.cp * geo.r, (geo.cp + geo.c1) * geo.r
    two = x[b:].reshape(geo.r2 // TL, D // geo.nz, TL).transpose(0, 2, 1).reshape(geo.r2, D // geo.nz)
    return unslab(x[:a], geo.cp), unslab(x[a:b], geo.c1), two


def body(nw, nz, tokens, live, vectors, fc1_bias, w_qkv, w_proj, w_fc1, w_fc2, rel_table, cotangent):
    both = ("fsdp", "win")
    fast = D // nz % TL == 0 and FF // nw % TL == 0 and D // nw % 16 == 0 and nw > 1 and nz > 1
    fast = fast and nw & (nw - 1) == 0 and nz & (nz - 1) == 0
    place = offset_place()
    table = jnp.pad(rel_table.T, ((0, 0), (0, TT - TABLE)))
    if fast:
        geo = Geometry(nw, nz)
        me = jnp.stack([lax.axis_index("win"), lax.axis_index("fsdp")]).astype(jnp.int32)
        buf_a, buf_b = pack(geo, w_qkv, w_proj, w_fc1, w_fc2, vectors, fc1_bias.reshape(1, -1))
        bufs_a = gather_pieces(buf_a, nw, nz)
        bufs_b = gather_pieces(buf_b, nw, nz)
        pb = bias(table, place)
        n1, q, k, v, p, att, vec, b1 = attn_fwd(geo, me, tokens, pb, bufs_a)
    else:
        geo = Geometry(1, 1)
        me = jnp.zeros((2,), jnp.int32)

        def full(w):
            return lax.all_gather(lax.all_gather(w, "fsdp", axis=1, tiled=True), "win", axis=0, tiled=True)

        bufs_a = [slabs(full(w_qkv))[None]]
        bufs_b = [jnp.concatenate([slabs(full(w)) for w in (w_proj, w_fc1, w_fc2)], 0)[None]]
        vec = lax.all_gather(vectors, both, axis=1, tiled=True)
        b1 = lax.all_gather(fc1_bias, both, axis=0, tiled=True).reshape(1, -1)
        pb = bias(table, place)
        n1, q, k, v, p, att = attn_fwd(geo, me, tokens, pb, bufs_a, vec)
    out, dx1, da, gv2, gb1, *gw = mlp(geo, me, live, tokens, cotangent, att, bufs_b, vec, b1)
    dc, gb, gt, *gq = attn_bwd(geo, me, q, k, v, p, da, n1)
    grad_tokens, small = input_bwd(geo, me, tokens, dc, dx1, vec, gv2, gb, gb1, gt, place, bufs_a)
    if fast:
        own_b = scatter_sum(*gw, nw, nz)
        own_a = scatter_sum(*gq, nw, nz)
        small = sum_all(small, nw, nz)
        grad_qkv = unslab(own_a, geo.cq)
        grad_proj, grad_one, grad_two = split_b(geo, own_b)
    else:

        def down(g):
            g = lax.psum_scatter(g.astype(bf16), "win", scatter_dimension=0, tiled=True)
            return lax.psum_scatter(g, "fsdp", scatter_dimension=1, tiled=True).astype(f32)

        grad_qkv = down(unslab(gq[0][0, 0], geo.cq))
        grad_proj, grad_one, grad_two = [down(g) for g in split_b(geo, gw[0][0, 0])]
        small = lax.psum(small, both)
    dev = lax.axis_index(both)
    own, own1 = D // (nw * nz), FF // (nw * nz)
    grad_vectors = lax.dynamic_slice_in_dim(small[:8], dev * own, own, 1)
    grad_bias = lax.dynamic_slice_in_dim(small[8:, TT:].reshape(FF), dev * own1, own1, 0)
    grad_table = small[8:, :TABLE].T
    return out, grad_tokens, grad_vectors, grad_bias, grad_qkv, grad_proj, grad_one, grad_two, grad_table


def solution(mesh):
    split = P(("fsdp", "win"), None, None)
    vecs = P(None, ("fsdp", "win"))
    flat = P(("fsdp", "win"))
    cut = P("win", "fsdp")
    return jax.shard_map(
        functools.partial(body, mesh.shape["win"], mesh.shape["fsdp"]),
        mesh=mesh,
        in_specs=(split, flat, vecs, flat, cut, cut, cut, cut, P(), split),
        out_specs=(split, split, vecs, flat, cut, cut, cut, cut, P()),
        check_vma=False,
    )
```

time: 783 us -> 250 us (0.32)
  blocking collectives: 187 us -> 0 us
  matrix products: 154 us -> 0 us
  local copies, waits for them, and re-layouts: 174 us -> 20.2 us
  waiting for transfers between devices: 192 us -> 65.2 us
  Pallas kernels: 0 us -> 116 us
  other arithmetic: 51.6 us -> 4.14 us
  starting transfers between devices: 1.26 us -> 41.5 us
  between operations: 16 us -> 1.68 us
    dot_general x23 -> x0, matrix products: 154 us -> none  [the longest x1 15.7 us: body(): jnp.einsum('rd,fd->rf', grad_out_low, back_two, preferred_element_type=f32)]
    unnamed x16 -> x0, waiting for transfers between devices: 141 us -> none
    pallas_call x0 -> x6, Pallas kernels: none -> 116 us  [the longest x1 41.8 us: mlp(): pl.pallas_call(functools.partial(mlp_body, geo, G, FC), grid=(B // G,), i...]
    all_gather x6 -> x0, blocking collectives: 107 us -> none  [the longest x1 39 us: body(): lax.all_gather(vectors, ('fsdp', 'win'), axis=1, tiled=True)]
    unnamed x2 -> x0, blocking collectives: 79.3 us -> none
    reshape x12 -> x1, local copies, waits for them, and re-layouts: 69.7 us -> 0.01 us  [body(): small[8:, TT:].reshape(FF)]
    ppermute x0 -> x41, waiting for transfers between devices: none -> 65.2 us  [swap(): return lax.ppermute(x, axis, [(i, i ^ d) for i in range(size)])]
    reduce_scatter x5 -> x0, waiting for transfers between devices: 50.9 us -> none  [the longest x1 27.1 us: body(): lax.psum_scatter(weight_grads[3].astype(jnp.bfloat16), 'win', scatter_dim...]
  transfers between devices with their start and end apart: 12 -> 41, of which waited for: 7 -> 21; matrix products, arithmetic and copies ran while one was open for 38% -> 5% of each run, Pallas kernels for 0% -> 18%
where the time goes in v1:
time: 250 us; the launch traced here: 249 us
  Pallas kernels  116 us (46%)
  waiting for transfers between devices  65.2 us (26%)
  starting transfers between devices  41.5 us (17%)
  local copies, waits for them, and re-layouts  20.2 us (8%)
  other arithmetic  4.14 us (2%)
    ppermute x41, waiting for transfers between devices, swap(): return lax.ppermute(x, axis, [(i, i ^ d) for i in range(size)])  65.2 us
    pallas_call x1, Pallas kernels, mlp(): pl.pallas_call(functools.partial(mlp_body, geo, G, FC), grid=(B // G,), i...  41.8 us
    ppermute x41, starting transfers between devices, swap(): return lax.ppermute(x, axis, [(i, i ^ d) for i in range(size)])  41.5 us
    pallas_call x1, Pallas kernels, attn_fwd(): pl.pallas_call(functools.partial(attn_fwd_body, geo, G, vec is not None),...  32.8 us
    pallas_call x1, Pallas kernels, attn_bwd(): pl.pallas_call(functools.partial(attn_bwd_body, geo, G), grid=(B // G,),...  29.1 us
    unnamed x50, local copies, waits for them, and re-layouts  16.9 us
    pallas_call x1, Pallas kernels, input_bwd(): pl.pallas_call(functools.partial(input_bwd_body, geo, G), grid=(B // G,),...  11.4 us
  transfers between devices with their start and end apart: 41, of which 21 were waited for; matrix products, arithmetic and copies ran while one was open for 5% of the time, Pallas kernels for 18%

profile of v1, /device:TPU:0, one launch (start us, length us, event | category | flops | bytes accessed | tf_op | source)
XLA Modules:
  0.0 248.9 jit_solution(6242515557120419201)
XLA Ops:
  5.2 5.1 %collective-permute-start.2 = (bf16[224,128]{1,0:T(8,128)(2,1)S(1)}, bf16[224,128]{1,0:T(8,128)(2,1)S(1)}, u32[]{:S(2)}, u32[]{:S(2)}) collective-permute-start(bf16[224,128]{1,0:T(8,128)(2,1)S(1)} %get-tuple-element.33), channel_id=1, source_target_pairs={{0,24},{8,16},{16,8},{24,0},{1,25},{9,17},{17,9},{25,1},{2,26},{10... | collective-permute-start | bytes 172040 | tf_op jit(solution)/shard_map/ppermute | solution.py:669
  12.7 2.7 %collective-permute-done.1 = bf16[224,128]{1,0:T(8,128)(2,1)S(1)} collective-permute-done((bf16[224,128]{1,0:T(8,128)(2,1)S(1)}, bf16[224,128]{1,0:T(8,128)(2,1)S(1)}, u32[]{:S(2)}, u32[]{:S(2)}) %collective-permute-start.1) | collective-permute-done | bytes 57376 | tf_op jit(solution)/shard_map/ppermute | solution.py:669
  15.5 2.5 %collective-permute-start.8 = (bf16[4,224,128]{2,1,0:T(8,128)(2,1)S(1)}, bf16[4,224,128]{2,1,0:T(8,128)(2,1)S(1)}, u32[]{:S(2)}, u32[]{:S(2)}) collective-permute-start(bf16[4,224,128]{2,1,0:T(8,128)(2,1)S(1)} %pad_maximum_fusion.1.refs_3_.refs_10_), channel_id=1, source_target_pairs={{0,6},{1,7},{2,4},{3,5},{4,2},{5,3},{6,0},{7,1},{8,14},{9,15},{10,... | collective-permute-start | bytes 688136 | tf_op jit(solution)/shard_map/ppermute | solution.py:669
  18.0 2.6 %collective-permute-start.12 = (bf16[576,128]{1,0:T(8,128)(2,1)S(1)}, bf16[576,128]{1,0:T(8,128)(2,1)S(1)}, u32[]{:S(2)}, u32[]{:S(2)}) collective-permute-start(bf16[576,128]{1,0:T(8,128)(2,1)S(1)} %get-tuple-element.35), channel_id=1, source_target_pairs={{0,24},{8,16},{16,8},{24,0},{1,25},{9,17},{17,9},{25,1},{2,26},{10... | collective-permute-start | bytes 442376 | tf_op jit(solution)/shard_map/ppermute | solution.py:669
  22.9 3.7 %collective-permute-done.12 = bf16[576,128]{1,0:T(8,128)(2,1)S(1)} collective-permute-done((bf16[576,128]{1,0:T(8,128)(2,1)S(1)}, bf16[576,128]{1,0:T(8,128)(2,1)S(1)}, u32[]{:S(2)}, u32[]{:S(2)}) %collective-permute-start.12) | collective-permute-done | bytes 147488 | tf_op jit(solution)/shard_map/ppermute | solution.py:669
  27.2 5.2 %collective-permute-done.11 = bf16[576,128]{1,0:T(8,128)(2,1)S(1)} collective-permute-done((bf16[576,128]{1,0:T(8,128)(2,1)S(1)}, bf16[576,128]{1,0:T(8,128)(2,1)S(1)}, u32[]{:S(2)}, u32[]{:S(2)}) %collective-permute-start.11) | collective-permute-done | bytes 147488 | tf_op jit(solution)/shard_map/ppermute | solution.py:669
  40.7 2.1 copy.21.refs_1_.refs_2_
  42.8 2.1 copy.22.refs_3_
  46.0 4.1 %collective-permute-done.18.refs_11_ = bf16[4,576,128]{2,1,0:T(8,128)(2,1)S(1)} collective-permute-done((bf16[4,576,128]{2,1,0:T(8,128)(2,1)S(1)}, bf16[4,576,128]{2,1,0:T(8,128)(2,1)S(1)}, u32[]{:S(2)}, u32[]{:S(2)}) %collective-permute-start.18) | collective-permute-done | bytes 589856 | tf_op jit(solution)/shard_map/ppermute | solution.py:669
  50.2 10.9 %collective-permute-done.16.refs_9_ = bf16[4,576,128]{2,1,0:T(8,128)(2,1)S(1)} collective-permute-done((bf16[4,576,128]{2,1,0:T(8,128)(2,1)S(1)}, bf16[4,576,128]{2,1,0:T(8,128)(2,1)S(1)}, u32[]{:S(2)}, u32[]{:S(2)}) %collective-permute-start.16) | collective-permute-done | bytes 589856 | tf_op jit(solution)/shard_map/ppermute | solution.py:669
  61.6 32.8 %attn_fwd.1 = (bf16[1792,512]{1,0:T(8,128)(2,1)}, bf16[1792,512]{1,0:T(8,128)(2,1)}, bf16[1792,512]{1,0:T(8,128)(2,1)}, bf16[1792,512]{1,0:T(8,128)(2,1)}, bf16[...) custom-call(s32[2]{0:T(128)} %pad_add_fusion.refs_0_, ...), custom_call_target="tpu_custom_call" | custom-call | flops 32999999488 | bytes 30000000 | tf_op jit(solution)/shard_map/attn_fwd/pallas_call | solution.py:336
  95.5 41.8 %mlp.1 = (bf16[16,100,512]{2,1,0:T(8,128)(2,1)}, f32[1792,512]{1,0:T(8,128)}, bf16[1792,512]{1,0:T(8,128)(2,1)}, f32[8,512]{1,0:T(8,128)}, f32[1,2048]{1,0:T(1,1...) custom-call(s32[2]{0:T(128)} %pad_add_fusion.refs_0_, s32[1]{0:T(128)S(6)} %copy.27.refs_1_, ...), custom_call_target="tpu_custom_call" | custom-call | flops 48399998976 | bytes 44000000 | tf_op jit(solution)/shard_map/mlp/pallas_call | solution.py:489
  137.3 29.1 %attn_bwd.1 = (bf16[1792,1536]{1,0:T(8,128)(2,1)}, f32[1,1536]{1,0:T(1,128)}, f32[4,112,512]{2,1,0:T(8,128)}, bf16[4,4,192,128]{3,2,1,0:T(8,128)(2,1)}, bf16[4,4,192,128]{3,2,1,0:T(8,128)(2,1)}) custom-call(s32[2]{0:T(128)} %pad_add_fusion.refs_0_, bf16[1792,512]{1,0:T(8,128)(2,1)} %get-tuple-element.39.refs_1_, ...), custom_call_target="tpu_custom_call" | custom-call | flops 32999999488 | bytes 30000000 | tf_op jit(solution)/shard_map/attn_bwd/pallas_call | solution.py:582
  167.0 11.4 %input_bwd.1 = (bf16[16,100,512]{2,1,0:T(8,128)(2,1)}, f32[24,512]{1,0:T(8,128)}) custom-call(s32[2]{0:T(128)} %pad_add_fusion.refs_0_, bf16[16,100,512]{2,1,0:T(8,128)(2,1)} %copy.21.refs_1_.refs_2_, bf16[1792,1536]{1,0:T(8,128)(2,1)} %get-tuple-element.45.refs_2_, f32[1792,512]{1,0:T(8,128)} %get-tuple-element.46.refs_3_, ...), custom_call_target="tpu_custom_call" | custom-call | flops 12099999744 | bytes 11000000 | tf_op jit(solution)/shard_map/input_bwd/pallas_call | solution.py:647
  187.6 2.1 collective-permute-start.26
  189.7 2.3 collective-permute-start.24
  192.1 3.3 %copy.25 = bf16[16,100,512]{2,0,1:T(8,128)(2,1)} copy(bf16[16,100,512]{2,1,0:T(8,128)(2,1)} %get-tuple-element.57) | data formatting | bytes 3276800
  201.4 2.8 %collective-permute-done.28 = bf16[4,192,128]{2,1,0:T(8,128)(2,1)S(1)} collective-permute-done((bf16[4,192,128]{2,1,0:T(8,128)(2,1)S(1)}, bf16[4,192,128]{2,1,0:T(8,128)(2,1)S(1)}, u32[]{:S(2)}, u32[]{:S(2)}) %collective-permute-start.28) | collective-permute-done | bytes 196640 | tf_op jit(solution)/shard_map/ppermute | solution.py:669
  204.2 2.8 %collective-permute-done.30 = bf16[4,192,128]{2,1,0:T(8,128)(2,1)S(1)} collective-permute-done((bf16[4,192,128]{2,1,0:T(8,128)(2,1)S(1)}, bf16[4,192,128]{2,1,0:T(8,128)(2,1)S(1)}, u32[]{:S(2)}, u32[]{:S(2)}) %collective-permute-start.30) | collective-permute-done | bytes 196640 | tf_op jit(solution)/shard_map/ppermute | solution.py:669
  218.9 3.1 %collective-permute-done.32 = bf16[192,128]{1,0:T(8,128)(2,1)S(1)} collective-permute-done((bf16[192,128]{1,0:T(8,128)(2,1)S(1)}, bf16[192,128]{1,0:T(8,128)(2,1)S(1)}, u32[]{:S(2)}, u32[]{:S(2)}) %collective-permute-start.32) | collective-permute-done | bytes 49184 | tf_op jit(solution)/shard_map/ppermute | solution.py:669
  222.1 3.3 %collective-permute-done.35 = bf16[4,576,128]{2,1,0:T(8,128)(2,1)S(1)} collective-permute-done((bf16[4,576,128]{2,1,0:T(8,128)(2,1)S(1)}, bf16[4,576,128]{2,1,0:T(8,128)(2,1)S(1)}, u32[]{:S(2)}, u32[]{:S(2)}) %collective-permute-start.35) | collective-permute-done | bytes 589856 | tf_op jit(solution)/shard_map/ppermute | solution.py:669
  225.4 8.2 %collective-permute-done.37 = bf16[4,576,128]{2,1,0:T(8,128)(2,1)S(1)} collective-permute-done((bf16[4,576,128]{2,1,0:T(8,128)(2,1)S(1)}, bf16[4,576,128]{2,1,0:T(8,128)(2,1)S(1)}, u32[]{:S(2)}, u32[]{:S(2)}) %collective-permute-start.37) | collective-permute-done | bytes 589856 | tf_op jit(solution)/shard_map/ppermute | solution.py:669
  235.7 2.1 collective-permute-start.40
  242.8 4.0 %collective-permute-done.39 = bf16[576,128]{1,0:T(8,128)(2,1)S(1)} collective-permute-done((bf16[576,128]{1,0:T(8,128)(2,1)S(1)}, bf16[576,128]{1,0:T(8,128)(2,1)S(1)}, u32[]{:S(2)}, u32[]{:S(2)}) %collective-permute-start.39) | collective-permute-done | bytes 147488 | tf_op jit(solution)/shard_map/ppermute | solution.py:669
  (140 shorter events, 56.9 us)
Async XLA Ops:
  15.5 16.9 %collective-permute-start.8 = (bf16[4,224,128]{2,1,0:T(8,128)(2,1)S(1)}, bf16[4,224,128]{2,1,0:T(8,128)(2,1)S(1)}, u32[]{:S(2)}, u32[]{:S(2)}) collective-permute-start(bf16[4,224,128]{2,1,0:T(8,128)(2,1)S(1)} %pad_maximum_fusion.1.refs_3_.refs_10_), channel_id=1, source_target_pairs={{0,6},{1,7},{2,4},{3,5},{4,2},{5,3},{6,0},{7,1},{8,14},{9,15},{10,... | collective-permute-start | bytes 688136 | tf_op jit(solution)/shard_map/ppermute | solution.py:669
  18.0 8.6 %collective-permute-start.12 = (bf16[576,128]{1,0:T(8,128)(2,1)S(1)}, bf16[576,128]{1,0:T(8,128)(2,1)S(1)}, u32[]{:S(2)}, u32[]{:S(2)}) collective-permute-start(bf16[576,128]{1,0:T(8,128)(2,1)S(1)} %get-tuple-element.35), channel_id=1, source_target_pairs={{0,24},{8,16},{16,8},{24,0},{1,25},{9,17},{17,9},{25,1},{2,26},{10... | collective-permute-start | bytes 442376 | tf_op jit(solution)/shard_map/ppermute | solution.py:669
  20.6 11.8 %collective-permute-start.11 = (bf16[576,128]{1,0:T(8,128)(2,1)S(1)}, bf16[576,128]{1,0:T(8,128)(2,1)S(1)}, u32[]{:S(2)}, u32[]{:S(2)}) collective-permute-start(bf16[576,128]{1,0:T(8,128)(2,1)S(1)} %get-tuple-element.35), channel_id=1, source_target_pairs={{0,16},{8,24},{16,0},{24,8},{1,17},{9,25},{17,1},{25,9},{2,18},{10... | collective-permute-start | bytes 442376 | tf_op jit(solution)/shard_map/ppermute | solution.py:669
  20.6 12.3 %collective-permute-start.10 = (bf16[576,128]{1,0:T(8,128)(2,1)S(1)}, bf16[576,128]{1,0:T(8,128)(2,1)S(1)}, u32[]{:S(2)}, u32[]{:S(2)}) collective-permute-start(bf16[576,128]{1,0:T(8,128)(2,1)S(1)} %get-tuple-element.35), channel_id=1, source_target_pairs={{0,8},{8,0},{16,24},{24,16},{1,9},{9,1},{17,25},{25,17},{2,10},{10... | collective-permute-start | bytes 442376 | tf_op jit(solution)/shard_map/ppermute | solution.py:669
  22.4 11.0 %collective-permute-start.6 = (bf16[4,224,128]{2,1,0:T(8,128)(2,1)S(1)}, bf16[4,224,128]{2,1,0:T(8,128)(2,1)}, u32[]{:S(2)}, u32[]{:S(2)}) collective-permute-start(bf16[4,224,128]{2,1,0:T(8,128)(2,1)S(1)} %pad_maximum_fusion.1.refs_3_.refs_10_), channel_id=1, source_target_pairs={{0,4},{1,5},{2,6},{3,7},{4,0},{5,1},{6,2},{7,3},{8,12},{9,13},{10,... | collective-permute-start | bytes 688136 | tf_op jit(solution)/shard_map/ppermute | solution.py:669
  26.6 8.4 %collective-permute-start.4 = (bf16[4,224,128]{2,1,0:T(8,128)(2,1)S(1)}, bf16[4,224,128]{2,1,0:T(8,128)(2,1)}, u32[]{:S(2)}, u32[]{:S(2)}) collective-permute-start(bf16[4,224,128]{2,1,0:T(8,128)(2,1)S(1)} %pad_maximum_fusion.1.refs_3_.refs_10_), channel_id=1, source_target_pairs={{0,2},{1,3},{2,0},{3,1},{4,6},{5,7},{6,4},{7,5},{8,10},{9,11},{10,... | collective-permute-start | bytes 688136 | tf_op jit(solution)/shard_map/ppermute | solution.py:669
  33.0 17.2 %collective-permute-start.18 = (bf16[4,576,128]{2,1,0:T(8,128)(2,1)S(1)}, bf16[4,576,128]{2,1,0:T(8,128)(2,1)S(1)}, u32[]{:S(2)}, u32[]{:S(2)}) collective-permute-start(bf16[4,576,128]{2,1,0:T(8,128)(2,1)S(1)} %pad_maximum_fusion.refs_5_), channel_id=1, source_target_pairs={{0,6},{1,7},{2,4},{3,5},{4,2},{5,3},{6,0},{7,1},{8,14},{9,15},{10,... | collective-permute-start | bytes 1769480 | tf_op jit(solution)/shard_map/ppermute | solution.py:669
  33.4 27.7 %collective-permute-start.16 = (bf16[4,576,128]{2,1,0:T(8,128)(2,1)S(1)}, bf16[4,576,128]{2,1,0:T(8,128)(2,1)S(1)}, u32[]{:S(2)}, u32[]{:S(2)}) collective-permute-start(bf16[4,576,128]{2,1,0:T(8,128)(2,1)S(1)} %pad_maximum_fusion.refs_5_), channel_id=1, source_target_pairs={{0,4},{1,5},{2,6},{3,7},{4,0},{5,1},{6,2},{7,3},{8,12},{9,13},{10,... | collective-permute-start | bytes 1769480 | tf_op jit(solution)/shard_map/ppermute | solution.py:669
  35.1 26.1 %collective-permute-start.14 = (bf16[4,576,128]{2,1,0:T(8,128)(2,1)S(1)}, bf16[4,576,128]{2,1,0:T(8,128)(2,1)}, u32[]{:S(2)}, u32[]{:S(2)}) collective-permute-start(bf16[4,576,128]{2,1,0:T(8,128)(2,1)S(1)} %pad_maximum_fusion.refs_5_), channel_id=1, source_target_pairs={{0,2},{1,3},{2,0},{3,1},{4,6},{5,7},{6,4},{7,5},{8,10},{9,11},{10,... | collective-permute-start | bytes 1769480 | tf_op jit(solution)/shard_map/ppermute | solution.py:669
  36.6 8.9 %collective-permute-start.7 = (bf16[4,224,128]{2,1,0:T(8,128)(2,1)}, bf16[4,224,128]{2,1,0:T(8,128)(2,1)}, u32[]{:S(2)}, u32[]{:S(2)}) collective-permute-start(bf16[4,224,128]{2,1,0:T(8,128)(2,1)} %collective-permute-done.6.refs_7_.refs_14_), channel_id=1, source_target_pairs={{0,1},{1,0},{2,3},{3,2},{4,5},{5,4},{6,7},{7,6},{8,9},{9,8},{10,11... | collective-permute-start | bytes 688136 | tf_op jit(solution)/shard_map/ppermute | solution.py:669
  38.0 23.7 %collective-permute-start.5 = (bf16[4,224,128]{2,1,0:T(8,128)(2,1)}, bf16[4,224,128]{2,1,0:T(8,128)(2,1)}, u32[]{:S(2)}, u32[]{:S(2)}) collective-permute-start(bf16[4,224,128]{2,1,0:T(8,128)(2,1)} %collective-permute-done.4.refs_5_.refs_12_), channel_id=1, source_target_pairs={{0,1},{1,0},{2,3},{3,2},{4,5},{5,4},{6,7},{7,6},{8,9},{9,8},{10,11... | collective-permute-start | bytes 688136 | tf_op jit(solution)/shard_map/ppermute | solution.py:669
  45.5 48.9 %collective-permute-start.13 = (bf16[4,576,128]{2,1,0:T(8,128)(2,1)S(1)}, bf16[4,576,128]{2,1,0:T(8,128)(2,1)S(1)}, u32[]{:S(2)}, u32[]{:S(2)}) collective-permute-start(bf16[4,576,128]{2,1,0:T(8,128)(2,1)S(1)} %pad_maximum_fusion.refs_5_), channel_id=1, source_target_pairs={{0,1},{1,0},{2,3},{3,2},{4,5},{5,4},{6,7},{7,6},{8,9},{9,8},{10,11... | collective-permute-start | bytes 1769480 | tf_op jit(solution)/shard_map/ppermute | solution.py:669
  50.2 44.3 %collective-permute-start.19 = (bf16[4,576,128]{2,1,0:T(8,128)(2,1)S(1)}, bf16[4,576,128]{2,1,0:T(8,128)(2,1)S(1)}, u32[]{:S(2)}, u32[]{:S(2)}) collective-permute-start(bf16[4,576,128]{2,1,0:T(8,128)(2,1)S(1)} %collective-permute-done.18.refs_11_), channel_id=1, source_target_pairs={{0,1},{1,0},{2,3},{3,2},{4,5},{5,4},{6,7},{7,6},{8,9},{9,8},{10,11... | collective-permute-start | bytes 1769480 | tf_op jit(solution)/shard_map/ppermute | solution.py:669
  61.1 33.4 %collective-permute-start.17 = (bf16[4,576,128]{2,1,0:T(8,128)(2,1)S(1)}, bf16[4,576,128]{2,1,0:T(8,128)(2,1)}, u32[]{:S(2)}, u32[]{:S(2)}) collective-permute-start(bf16[4,576,128]{2,1,0:T(8,128)(2,1)S(1)} %collective-permute-done.16.refs_9_), channel_id=1, source_target_pairs={{0,1},{1,0},{2,3},{3,2},{4,5},{5,4},{6,7},{7,6},{8,9},{9,8},{10,11... | collective-permute-start | bytes 1769480 | tf_op jit(solution)/shard_map/ppermute | solution.py:669
  61.1 33.4 %collective-permute-start.15 = (bf16[4,576,128]{2,1,0:T(8,128)(2,1)}, bf16[4,576,128]{2,1,0:T(8,128)(2,1)}, u32[]{:S(2)}, u32[]{:S(2)}) collective-permute-start(bf16[4,576,128]{2,1,0:T(8,128)(2,1)} %collective-permute-done.14.refs_7_), channel_id=1, source_target_pairs={{0,1},{1,0},{2,3},{3,2},{4,5},{5,4},{6,7},{7,6},{8,9},{9,8},{10,11... | collective-permute-start | bytes 1769480 | tf_op jit(solution)/shard_map/ppermute | solution.py:669
  166.4 30.7 %collective-permute-start.27 = (bf16[4,4,192,128]{3,2,1,0:T(8,128)(2,1)}, bf16[4,4,192,128]{3,2,1,0:T(8,128)(2,1)S(1)}, u32[]{:S(2)}, u32[]{:S(2)}) collective-permute-start(bf16[4,4,192,128]{3,2,1,0:T(8,128)(2,1)} %get-tuple-element.54), channel_id=1, source_target_pairs={{0,1},{1,0},{2,3},{3,2},{4,5},{5,4},{6,7},{7,6},{8,9},{9,8},{10,11... | collective-permute-start | bytes 2359304 | tf_op jit(solution)/shard_map/ppermute | solution.py:669
  166.5 42.0 %collective-permute-start.34 = (bf16[4,4,576,128]{3,2,1,0:T(8,128)(2,1)}, bf16[4,4,576,128]{3,2,1,0:T(8,128)(2,1)S(1)}, u32[]{:S(2)}, u32[]{:S(2)}) collective-permute-start(bf16[4,4,576,128]{3,2,1,0:T(8,128)(2,1)} %get-tuple-element.56), channel_id=1, source_target_pairs={{0,1},{1,0},{2,3},{3,2},{4,5},{5,4},{6,7},{7,6},{8,9},{9,8},{10,11... | collective-permute-start | bytes 7077896 | tf_op jit(solution)/shard_map/ppermute | solution.py:669
  187.6 9.4 %collective-permute-start.26 = (f32[24,512]{1,0:T(8,128)S(1)}, f32[24,512]{1,0:T(8,128)S(1)}, u32[]{:S(2)}, u32[]{:S(2)}) collective-permute-start(f32[24,512]{1,0:T(8,128)S(1)} %add_add_fusion.1), channel_id=1, source_target_pairs={{0,24},{8,16},{16,8},{24,0},{1,25},{9,17},{17,9},{25,1},{2,26},{10... | collective-permute-start | bytes 147464 | tf_op jit(solution)/shard_map/ppermute | solution.py:669
  198.0 9.0 %collective-permute-start.30 = (bf16[4,192,128]{2,1,0:T(8,128)(2,1)S(1)}, bf16[4,192,128]{2,1,0:T(8,128)(2,1)S(1)}, u32[]{:S(2)}, u32[]{:S(2)}) collective-permute-start(bf16[4,192,128]{2,1,0:T(8,128)(2,1)S(1)} %get-tuple-element.74), channel_id=1, source_target_pairs={{0,6},{1,7},{2,4},{3,5},{4,2},{5,3},{6,0},{7,1},{8,14},{9,15},{10,... | collective-permute-start | bytes 589832 | tf_op jit(solution)/shard_map/ppermute | solution.py:669
  199.2 9.2 %collective-permute-start.29 = (bf16[4,192,128]{2,1,0:T(8,128)(2,1)S(1)}, bf16[4,192,128]{2,1,0:T(8,128)(2,1)S(1)}, u32[]{:S(2)}, u32[]{:S(2)}) collective-permute-start(bf16[4,192,128]{2,1,0:T(8,128)(2,1)S(1)} %get-tuple-element.75), channel_id=1, source_target_pairs={{0,4},{1,5},{2,6},{3,7},{4,0},{5,1},{6,2},{7,3},{8,12},{9,13},{10,... | collective-permute-start | bytes 589832 | tf_op jit(solution)/shard_map/ppermute | solution.py:669
  209.1 16.3 %collective-permute-start.35 = (bf16[4,576,128]{2,1,0:T(8,128)(2,1)S(1)}, bf16[4,576,128]{2,1,0:T(8,128)(2,1)S(1)}, u32[]{:S(2)}, u32[]{:S(2)}) collective-permute-start(bf16[4,576,128]{2,1,0:T(8,128)(2,1)S(1)} %get-tuple-element.70), channel_id=1, source_target_pairs={{0,2},{1,3},{2,0},{3,1},{4,6},{5,7},{6,4},{7,5},{8,10},{9,11},{10,... | collective-permute-start | bytes 1769480 | tf_op jit(solution)/shard_map/ppermute | solution.py:669
  209.9 23.7 %collective-permute-start.37 = (bf16[4,576,128]{2,1,0:T(8,128)(2,1)S(1)}, bf16[4,576,128]{2,1,0:T(8,128)(2,1)S(1)}, u32[]{:S(2)}, u32[]{:S(2)}) collective-permute-start(bf16[4,576,128]{2,1,0:T(8,128)(2,1)S(1)} %get-tuple-element.71), channel_id=1, source_target_pairs={{0,6},{1,7},{2,4},{3,5},{4,2},{5,3},{6,0},{7,1},{8,14},{9,15},{10,... | collective-permute-start | bytes 1769480 | tf_op jit(solution)/shard_map/ppermute | solution.py:669
  211.3 23.6 %collective-permute-start.36 = (bf16[4,576,128]{2,1,0:T(8,128)(2,1)S(1)}, bf16[4,576,128]{2,1,0:T(8,128)(2,1)S(1)}, u32[]{:S(2)}, u32[]{:S(2)}) collective-permute-start(bf16[4,576,128]{2,1,0:T(8,128)(2,1)S(1)} %get-tuple-element.72), channel_id=1, source_target_pairs={{0,4},{1,5},{2,6},{3,7},{4,0},{5,1},{6,2},{7,3},{8,12},{9,13},{10,... | collective-permute-start | bytes 1769480 | tf_op jit(solution)/shard_map/ppermute | solution.py:669
  237.8 8.9 %collective-permute-start.39 = (bf16[576,128]{1,0:T(8,128)(2,1)S(1)}, bf16[576,128]{1,0:T(8,128)(2,1)S(1)}, u32[]{:S(2)}, u32[]{:S(2)}) collective-permute-start(bf16[576,128]{1,0:T(8,128)(2,1)S(1)} %get-tuple-element.78), channel_id=1, source_target_pairs={{0,16},{8,24},{16,0},{24,8},{1,17},{9,25},{17,1},{25,9},{2,18},{10... | collective-permute-start | bytes 442376 | tf_op jit(solution)/shard_map/ppermute | solution.py:669
  (40 other events, 304.6 us)

commit v2 on v1

--- a/solution.py
+++ b/solution.py
@@ -85,34 +85,48 @@
     return jnp.concatenate([x[:, i : i + TL] for i in range(0, x.shape[1], TL)], 0)
 
 
-def pack_body(wq, wp, w1, w2, vec, b1, a_o, b_o):
-    ra = 0
-    for i in range(0, wq.shape[1], TL):
-        a_o[ra : ra + wq.shape[0], :] = wq[:, i : i + TL]
-        ra += wq.shape[0]
-    buf = jnp.zeros((EXTRA, TL), f32)
-    own = vec.shape[1]
-    pieces = [p.astype(f32) for p in three(vec[...])] + [p.astype(f32) for p in three(b1[...])]
-    rows = [jnp.concatenate([p, jnp.zeros((8, TL - own), f32)], 1) for p in pieces[:3]]
-    tail = [jnp.concatenate([p, jnp.zeros((1, TL - b1.shape[1]), f32)], 1) for p in pieces[3:]]
-    tail = jnp.concatenate(tail + [jnp.zeros((5, TL), f32)], 0)
-    a_o[ra : ra + EXTRA, :] = jnp.concatenate(rows + [tail], 0).astype(bf16)
-    rb = 0
-    for w in (wp, w1, w2):
+def pack_body(count, *refs):
+    srcs, out = refs[:count], refs[count]
+    rest = refs[count + 1 :]
+    stage, flat, sem = rest[: len(srcs)], rest[-2], rest[-1]
+    moves = [pltpu.make_async_copy(x, y, sem.at[i]) for i, (x, y) in enumerate(zip(srcs, stage))]
+    for m in moves:
+        m.start()
+    at = 0
+    for m, w in zip(moves, stage):
+        m.wait()
+        if w.dtype == f32:
+            part = [p.astype(f32) for p in three(w[...])]
+            part = [jnp.concatenate([p, jnp.zeros((p.shape[0], TL - p.shape[1]), f32)], 1) for p in part]
+            part = jnp.concatenate(part, 0)
+            if part.shape[0] == 24:
+                kept = part
+                continue
+            part = jnp.concatenate([kept, part, jnp.zeros((EXTRA - 27, TL), f32)], 0)
+            flat[at : at + EXTRA, :] = part.astype(bf16)
+            at += EXTRA
+            continue
         for i in range(0, w.shape[1], TL):
-            b_o[rb : rb + w.shape[0], :] = w[:, i : i + TL]
-            rb += w.shape[0]
-
-
-def pack(geo, wq, wp, w1, w2, vec, b1):
-    S = jax.ShapeDtypeStruct
+            flat[at : at + w.shape[0], :] = w[:, i : i + TL]
+            at += w.shape[0]
+    last = pltpu.make_async_copy(flat, out, sem.at[count])
+    last.start()
+    last.wait()
+
+
+def pack(rows, *arrays):
+    V = pltpu.VMEM
     return pl.pallas_call(
-        pack_body,
-        out_shape=[S((geo.rows_a + EXTRA, TL), bf16), S((geo.rows_b, TL), bf16)],
-        compiler_params=pltpu.CompilerParams(vmem_limit_bytes=16 * 2**20),
-        cost_estimate=cost(1),
+        functools.partial(pack_body, len(arrays)),
+        in_specs=[anyspace()] * len(arrays),
+        out_specs=anyspace(),
+        out_shape=jax.ShapeDtypeStruct((rows, TL), bf16),
+        scratch_shapes=[V(x.shape, x.dtype) for x in arrays]
+        + [V((rows, TL), bf16), pltpu.SemaphoreType.DMA((len(arrays) + 1,))],
+        compiler_params=pltpu.CompilerParams(vmem_limit_bytes=60 * 2**20),
+        cost_estimate=cost(2),
         name="pack",
-    )(wq, wp, w1, w2, vec, b1)
+    )(*arrays)
 
 
 def copies_a(geo, bufs, me, wq, sem):
@@ -294,7 +308,7 @@
         xs[g * TP : g * TP + WT, :] = tok[g].astype(f32)
     xhat, _ = norm(xs[...])
     n1 = (xhat * vec[0:1, :] + vec[1:2, :]).astype(bf16)
-    n1_o[...] = n1
+    n1_o[...] = xhat.astype(bf16)
     q_o[...] = ((dot(n1, wide(wq, 0, NG)) + vec[2:3, :]) * SCALE).astype(bf16)
     k_o[...] = dot(n1, wide(wq, NG, NG)).astype(bf16)
     v_o[...] = (dot(n1, wide(wq, 2 * NG, NG)) + vec[3:4, :]).astype(bf16)
@@ -515,17 +529,25 @@
 
 
 def attn_bwd_body(geo, G, *refs):
-    me, q, k, v, p, da, n1, dc_o, gb_o, gt_o = refs[:10]
-    cores = 2 if geo.nw > 1 else 1
-    outs = refs[10 : 10 + cores]
-    bdq, bda, gq, gb, gt = refs[10 + cores :]
+    nb = geo.nw
+    me, q, k, v, p, da, xh, vec, gv2, gb1, place = refs[:11]
+    bufs = refs[11 : 11 + nb]
+    refs = refs[11 + nb :]
+    cores = 2 if nb > 1 else 1
+    dc_o, small_o = refs[:2]
+    outs = refs[2 : 2 + cores]
+    bdq, bda, gq, gb, gt, wq, rs, ex, sem = refs[2 + cores :]
     i = pl.program_id(0)
     n = pl.num_programs(0)
 
     @pl.when(i == 0)
     def _():
+        for m in copies_a(geo, bufs, me, wq, sem):
+            m.start()
         for ref in (bdq, bda, gq, gb, gt):
             ref[...] = jnp.zeros_like(ref)
+        for m in copies_a(geo, bufs, me, wq, sem):
+            m.wait()
 
     def window(g, carry):
         rows = pl.ds(pl.multiple_of(g * TP, 16), TP)
@@ -550,73 +572,110 @@
         return carry
 
     lax.fori_loop(0, G, window, 0)
-    n1t = n1[...].T
+    xt = xh[...].T
     for c in range(3):
         cols = slice(c * D, (c + 1) * D)
         dc = dc_o[:, cols]
-        t = dot(n1t, dc)
+        t = dot(xt, dc)
         for s in range(NG):
             gq[c * NG + s] += t[:, s * TL : (s + 1) * TL]
         gb[:, cols] += jnp.sum(dc.astype(f32), 0, keepdims=True)
 
     @pl.when(i == n - 1)
     def _():
-        gb_o[...] = gb[...]
-        gt_o[...] = gt[...]
+        sums = gb[...]
+        ones = jnp.ones((8, D), bf16)
+        gain = jnp.zeros((8, D), f32)
+        shift = jnp.zeros((8, D), f32)
+        for c in range(3):
+            w = wide(wq, c * NG, NG)
+            prod = wide(gq, c * NG, NG) * w.astype(f32)
+            for part in three(prod)[:2]:
+                gain = gain + dot(ones, part, NT)
+            part = [x.astype(f32) for x in three(sums[:, c * D : (c + 1) * D])]
+            part = jnp.concatenate(part + [jnp.zeros((5, D), f32)], 0).astype(bf16)
+            shift = shift + dot(part, w, NT)
+        g_col = jnp.broadcast_to(vec[0:1, :], (TL, D)).T
+        s_col = jnp.broadcast_to(vec[1:2, :], (TL, D)).T
+        for s in range(3 * NG):
+            gq[s] = gq[s] * g_col + s_col * sums[:, s * TL : (s + 1) * TL]
+        small_o[0:1, :] = gain[0:1]
+        small_o[1:2, :] = shift[0:1] + shift[1:2] + shift[2:3]
+        small_o[2:3, :] = sums[:, :D]
+        small_o[3:4, :] = sums[:, 2 * D :]
+        small_o[4:8, :] = gv2[4:8, :]
+        small_o[8:24, :TT] = table_sum(gt, place, rs)
+        for k in range(FF // TL):
+            small_o[8 + k : 9 + k, TT:] = gb1[:, k * TL : (k + 1) * TL]
+
+        if nb > 1:
+            for z in range(geo.nz):
+                ex[z] = extra_rows(geo, small_o, gb1, z)
 
         def rows(ref, w, z):
             at = pl.multiple_of(w * geo.r, geo.r)
-            return [ref[z * geo.cq + s, pl.ds(at, geo.r), :] for s in range(geo.cq)]
+            parts = [ref[z * geo.cq + s, pl.ds(at, geo.r), :] for s in range(geo.cq)]
+            return parts if nb == 1 else parts + [ex[z]]
 
         scatter_out(geo, me, [(gq, rows)], outs)
 
 
-def attn_bwd(geo, me, q, k, v, p, da, n1, G=4):
+def extra_rows(geo, small, gb1, z):
+    nh = HEADS // geo.nz
+    vec = small[0:8, z * TL : (z + 1) * TL]
+    first = z * (FF // geo.nz)
+    bias = [gb1[:, first + k * TL : first + (k + 1) * TL] for k in range(FF // geo.nz // TL)]
+    table = [small[8 + z * nh : 8 + (z + 1) * nh, k * TL : (k + 1) * TL] for k in range(TT // TL)]
+    rows = [vec] + bias + table
+    used = sum(r.shape[0] for r in rows)
+    return jnp.concatenate(rows + [jnp.zeros((EXTRA - used, TL), f32)], 0)
+
+
+def attn_bwd(geo, me, q, k, v, p, da, xh, vec, gv2, gb1, place, bufs, G=4):
     R = q.shape[0]
     B = R // TP
     blk = pl.BlockSpec((G * TP, D), lambda i: (i, 0))
     S = jax.ShapeDtypeStruct
     V = pltpu.VMEM
     cores = 2 if geo.nw > 1 else 1
-    gshape = (geo.nw // cores, geo.nz, geo.rows_a, TL)
+    gshape = (geo.nw // cores, geo.nz, geo.rows_a + (EXTRA if cores == 2 else 0), TL)
     return pl.pallas_call(
         functools.partial(attn_bwd_body, geo, G),
         grid=(B // G,),
-        in_specs=[smem(), blk, blk, blk, pl.BlockSpec((G, NG, TP, GH * TL), lambda i: (i, 0, 0, 0)), blk, blk],
-        out_specs=[pl.BlockSpec((G * TP, 3 * D), lambda i: (i, 0)), whole((1, 3 * D)), whole((NG, TP, GH * TL))]
-        + [whole(gshape)] * cores,
-        out_shape=[S((R, 3 * D), bf16), S((1, 3 * D), f32), S((NG, TP, GH * TL), f32)] + [S(gshape, bf16)] * cores,
+        in_specs=[smem(), blk, blk, blk, pl.BlockSpec((G, NG, TP, GH * TL), lambda i: (i, 0, 0, 0)), blk, blk]
+        + [whole(x.shape) for x in (vec, gv2, gb1, place)]
+        + [anyspace()] * len(bufs),
+        out_specs=[pl.BlockSpec((G * TP, 3 * D), lambda i: (i, 0)), whole((24, D))] + [whole(gshape)] * cores,
+        out_shape=[S((R, 3 * D), bf16), S((24, D), f32)] + [S(gshape, bf16)] * cores,
         scratch_shapes=[
             V((NG, GH * TL, TL), bf16),
             V((NG, GH * TL, TL), bf16),
             V((3 * NG, D, TL), f32),
             V((1, 3 * D), f32),
             V((NG, TP, GH * TL), f32),
+            V((3 * NG, D, TL), bf16),
+            V((2, HEADS * 16, TL), f32),
+            V((geo.nz, EXTRA, TL), f32),
+            pltpu.SemaphoreType.DMA,
         ],
         compiler_params=params(),
         cost_estimate=cost(30),
         name="attn_bwd",
-    )(me, q, k, v, p, da, n1)
+    )(me, q, k, v, p, da, xh, vec, gv2, gb1, place, *bufs)
 
 
 def input_bwd_body(geo, G, *refs):
     nb = geo.nw
-    me, tok, dc, dx1, vec, gv2, gb, gb1, gt, place = refs[:10]
-    bufs = refs[10 : 10 + nb]
-    gt_o, small_o, xs, gv, rs, wq, sem = refs[10 + nb :]
-    i = pl.program_id(0)
-    n = pl.num_programs(0)
-
-    @pl.when(i == 0)
+    me, tok, dc, dx1, vec = refs[:5]
+    bufs = refs[5 : 5 + nb]
+    gt_o, xs, wq, sem = refs[5 + nb :]
+
+    @pl.when(pl.program_id(0) == 0)
     def _():
         moves = copies_a(geo, bufs, me, wq, sem)
         for m in moves:
             m.start()
         xs[...] = jnp.zeros_like(xs)
-        gv[...] = jnp.zeros_like(gv)
-        small_o[8:24, :TT] = table_sum(gt, place, rs)
-        for k in range(FF // TL):
-            small_o[8 + k : 9 + k, TT:] = gb1[:, k * TL : (k + 1) * TL]
         for m in moves:
             m.wait()
 
@@ -624,21 +683,12 @@
         xs[g * TP : g * TP + WT, :] = tok[g].astype(f32)
     dn = dot(dc[...], wide(wq, 0, 3 * NG), NT)
     xhat, r = norm(xs[...])
-    gv[0:1, :] += jnp.sum(dn * xhat, 0, keepdims=True)
-    gv[1:2, :] += jnp.sum(dn, 0, keepdims=True)
     dx = dx1[...] + norm_back(dn, xhat, r, vec[0:1, :])
     for g in range(G):
         gt_o[g] = dx[g * TP : g * TP + WT].astype(bf16)
 
-    @pl.when(i == n - 1)
-    def _():
-        small_o[0:2, :] = gv[0:2, :]
-        small_o[2:3, :] = gb[:, :D]
-        small_o[3:4, :] = gb[:, 2 * D :]
-        small_o[4:8, :] = gv2[4:8, :]
-
-
-def input_bwd(geo, me, tok, dc, dx1, vec, gv2, gb, gb1, gt, place, bufs, G=4):
+
+def input_bwd(geo, me, tok, dc, dx1, vec, bufs, G=4):
     B = tok.shape[0]
     blk = pl.BlockSpec((G * TP, D), lambda i: (i, 0))
     win = pl.BlockSpec((G, WT, D), lambda i: (i, 0, 0))
@@ -647,54 +697,119 @@
     return pl.pallas_call(
         functools.partial(input_bwd_body, geo, G),
         grid=(B // G,),
-        in_specs=[smem(), win, pl.BlockSpec((G * TP, 3 * D), lambda i: (i, 0)), blk]
-        + [whole(x.shape) for x in (vec, gv2, gb, gb1, gt, place)]
+        in_specs=[smem(), win, pl.BlockSpec((G * TP, 3 * D), lambda i: (i, 0)), blk, whole(vec.shape)]
         + [anyspace()] * len(bufs),
-        out_specs=[win, whole((24, D))],
-        out_shape=[S(tok.shape, bf16), S((24, D), f32)],
-        scratch_shapes=[
-            V((G * TP, D), f32),
-            V((8, D), f32),
-            V((2, HEADS * 16, TL), f32),
-            V((3 * NG, D, TL), bf16),
-            pltpu.SemaphoreType.DMA,
+        out_specs=win,
+        out_shape=S(tok.shape, bf16),
+        scratch_shapes=[V((G * TP, D), f32), V((3 * NG, D, TL), bf16), pltpu.SemaphoreType.DMA],
+        compiler_params=params(),
+        cost_estimate=cost(10),
+        name="input_bwd",
+    )(me, tok, dc, dx1, vec, *bufs)
+
+
+def finish_body(geo, nz, *refs):
+    me, low_a, low_b = refs[:3]
+    got_b = refs[3 : 2 + nz]
+    got_a = refs[2 + nz : 1 + 2 * nz]
+    gq_o, gp_o, g1_o, g2_o, vec_o, b1_o, tab_o, tab = refs[1 + 2 * nz :]
+    r, r2 = geo.r, geo.r2
+    rows = geo.rows_a + EXTRA
+
+    def total(low, got, lo, n):
+        out = low[0, lo : lo + n, :].astype(f32)
+        for x in got:
+            out = out + x[lo : lo + n, :].astype(f32)
+        return out
+
+    for i in range(geo.cq):
+        gq_o[:, i * TL : (i + 1) * TL] = total(low_a, got_a, i * r, r)
+    at = 0
+    for ref, n in ((gp_o, geo.cp), (g1_o, geo.c1)):
+        for i in range(n):
+            ref[:, i * TL : (i + 1) * TL] = total(low_b, got_b, at, r)
+            at += r
+    wide_z = D // nz
+    for k in range(r2 // TL):
+        g2_o[k * TL : (k + 1) * TL, :] = total(low_b, got_b, at, wide_z).T
+        at += wide_z
+    nb = FF // nz // TL
+    small = total(low_a, got_a, geo.rows_a, 16)
+    own, own1 = vec_o.shape[1], b1_o.shape[1]
+    vec_o[...] = pltpu.roll(small[:8], (TL - me[0] * own) % TL, 1)[:, :own]
+    first = me[0] * own1
+    b1 = pltpu.roll(small[8 : 8 + nb], (TL - first % TL) % TL, 1)
+    row = lax.broadcasted_iota(jnp.int32, b1.shape, 0) == first // TL
+    b1_o[...] = jnp.sum(jnp.where(row, b1, 0.0), 0, keepdims=True)[:, :own1]
+    nh = HEADS // nz
+    lo = 8 + nb
+    for e in range(nz):
+        t = low_a[e, geo.rows_a : rows, :].astype(f32)
+        for d in range(1, nz):
+            t = t + got_a[d - 1][rows + (e ^ d) * EXTRA : rows + ((e ^ d) + 1) * EXTRA, :].astype(f32)
+        for k in range(TT // TL):
+            tab[me[1] ^ e, :, k * TL : (k + 1) * TL] = t[lo + k * nh : lo + (k + 1) * nh]
+    full = jnp.concatenate([tab[z] for z in range(nz)], 0)
+    tab_o[...] = full.T[:TABLE]
+
+
+def finish(geo, nw, nz, me, low_a, low_b, got_b, got_a):
+    S = jax.ShapeDtypeStruct
+    vmem = pl.BlockSpec(memory_space=pltpu.VMEM)
+    return pl.pallas_call(
+        functools.partial(finish_body, geo, nz),
+        in_specs=[smem()] + [vmem] * (2 * nz),
+        out_specs=[vmem] * 7,
+        out_shape=[
+            S((geo.r, geo.cq * TL), f32),
+            S((geo.r, geo.cp * TL), f32),
+            S((geo.r, geo.c1 * TL), f32),
+            S((geo.r2, geo.cp * TL), f32),
+            S((8, D // (nw * nz)), f32),
+            S((1, FF // (nw * nz)), f32),
+            S((TABLE, HEADS), f32),
         ],
-        compiler_params=params(),
-        cost_estimate=cost(11),
-        name="input_bwd",
-    )(me, tok, dc, dx1, vec, gv2, gb, gb1, gt, place, *bufs)
+        scratch_shapes=[pltpu.VMEM((nz, HEADS // nz, TT), f32)],
+        compiler_params=pltpu.CompilerParams(vmem_limit_bytes=60 * 2**20),
+        cost_estimate=cost(3),
+        name="finish",
+    )(me, low_a, low_b, *got_b, *got_a)
 
 
 def swap(x, axis, size, d):
     return lax.ppermute(x, axis, [(i, i ^ d) for i in range(size)])
 
 
-def gather_pieces(buf, nw, nz):
-    mine = jnp.stack([buf] + [swap(buf, "fsdp", nz, e) for e in range(1, nz)])
-    planes = [mine] + [swap(mine, "win", nw, 2 * d) for d in range(1, nw // 2)]
-    out = []
-    for x in planes:
-        out += [x, swap(x, "win", nw, 1)]
-    return out
-
-
-def scatter_sum(keep, send, nw, nz):
-    got = swap(send, "win", nw, 1)
-    sums = [(keep[d].astype(f32) + got[d].astype(f32)).astype(bf16) for d in range(nw // 2)]
-    total = sums[0].astype(f32)
-    for d in range(1, nw // 2):
-        total = total + swap(sums[d], "win", nw, 2 * d).astype(f32)
-    low = total.astype(bf16)
-    own = total[0]
-    for e in range(1, nz):
-        own = own + swap(low[e], "fsdp", nz, e).astype(f32)
-    return own
-
-
-def sum_all(x, nw, nz):
-    x = x + swap(x, "win", nw, 1)
-    x = x + functools.reduce(jnp.add, [swap(x, "win", nw, 2 * d) for d in range(1, nw // 2)])
-    return x + functools.reduce(jnp.add, [swap(x, "fsdp", nz, e) for e in range(1, nz)])
+def after(x, *deps):
+    return lax.optimization_barrier((x, *deps))[0]
+
+
+def gather_z(buf, nz):
+    return jnp.stack([buf] + [swap(buf, "fsdp", nz, e) for e in range(1, nz)])
+
+
+def gather_xy(mine, nw):
+    return [mine] + [swap(mine, "win", nw, 2 * d) for d in range(1, nw // 2)]
+
+
+def gather_core(planes, nw):
+    return [y for x in planes for y in (x, swap(x, "win", nw, 1))]
+
+
+def sum_core(keep, got, nw):
+    return [(keep[d].astype(f32) + got[d].astype(f32)).astype(bf16) for d in range(nw // 2)]
+
+
+def swap_xy(sums, nw):
+    return [sums[0]] + [swap(sums[d], "win", nw, 2 * d) for d in range(1, nw // 2)]
+
+
+def sum_xy(parts):
+    return functools.reduce(jnp.add, [x.astype(f32) for x in parts]).astype(bf16)
+
+
+def swap_z(low, nz):
+    return [swap(low[e], "fsdp", nz, e) for e in range(1, nz)]
 
 
 def unslab(x, n):
@@ -710,18 +825,46 @@
 
 def body(nw, nz, tokens, live, vectors, fc1_bias, w_qkv, w_proj, w_fc1, w_fc2, rel_table, cotangent):
     both = ("fsdp", "win")
-    fast = D // nz % TL == 0 and FF // nw % TL == 0 and D // nw % 16 == 0 and nw > 1 and nz > 1
+    fast = D // nz == TL and FF // nw % TL == 0 and D // nw % 16 == 0 and nw > 1 and nz > 1
     fast = fast and nw & (nw - 1) == 0 and nz & (nz - 1) == 0
     place = offset_place()
     table = jnp.pad(rel_table.T, ((0, 0), (0, TT - TABLE)))
+    dev = lax.axis_index(both)
+    own, own1 = D // (nw * nz), FF // (nw * nz)
     if fast:
         geo = Geometry(nw, nz)
         me = jnp.stack([lax.axis_index("win"), lax.axis_index("fsdp")]).astype(jnp.int32)
-        buf_a, buf_b = pack(geo, w_qkv, w_proj, w_fc1, w_fc2, vectors, fc1_bias.reshape(1, -1))
-        bufs_a = gather_pieces(buf_a, nw, nz)
-        bufs_b = gather_pieces(buf_b, nw, nz)
+        buf_a = pack(geo.rows_a + EXTRA, w_qkv, vectors, fc1_bias.reshape(1, -1))
+        buf_b = pack(geo.rows_b, w_proj, w_fc1, w_fc2)
+        mine_a = gather_z(buf_a, nz)
         pb = bias(table, place)
-        n1, q, k, v, p, att, vec, b1 = attn_fwd(geo, me, tokens, pb, bufs_a)
+        planes_a = gather_xy(mine_a, nw)
+        mine_b = gather_z(after(buf_b, mine_a), nz)
+        bufs_a = gather_core(planes_a, nw)
+        planes_b = gather_xy(after(mine_b, *bufs_a), nw)
+        xh, q, k, v, p, att, vec, b1 = attn_fwd(geo, me, tokens, pb, bufs_a)
+        planes_b = lax.optimization_barrier((*planes_b, att))[:-1]
+        bufs_b = gather_core(planes_b, nw)
+        out, dx1, da, gv2, gb1, keep_b, send_b = mlp(geo, me, live, tokens, cotangent, att, bufs_b, vec, b1)
+        sums_b = sum_core(keep_b, swap(send_b, "win", nw, 1), nw)
+        parts_b = swap_xy(sums_b, nw)
+        da = after(da, *sums_b)
+        dc, _, keep_a, send_a = attn_bwd(geo, me, q, k, v, p, da, xh, vec, gv2, gb1, place, bufs_a)
+        *parts_b, send_a = lax.optimization_barrier((*parts_b, send_a))
+        low_b = sum_xy(parts_b)
+        sums_a = sum_core(keep_a, swap(send_a, "win", nw, 1), nw)
+        parts_a = swap_xy(sums_a, nw)
+        own_b = swap_z(low_b, nz)
+        dc = after(dc, *sums_a)
+        grad_tokens = input_bwd(geo, me, tokens, dc, dx1, vec, bufs_a)
+        parts_a = lax.optimization_barrier((*parts_a, grad_tokens))[:-1]
+        low_a = sum_xy(parts_a)
+        tail = low_a[:, geo.rows_a :].reshape(nz * EXTRA, TL)
+        own_a = [swap(jnp.concatenate([low_a[e], tail], 0), "fsdp", nz, e) for e in range(1, nz)]
+        grad_qkv, grad_proj, grad_one, grad_two, grad_vectors, grad_bias, grad_table = finish(
+            geo, nw, nz, me, low_a, low_b, own_b, own_a
+        )
+        grad_bias = grad_bias.reshape(-1)
     else:
         geo = Geometry(1, 1)
         me = jnp.zeros((2,), jnp.int32)
@@ -734,30 +877,21 @@
         vec = lax.all_gather(vectors, both, axis=1, tiled=True)
         b1 = lax.all_gather(fc1_bias, both, axis=0, tiled=True).reshape(1, -1)
         pb = bias(table, place)
-        n1, q, k, v, p, att = attn_fwd(geo, me, tokens, pb, bufs_a, vec)
-    out, dx1, da, gv2, gb1, *gw = mlp(geo, me, live, tokens, cotangent, att, bufs_b, vec, b1)
-    dc, gb, gt, *gq = attn_bwd(geo, me, q, k, v, p, da, n1)
-    grad_tokens, small = input_bwd(geo, me, tokens, dc, dx1, vec, gv2, gb, gb1, gt, place, bufs_a)
-    if fast:
-        own_b = scatter_sum(*gw, nw, nz)
-        own_a = scatter_sum(*gq, nw, nz)
-        small = sum_all(small, nw, nz)
-        grad_qkv = unslab(own_a, geo.cq)
-        grad_proj, grad_one, grad_two = split_b(geo, own_b)
-    else:
+        xh, q, k, v, p, att = attn_fwd(geo, me, tokens, pb, bufs_a, vec)
+        out, dx1, da, gv2, gb1, gw = mlp(geo, me, live, tokens, cotangent, att, bufs_b, vec, b1)
+        dc, small, gq = attn_bwd(geo, me, q, k, v, p, da, xh, vec, gv2, gb1, place, bufs_a)
+        grad_tokens = input_bwd(geo, me, tokens, dc, dx1, vec, bufs_a)
 
         def down(g):
             g = lax.psum_scatter(g.astype(bf16), "win", scatter_dimension=0, tiled=True)
             return lax.psum_scatter(g, "fsdp", scatter_dimension=1, tiled=True).astype(f32)
 
-        grad_qkv = down(unslab(gq[0][0, 0], geo.cq))
-        grad_proj, grad_one, grad_two = [down(g) for g in split_b(geo, gw[0][0, 0])]
+        grad_qkv = down(unslab(gq[0, 0], geo.cq))
+        grad_proj, grad_one, grad_two = [down(g) for g in split_b(geo, gw[0, 0])]
         small = lax.psum(small, both)
-    dev = lax.axis_index(both)
-    own, own1 = D // (nw * nz), FF // (nw * nz)
-    grad_vectors = lax.dynamic_slice_in_dim(small[:8], dev * own, own, 1)
-    grad_bias = lax.dynamic_slice_in_dim(small[8:, TT:].reshape(FF), dev * own1, own1, 0)
-    grad_table = small[8:, :TABLE].T
+        grad_vectors = lax.dynamic_slice_in_dim(small[:8], dev * own, own, 1)
+        grad_bias = lax.dynamic_slice_in_dim(small[8:, TT:].reshape(FF), dev * own1, own1, 0)
+        grad_table = small[8:, :TABLE].T
     return out, grad_tokens, grad_vectors, grad_bias, grad_qkv, grad_proj, grad_one, grad_two, grad_table
 
 

time: 250 us -> 198 us (0.79)
  waiting for transfers between devices: 65.2 us -> 14.1 us
  Pallas kernels: 116 us -> 124 us
  local copies, waits for them, and re-layouts: 20.2 us -> 14.5 us
  starting transfers between devices: 41.5 us -> 38.1 us
    ppermute x41 -> x34, waiting for transfers between devices: 65.2 us -> 14.1 us  [swap(): return lax.ppermute(x, axis, [(i, i ^ d) for i in range(size)])]
    pallas_call x1 -> x3, Pallas kernels: 0.03 us -> 5.34 us  [the longest x2 3.07 us: pack(): pl.pallas_call(functools.partial(pack_body, len(arrays)), in_specs=[anysp...]
    pallas_call x1, Pallas kernels: 29.1 us -> 33.7 us  [attn_bwd(): pl.pallas_call(functools.partial(attn_bwd_body, geo, G), grid=(B // G,),...]
    ppermute x41 -> x34, starting transfers between devices: 41.5 us -> 38.1 us  [swap(): return lax.ppermute(x, axis, [(i, i ^ d) for i in range(size)])]
    unnamed x50 -> x67, local copies, waits for them, and re-layouts: 16.9 us -> 14.4 us
  transfers between devices with their start and end apart: 41 -> 34, of which waited for: 21 -> 10; matrix products, arithmetic and copies ran while one was open for 5% -> 5% of each run, Pallas kernels for 18% -> 40%
where the time goes in v2:
time: 198 us; the launch traced here: 197 us
  Pallas kernels  124 us (63%)
  starting transfers between devices  38.1 us (19%)
  local copies, waits for them, and re-layouts  14.5 us (7%)
  waiting for transfers between devices  14.1 us (7%)
  other arithmetic  4.59 us (2%)
    pallas_call x1, Pallas kernels, mlp(): pl.pallas_call(functools.partial(mlp_body, geo, G, FC), grid=(B // G,), i...  41.8 us
    ppermute x34, starting transfers between devices, swap(): return lax.ppermute(x, axis, [(i, i ^ d) for i in range(size)])  38.1 us
    pallas_call x1, Pallas kernels, attn_bwd(): pl.pallas_call(functools.partial(attn_bwd_body, geo, G), grid=(B // G,),...  33.7 us
    pallas_call x1, Pallas kernels, attn_fwd(): pl.pallas_call(functools.partial(attn_fwd_body, geo, G, vec is not None),...  32.6 us
    unnamed x67, local copies, waits for them, and re-layouts  14.4 us
    ppermute x34, waiting for transfers between devices, swap(): return lax.ppermute(x, axis, [(i, i ^ d) for i in range(size)])  14.1 us
    pallas_call x1, Pallas kernels, input_bwd(): pl.pallas_call(functools.partial(input_bwd_body, geo, G), grid=(B // G,),...  9.79 us
  transfers between devices with their start and end apart: 34, of which 10 were waited for; matrix products, arithmetic and copies ran while one was open for 5% of the time, Pallas kernels for 40%

profile of v2, /device:TPU:0, one launch (start us, length us, event | category | flops | bytes accessed | tf_op | source)
XLA Modules:
  0.0 197.3 jit_solution(8838068861282132899)
XLA Ops:
  2.2 5.1 %collective-permute-start.2 = (bf16[224,128]{1,0:T(8,128)(2,1)}, bf16[224,128]{1,0:T(8,128)(2,1)S(1)}, u32[]{:S(2)}, u32[]{:S(2)}) collective-permute-start(bf16[224,128]{1,0:T(8,128)(2,1)} %pack.2), channel_id=1, source_target_pairs={{0,24},{8,16},{16,8},{24,0},{1,25},{9,17},{17,9},{25,1},{2,26},{10... | collective-permute-start | bytes 172040 | tf_op jit(solution)/shard_map/ppermute | solution.py:780
  9.9 2.6 %collective-permute-done.1 = bf16[224,128]{1,0:T(8,128)(2,1)S(1)} collective-permute-done((bf16[224,128]{1,0:T(8,128)(2,1)}, bf16[224,128]{1,0:T(8,128)(2,1)S(1)}, u32[]{:S(2)}, u32[]{:S(2)}) %collective-permute-start.1) | collective-permute-done | bytes 57376 | tf_op jit(solution)/shard_map/ppermute | solution.py:780
  12.6 2.7 %collective-permute-start.12 = (bf16[576,128]{1,0:T(8,128)(2,1)}, bf16[576,128]{1,0:T(8,128)(2,1)S(1)}, u32[]{:S(2)}, u32[]{:S(2)}) collective-permute-start(bf16[576,128]{1,0:T(8,128)(2,1)} %pack.3), channel_id=1, source_target_pairs={{0,24},{8,16},{16,8},{24,0},{1,25},{9,17},{17,9},{25,1},{2,26},{10... | collective-permute-start | bytes 442376 | tf_op jit(solution)/shard_map/ppermute | solution.py:780
  15.4 1.7 collective-permute-start.10
  17.2 2.5 %collective-permute-start.8 = (bf16[4,224,128]{2,1,0:T(8,128)(2,1)S(1)}, bf16[4,224,128]{2,1,0:T(8,128)(2,1)}, u32[]{:S(2)}, u32[]{:S(2)}) collective-permute-start(bf16[4,224,128]{2,1,0:T(8,128)(2,1)S(1)} %pad_maximum_fusion.1.refs_3_.refs_11_.refs_5_), channel_id=1, source_target_pairs={{0,6},{1,7},{2,4},{3,5},{4,2},{5,3},{6,0},{7,1},{8,14},{9,15},{10,... | collective-permute-start | bytes 688136 | tf_op jit(solution)/shard_map/ppermute | solution.py:780
  25.1 2.1 %copy.21.refs_1_.refs_2_ = bf16[16,100,512]{2,1,0:T(8,128)(2,1)} copy(bf16[16,100,512]{2,0,1:T(8,128)(2,1)S(1)} %copy-done.5) | data formatting | bytes 3276800 | tf_op args[0]
  33.2 1.7 collective-permute-start.15
  36.7 32.6 %attn_fwd.1 = (bf16[1792,512]{1,0:T(8,128)(2,1)}, bf16[1792,512]{1,0:T(8,128)(2,1)}, bf16[1792,512]{1,0:T(8,128)(2,1)}, bf16[1792,512]{1,0:T(8,128)(2,1)}, bf16[...) custom-call(s32[2]{0:T(128)} %pad_add_fusion.refs_0_, ...), custom_call_target="tpu_custom_call" | custom-call | flops 32999999488 | bytes 30000000 | tf_op jit(solution)/shard_map/attn_fwd/pallas_call | solution.py:350
  71.1 2.1 %copy.22.refs_3_ = bf16[16,100,512]{2,1,0:T(8,128)(2,1)} copy(bf16[16,100,512]{2,0,1:T(8,128)(2,1)S(1)} %copy-done.6) | data formatting | bytes 3276800 | tf_op args[9]
  74.9 41.8 %mlp.1 = (bf16[16,100,512]{2,1,0:T(8,128)(2,1)}, f32[1792,512]{1,0:T(8,128)}, bf16[1792,512]{1,0:T(8,128)(2,1)}, f32[8,512]{1,0:T(8,128)}, f32[1,2048]{1,0:T(1,1...) custom-call(s32[2]{0:T(128)} %pad_add_fusion.refs_0_, s32[1]{0:T(128)S(6)} %copy.27.refs_1_, ...), custom_call_target="tpu_custom_call" | custom-call | flops 48399998976 | bytes 44000000 | tf_op jit(solution)/shard_map/mlp/pallas_call | solution.py:503
  116.8 4.7 %collective-permute-done.20 = bf16[4,4,576,128]{3,2,1,0:T(8,128)(2,1)S(1)} collective-permute-done((bf16[4,4,576,128]{3,2,1,0:T(8,128)(2,1)}, bf16[4,4,576,128]{3,2,1,0:T(8,128)(2,1)S(1)}, u32[]{:S(2)}, u32[]{:S(2)}) %collective-permute-start.20) | collective-permute-done | bytes 2359328 | tf_op jit(solution)/shard_map/ppermute | solution.py:780
  121.5 2.3 %fusion.3 = (bf16[4,576,128]{2,1,0:T(8,128)(2,1)S(1)}, bf16[4,576,128]{2,1,0:T(8,128)(2,1)S(1)}, bf16[4,576,128]{2,1,0:T(8,128)(2,1)S(1)}, bf16[4,576,128]{2,1,0:T(8,128)(2,1)S(1)}) fusion(bf16[4,4,576,128]{3,2,1,0:T(8,128)(2,1)S(1)} %collective-permute-done.20, bf16[4,4,576,128]{3,2,1,0:T(8,128)(2,1)} %get-tuple-element.66), kind=kLoop, calls=%fused_computation.8 | loop fusion | flops 4718592 | bytes 7077888 | tf_op jit(solution)/shard_map/convert_element_type | solution.py:800
  123.7 1.8 collective-permute-start.23
  127.3 33.7 %attn_bwd.1 = (bf16[1792,1536]{1,0:T(8,128)(2,1)}, f32[24,512]{1,0:T(8,128)}, bf16[4,4,224,128]{3,2,1,0:T(8,128)(2,1)}, bf16[4,4,224,128]{3,2,1,0:T(8,128)(2,1)}) custom-call(s32[2]{0:T(128)} %pad_add_fusion.refs_0_, bf16[1792,512]{1,0:T(8,128)(2,1)} %get-tuple-element.61.refs_1_, bf16[1792,512]{1,0:T(8,128)(2,1)} %get-tuple-element.62.refs_2_, ...), custom_call_target="tpu_custom_call" | custom-call | flops 32999999488 | bytes 30000000 | tf_op jit(solution)/shard_map/attn_bwd/pallas_call | solution.py:642
  161.4 2.2 %collective-permute-start.30 = (bf16[576,128]{1,0:T(8,128)(2,1)S(1)}, bf16[576,128]{1,0:T(8,128)(2,1)S(1)}, u32[]{:S(2)}, u32[]{:S(2)}) collective-permute-start(bf16[576,128]{1,0:T(8,128)(2,1)S(1)} %get-tuple-element.110), channel_id=1, source_target_pairs={{0,24},{8,16},{16,8},{24,0},{1,25},{9,17},{17,9},{25,1},{2,26},{10... | collective-permute-start | bytes 442376 | tf_op jit(solution)/shard_map/ppermute | solution.py:780
  163.7 3.1 %collective-permute-start.29 = (bf16[576,128]{1,0:T(8,128)(2,1)S(1)}, bf16[576,128]{1,0:T(8,128)(2,1)S(1)}, u32[]{:S(2)}, u32[]{:S(2)}) collective-permute-start(bf16[576,128]{1,0:T(8,128)(2,1)S(1)} %get-tuple-element.111), channel_id=1, source_target_pairs={{0,16},{8,24},{16,0},{24,8},{1,17},{9,25},{17,1},{25,9},{2,18},{10... | collective-permute-start | bytes 442376 | tf_op jit(solution)/shard_map/ppermute | solution.py:780
  167.0 2.0 %collective-permute-start.27 = (bf16[4,224,128]{2,1,0:T(8,128)(2,1)S(1)}, bf16[4,224,128]{2,1,0:T(8,128)(2,1)S(1)}, u32[]{:S(2)}, u32[]{:S(2)}) collective-permute-start(bf16[4,224,128]{2,1,0:T(8,128)(2,1)S(1)} %get-tuple-element.106), channel_id=1, source_target_pairs={{0,6},{1,7},{2,4},{3,5},{4,2},{5,3},{6,0},{7,1},{8,14},{9,15},{10,... | collective-permute-start | bytes 688136 | tf_op jit(solution)/shard_map/ppermute | solution.py:780
  170.6 9.8 %input_bwd.1 = bf16[16,100,512]{2,1,0:T(8,128)(2,1)} custom-call(s32[2]{0:T(128)} %pad_add_fusion.refs_0_, bf16[16,100,512]{2,1,0:T(8,128)(2,1)} %copy.21.refs_1_.refs_2_, bf16[1792,1536]{1,0:T(8,128)(2,1)} %get-tuple-element.76.refs_2_, f32[1792,512]{1,0:T(8,128)} %get-tuple-element.77.refs_3_, f32[8,512]{1,0:T(8,128)} %get-tuple-element.58.refs_13_.refs_7_.refs_4_, ...), custom_call_target="tpu_custom_call" | custom-call | flops 11000000512 | bytes 10000000 | tf_op jit(solution)/shard_map/input_bwd/pallas_call | solution.py:697
  181.4 2.2 %collective-permute-start.33 = (bf16[352,128]{1,0:T(8,128)(2,1)S(1)}, bf16[352,128]{1,0:T(8,128)(2,1)S(1)}, u32[]{:S(2)}, u32[]{:S(2)}) collective-permute-start(bf16[352,128]{1,0:T(8,128)(2,1)S(1)} %get-tuple-element.116), channel_id=1, source_target_pairs={{0,24},{8,16},{16,8},{24,0},{1,25},{9,17},{17,9},{25,1},{2,26},{10... | collective-permute-start | bytes 270344 | tf_op jit(solution)/shard_map/ppermute | solution.py:780
  184.2 1.7 collective-permute-start.31
  185.9 1.7 copy.24
  187.6 1.7 copy.25
  189.9 2.3 %collective-permute-done.32.refs_7_ = bf16[352,128]{1,0:T(8,128)(2,1)S(1)} collective-permute-done((bf16[352,128]{1,0:T(8,128)(2,1)S(1)}, bf16[352,128]{1,0:T(8,128)(2,1)S(1)}, u32[]{:S(2)}, u32[]{:S(2)}) %collective-permute-start.32) | collective-permute-done | bytes 90144 | tf_op jit(solution)/shard_map/ppermute | solution.py:780
  193.4 2.3 %finish.1 = (f32[64,384]{1,0:T(8,128)}, f32[64,128]{1,0:T(8,128)}, f32[64,512]{1,0:T(8,128)}, f32[256,128]{1,0:T(8,128)}, f32[8,16]{1,0:T(8,128)}, /*index=5*/f32[1,64]{1,0:T(1,128)}, f32[361,16]{1,0:T(8,128)}) custom-call(s32[2]{0:T(128)} %pad_add_fusion.refs_0_, bf16[4,224,128]{2,1,0:T(8,128)(2,1)} %copy-done.8, bf16[4,576,128]{2,1,0:T(8,128)(2,1)} %copy-done.2, ...), custom_call_target="tpu_custom_call" | custom-call | flops 3300000000 | bytes 3000000 | tf_op jit(solution)/shard_map/finish/pallas_call | solution.py:759
  (131 shorter events, 29.2 us)
Async XLA Ops:
  2.2 7.8 %collective-permute-start.2 = (bf16[224,128]{1,0:T(8,128)(2,1)}, bf16[224,128]{1,0:T(8,128)(2,1)S(1)}, u32[]{:S(2)}, u32[]{:S(2)}) collective-permute-start(bf16[224,128]{1,0:T(8,128)(2,1)} %pack.2), channel_id=1, source_target_pairs={{0,24},{8,16},{16,8},{24,0},{1,25},{9,17},{17,9},{25,1},{2,26},{10... | collective-permute-start | bytes 172040 | tf_op jit(solution)/shard_map/ppermute | solution.py:780
  7.3 5.3 %collective-permute-start.1 = (bf16[224,128]{1,0:T(8,128)(2,1)}, bf16[224,128]{1,0:T(8,128)(2,1)S(1)}, u32[]{:S(2)}, u32[]{:S(2)}) collective-permute-start(bf16[224,128]{1,0:T(8,128)(2,1)} %pack.2), channel_id=1, source_target_pairs={{0,16},{8,24},{16,0},{24,8},{1,17},{9,25},{17,1},{25,9},{2,18},{10... | collective-permute-start | bytes 172040 | tf_op jit(solution)/shard_map/ppermute | solution.py:780
  12.6 8.9 %collective-permute-start.12 = (bf16[576,128]{1,0:T(8,128)(2,1)}, bf16[576,128]{1,0:T(8,128)(2,1)S(1)}, u32[]{:S(2)}, u32[]{:S(2)}) collective-permute-start(bf16[576,128]{1,0:T(8,128)(2,1)} %pack.3), channel_id=1, source_target_pairs={{0,24},{8,16},{16,8},{24,0},{1,25},{9,17},{17,9},{25,1},{2,26},{10... | collective-permute-start | bytes 442376 | tf_op jit(solution)/shard_map/ppermute | solution.py:780
  15.3 12.2 %collective-permute-start.11 = (bf16[576,128]{1,0:T(8,128)(2,1)}, bf16[576,128]{1,0:T(8,128)(2,1)S(1)}, u32[]{:S(2)}, u32[]{:S(2)}) collective-permute-start(bf16[576,128]{1,0:T(8,128)(2,1)} %pack.3), channel_id=1, source_target_pairs={{0,16},{8,24},{16,0},{24,8},{1,17},{9,25},{17,1},{25,9},{2,18},{10... | collective-permute-start | bytes 442376 | tf_op jit(solution)/shard_map/ppermute | solution.py:780
  15.4 14.6 %collective-permute-start.10 = (bf16[576,128]{1,0:T(8,128)(2,1)}, bf16[576,128]{1,0:T(8,128)(2,1)}, u32[]{:S(2)}, u32[]{:S(2)}) collective-permute-start(bf16[576,128]{1,0:T(8,128)(2,1)} %pack.3), channel_id=1, source_target_pairs={{0,8},{8,0},{16,24},{24,16},{1,9},{9,1},{17,25},{25,17},{2,10},{10... | collective-permute-start | bytes 442376 | tf_op jit(solution)/shard_map/ppermute | solution.py:780
  17.2 10.3 %collective-permute-start.8 = (bf16[4,224,128]{2,1,0:T(8,128)(2,1)S(1)}, bf16[4,224,128]{2,1,0:T(8,128)(2,1)}, u32[]{:S(2)}, u32[]{:S(2)}) collective-permute-start(bf16[4,224,128]{2,1,0:T(8,128)(2,1)S(1)} %pad_maximum_fusion.1.refs_3_.refs_11_.refs_5_), channel_id=1, source_target_pairs={{0,6},{1,7},{2,4},{3,5},{4,2},{5,3},{6,0},{7,1},{8,14},{9,15},{10,... | collective-permute-start | bytes 688136 | tf_op jit(solution)/shard_map/ppermute | solution.py:780
  19.6 9.2 %collective-permute-start.6 = (bf16[4,224,128]{2,1,0:T(8,128)(2,1)S(1)}, bf16[4,224,128]{2,1,0:T(8,128)(2,1)}, u32[]{:S(2)}, u32[]{:S(2)}) collective-permute-start(bf16[4,224,128]{2,1,0:T(8,128)(2,1)S(1)} %pad_maximum_fusion.1.refs_3_.refs_11_.refs_5_), channel_id=1, source_target_pairs={{0,4},{1,5},{2,6},{3,7},{4,0},{5,1},{6,2},{7,3},{8,12},{9,13},{10,... | collective-permute-start | bytes 688136 | tf_op jit(solution)/shard_map/ppermute | solution.py:780
  21.5 7.5 %collective-permute-start.4 = (bf16[4,224,128]{2,1,0:T(8,128)(2,1)S(1)}, bf16[4,224,128]{2,1,0:T(8,128)(2,1)}, u32[]{:S(2)}, u32[]{:S(2)}) collective-permute-start(bf16[4,224,128]{2,1,0:T(8,128)(2,1)S(1)} %pad_maximum_fusion.1.refs_3_.refs_11_.refs_5_), channel_id=1, source_target_pairs={{0,2},{1,3},{2,0},{3,1},{4,6},{5,7},{6,4},{7,5},{8,10},{9,11},{10,... | collective-permute-start | bytes 688136 | tf_op jit(solution)/shard_map/ppermute | solution.py:780
  33.2 36.1 %collective-permute-start.15 = (bf16[4,576,128]{2,1,0:T(8,128)(2,1)S(1)}, bf16[4,576,128]{2,1,0:T(8,128)(2,1)S(1)}, u32[]{:S(2)}, u32[]{:S(2)}) collective-permute-start(bf16[4,576,128]{2,1,0:T(8,128)(2,1)S(1)} %pad_maximum_fusion.refs_5_), channel_id=1, source_target_pairs={{0,6},{1,7},{2,4},{3,5},{4,2},{5,3},{6,0},{7,1},{8,14},{9,15},{10,... | collective-permute-start | bytes 1769480 | tf_op jit(solution)/shard_map/ppermute | solution.py:780
  34.9 34.4 %collective-permute-start.14 = (bf16[4,576,128]{2,1,0:T(8,128)(2,1)S(1)}, bf16[4,576,128]{2,1,0:T(8,128)(2,1)S(1)}, u32[]{:S(2)}, u32[]{:S(2)}) collective-permute-start(bf16[4,576,128]{2,1,0:T(8,128)(2,1)S(1)} %pad_maximum_fusion.refs_5_), channel_id=1, source_target_pairs={{0,4},{1,5},{2,6},{3,7},{4,0},{5,1},{6,2},{7,3},{8,12},{9,13},{10,... | collective-permute-start | bytes 1769480 | tf_op jit(solution)/shard_map/ppermute | solution.py:780
  36.2 33.1 %collective-permute-start.13 = (bf16[4,576,128]{2,1,0:T(8,128)(2,1)S(1)}, bf16[4,576,128]{2,1,0:T(8,128)(2,1)S(1)}, u32[]{:S(2)}, u32[]{:S(2)}) collective-permute-start(bf16[4,576,128]{2,1,0:T(8,128)(2,1)S(1)} %pad_maximum_fusion.refs_5_), channel_id=1, source_target_pairs={{0,2},{1,3},{2,0},{3,1},{4,6},{5,7},{6,4},{7,5},{8,10},{9,11},{10,... | collective-permute-start | bytes 1769480 | tf_op jit(solution)/shard_map/ppermute | solution.py:780
  123.7 37.2 %collective-permute-start.23 = (bf16[4,576,128]{2,1,0:T(8,128)(2,1)S(1)}, bf16[4,576,128]{2,1,0:T(8,128)(2,1)S(1)}, u32[]{:S(2)}, u32[]{:S(2)}) collective-permute-start(bf16[4,576,128]{2,1,0:T(8,128)(2,1)S(1)} %get-tuple-element.102), channel_id=1, source_target_pairs={{0,6},{1,7},{2,4},{3,5},{4,2},{5,3},{6,0},{7,1},{8,14},{9,15},{10,... | collective-permute-start | bytes 1769480 | tf_op jit(solution)/shard_map/ppermute | solution.py:780
  125.5 35.4 %collective-permute-start.22 = (bf16[4,576,128]{2,1,0:T(8,128)(2,1)S(1)}, bf16[4,576,128]{2,1,0:T(8,128)(2,1)S(1)}, u32[]{:S(2)}, u32[]{:S(2)}) collective-permute-start(bf16[4,576,128]{2,1,0:T(8,128)(2,1)S(1)} %get-tuple-element.103), channel_id=1, source_target_pairs={{0,4},{1,5},{2,6},{3,7},{4,0},{5,1},{6,2},{7,3},{8,12},{9,13},{10,... | collective-permute-start | bytes 1769480 | tf_op jit(solution)/shard_map/ppermute | solution.py:780
  126.8 34.1 %collective-permute-start.21 = (bf16[4,576,128]{2,1,0:T(8,128)(2,1)S(1)}, bf16[4,576,128]{2,1,0:T(8,128)(2,1)S(1)}, u32[]{:S(2)}, u32[]{:S(2)}) collective-permute-start(bf16[4,576,128]{2,1,0:T(8,128)(2,1)S(1)} %get-tuple-element.104), channel_id=1, source_target_pairs={{0,2},{1,3},{2,0},{3,1},{4,6},{5,7},{6,4},{7,5},{8,10},{9,11},{10,... | collective-permute-start | bytes 1769480 | tf_op jit(solution)/shard_map/ppermute | solution.py:780
  161.0 5.8 %collective-permute-start.24 = (bf16[4,4,224,128]{3,2,1,0:T(8,128)(2,1)}, bf16[4,4,224,128]{3,2,1,0:T(8,128)(2,1)S(1)}, u32[]{:S(2)}, u32[]{:S(2)}) collective-permute-start(bf16[4,4,224,128]{3,2,1,0:T(8,128)(2,1)} %get-tuple-element.75), channel_id=1, source_target_pairs={{0,1},{1,0},{2,3},{3,2},{4,5},{5,4},{6,7},{7,6},{8,9},{9,8},{10,11... | collective-permute-start | bytes 2752520 | tf_op jit(solution)/shard_map/ppermute | solution.py:780
  161.4 22.8 %collective-permute-start.30 = (bf16[576,128]{1,0:T(8,128)(2,1)S(1)}, bf16[576,128]{1,0:T(8,128)(2,1)S(1)}, u32[]{:S(2)}, u32[]{:S(2)}) collective-permute-start(bf16[576,128]{1,0:T(8,128)(2,1)S(1)} %get-tuple-element.110), channel_id=1, source_target_pairs={{0,24},{8,16},{16,8},{24,0},{1,25},{9,17},{17,9},{25,1},{2,26},{10... | collective-permute-start | bytes 442376 | tf_op jit(solution)/shard_map/ppermute | solution.py:780
  163.7 25.6 %collective-permute-start.29 = (bf16[576,128]{1,0:T(8,128)(2,1)S(1)}, bf16[576,128]{1,0:T(8,128)(2,1)S(1)}, u32[]{:S(2)}, u32[]{:S(2)}) collective-permute-start(bf16[576,128]{1,0:T(8,128)(2,1)S(1)} %get-tuple-element.111), channel_id=1, source_target_pairs={{0,16},{8,24},{16,0},{24,8},{1,17},{9,25},{17,1},{25,9},{2,18},{10... | collective-permute-start | bytes 442376 | tf_op jit(solution)/shard_map/ppermute | solution.py:780
  167.0 13.4 %collective-permute-start.27 = (bf16[4,224,128]{2,1,0:T(8,128)(2,1)S(1)}, bf16[4,224,128]{2,1,0:T(8,128)(2,1)S(1)}, u32[]{:S(2)}, u32[]{:S(2)}) collective-permute-start(bf16[4,224,128]{2,1,0:T(8,128)(2,1)S(1)} %get-tuple-element.106), channel_id=1, source_target_pairs={{0,6},{1,7},{2,4},{3,5},{4,2},{5,3},{6,0},{7,1},{8,14},{9,15},{10,... | collective-permute-start | bytes 688136 | tf_op jit(solution)/shard_map/ppermute | solution.py:780
  169.0 12.2 %collective-permute-start.26 = (bf16[4,224,128]{2,1,0:T(8,128)(2,1)S(1)}, bf16[4,224,128]{2,1,0:T(8,128)(2,1)S(1)}, u32[]{:S(2)}, u32[]{:S(2)}) collective-permute-start(bf16[4,224,128]{2,1,0:T(8,128)(2,1)S(1)} %get-tuple-element.107), channel_id=1, source_target_pairs={{0,4},{1,5},{2,6},{3,7},{4,0},{5,1},{6,2},{7,3},{8,12},{9,13},{10,... | collective-permute-start | bytes 688136 | tf_op jit(solution)/shard_map/ppermute | solution.py:780
  169.5 11.7 %collective-permute-start.25 = (bf16[4,224,128]{2,1,0:T(8,128)(2,1)S(1)}, bf16[4,224,128]{2,1,0:T(8,128)(2,1)S(1)}, u32[]{:S(2)}, u32[]{:S(2)}) collective-permute-start(bf16[4,224,128]{2,1,0:T(8,128)(2,1)S(1)} %get-tuple-element.108), channel_id=1, source_target_pairs={{0,2},{1,3},{2,0},{3,1},{4,6},{5,7},{6,4},{7,5},{8,10},{9,11},{10,... | collective-permute-start | bytes 688136 | tf_op jit(solution)/shard_map/ppermute | solution.py:780
  180.4 8.9 %collective-permute-start.28 = (bf16[576,128]{1,0:T(8,128)(2,1)S(1)}, bf16[576,128]{1,0:T(8,128)(2,1)S(1)}, u32[]{:S(2)}, u32[]{:S(2)}) collective-permute-start(bf16[576,128]{1,0:T(8,128)(2,1)S(1)} %get-tuple-element.112), channel_id=1, source_target_pairs={{0,8},{8,0},{16,24},{24,16},{1,9},{9,1},{17,25},{25,17},{2,10},{10... | collective-permute-start | bytes 442376 | tf_op jit(solution)/shard_map/ppermute | solution.py:780
  181.4 8.4 %collective-permute-start.33 = (bf16[352,128]{1,0:T(8,128)(2,1)S(1)}, bf16[352,128]{1,0:T(8,128)(2,1)S(1)}, u32[]{:S(2)}, u32[]{:S(2)}) collective-permute-start(bf16[352,128]{1,0:T(8,128)(2,1)S(1)} %get-tuple-element.116), channel_id=1, source_target_pairs={{0,24},{8,16},{16,8},{24,0},{1,25},{9,17},{17,9},{25,1},{2,26},{10... | collective-permute-start | bytes 270344 | tf_op jit(solution)/shard_map/ppermute | solution.py:780
  183.6 8.5 %collective-permute-start.32 = (bf16[352,128]{1,0:T(8,128)(2,1)S(1)}, bf16[352,128]{1,0:T(8,128)(2,1)S(1)}, u32[]{:S(2)}, u32[]{:S(2)}) collective-permute-start(bf16[352,128]{1,0:T(8,128)(2,1)S(1)} %get-tuple-element.117), channel_id=1, source_target_pairs={{0,16},{8,24},{16,0},{24,8},{1,17},{9,25},{17,1},{25,9},{2,18},{10... | collective-permute-start | bytes 270344 | tf_op jit(solution)/shard_map/ppermute | solution.py:780
  184.2 7.9 %collective-permute-start.31 = (bf16[352,128]{1,0:T(8,128)(2,1)S(1)}, bf16[352,128]{1,0:T(8,128)(2,1)S(1)}, u32[]{:S(2)}, u32[]{:S(2)}) collective-permute-start(bf16[352,128]{1,0:T(8,128)(2,1)S(1)} %get-tuple-element.118), channel_id=1, source_target_pairs={{0,8},{8,0},{16,24},{24,16},{1,9},{9,1},{17,25},{25,17},{2,10},{10... | collective-permute-start | bytes 270344 | tf_op jit(solution)/shard_map/ppermute | solution.py:780
  (41 other events, 246.9 us)

commit v3 on v2

--- a/solution.py
+++ b/solution.py
@@ -35,8 +35,8 @@
     return lax.dot_general(a, b, dims, preferred_element_type=f32)
 
 
-def params(n=1):
-    return pltpu.CompilerParams(dimension_semantics=("arbitrary",) * n, vmem_limit_bytes=60 * 2**20)
+def params(mib):
+    return pltpu.CompilerParams(dimension_semantics=("arbitrary",), vmem_limit_bytes=mib * 2**20)
 
 
 def cost(us):
@@ -181,13 +181,13 @@
         for half in range(2):
             zs[half, cj * HEADS : (cj + 1) * HEADS, :] = z[:, half * TL : (half + 1) * TL]
     for j in range(NG):
-        pb_o[j, WT:TP, :] = jnp.full((TP - WT, GH * TL), -1e30, f32)
+        pb_o[j, WT:TP, :] = jnp.zeros((TP - WT, GH * TL), f32)
         for h in range(GH):
             zh = strided(zs, j * GH + h, WS, HEADS)
             for rj in range(WS):
                 off = (WS - 1 - rj) * WS
                 part = zh if off == 0 else pltpu.roll(zh, 256 - off, 1)
-                pb_o[j, rj * WS : (rj + 1) * WS, h * TL : (h + 1) * TL] = part[:, :TL]
+                pb_o[j, rj * WS : (rj + 1) * WS, h * TL : (h + 1) * TL] = jnp.exp(part[:, :TL])
 
 
 def bias(table, place):
@@ -237,10 +237,10 @@
     return (t - m1 - xhat * m2) * r
 
 
-def fill_blocks(bd, part):
+def spread(part):
     lane = lax.broadcasted_iota(jnp.int32, (1, TL), 1) // HD
-    for h in range(GH):
-        bd[h * TL : h * TL + TP, :] = jnp.where(lane == h, part, jnp.zeros_like(part))
+    none = jnp.zeros((TL - TP, TL), part.dtype)
+    return jnp.concatenate([x for h in range(GH) for x in (jnp.where(lane == h, part, jnp.zeros_like(part)), none)], 0)
 
 
 def diag_t(full):
@@ -281,7 +281,7 @@
     if not vectors_in:
         vec, b1_o = refs[:2]
         refs = refs[2:]
-    xs, bd, wq, tmp, sem, sem2 = refs
+    xs, wq, tmp, sem, sem2 = refs
 
     @pl.when(pl.program_id(0) == 0)
     def _():
@@ -296,7 +296,6 @@
             for m in small:
                 m.start()
         xs[...] = jnp.zeros_like(xs)
-        bd[...] = jnp.zeros_like(bd)
         if not vectors_in:
             for m in small:
                 m.wait()
@@ -306,6 +305,7 @@
 
     for g in range(G):
         xs[g * TP : g * TP + WT, :] = tok[g].astype(f32)
+        xs[g * TP + WT : (g + 1) * TP, :] = tok[g, : TP - WT, :].astype(f32)
     xhat, _ = norm(xs[...])
     n1 = (xhat * vec[0:1, :] + vec[1:2, :]).astype(bf16)
     n1_o[...] = xhat.astype(bf16)
@@ -315,24 +315,24 @@
 
     def window(g, carry):
         rows = pl.ds(pl.multiple_of(g * TP, 16), TP)
+        cols = [slice(j * TL, (j + 1) * TL) for j in range(NG)]
+        ks = [k_o[rows, c] for c in cols]
+        vs = [v_o[rows, c] for c in cols]
+        qs = [spread(q_o[rows, c]) for c in cols]
+        scores = [dot(ks[j], qs[j], NT) for j in range(NG)]
+        ps, outs = [], []
         for j in range(NG):
-            cols = slice(j * TL, (j + 1) * TL)
-            qg = q_o[rows, cols]
-            kg = k_o[rows, cols]
-            vg = v_o[rows, cols]
-            b = bd.at[j]
-            fill_blocks(b, qg)
-            s = dot(kg, b[...], NT) + pb[j]
-            m = jnp.max(s, 0, keepdims=True)
-            e = jnp.exp(s - m)
-            l = jnp.sum(e, 0, keepdims=True)
-            p = (e * (1.0 / l)).astype(bf16)
-            p_o[g, j] = p
-            at = diag_t(dot(vg, p, TN))
-            a_o[rows, cols] = at.T[:TP].astype(bf16)
+            s = scores[j]
+            e = jnp.exp(s - jnp.max(s, 0, keepdims=True)) * pb[j]
+            p = (e * (1.0 / jnp.sum(e, 0, keepdims=True))).astype(bf16)
+            ps.append(p)
+            outs.append(diag_t(dot(vs[j], p, TN)).T[:TP].astype(bf16))
+        for j in range(NG):
+            p_o[g, j] = ps[j]
+            a_o[rows, cols[j]] = outs[j]
         return carry
 
-    lax.fori_loop(0, G, window, 0)
+    lax.fori_loop(0, G, window, 0, unroll=G)
 
 
 def attn_fwd(geo, me, tok, pb, bufs, vec=None, G=4):
@@ -357,13 +357,12 @@
         out_shape=out_shape,
         scratch_shapes=[
             pltpu.VMEM((G * TP, D), f32),
-            pltpu.VMEM((NG, GH * TL, TL), bf16),
             pltpu.VMEM((3 * NG, D, TL), bf16),
             pltpu.VMEM((geo.nw, geo.nz, EXTRA, TL), bf16),
             pltpu.SemaphoreType.DMA,
             pltpu.SemaphoreType.DMA,
         ],
-        compiler_params=params(),
+        compiler_params=params(28),
         cost_estimate=cost(30),
         name="attn_fwd",
     )(me, tok, pb, *bufs, *given)
@@ -434,15 +433,19 @@
     dy = dyf.astype(bf16)
     dyt = dy.T
     ns = FC // TL
-    for c in range(FF // FC):
+    n = FF // FC
+
+    def first(c):
         cols = slice(c * FC, (c + 1) * FC)
         w1c = wide(w1, c * ns, ns)
         w2c = jnp.concatenate([w2[z, cols, :] for z in range(NG)], 1)
-        u = dot(n2, w1c) + b1[:, cols]
-        a, ga = gelu_both(u)
-        a = a.astype(bf16)
+        return w1c, w2c, dot(n2, w1c), dot(dy, w2c, NT)
+
+    def last(c):
+        cols = slice(c * FC, (c + 1) * FC)
+        w1c, w2c = work[c][:2]
+        a, du = mids[c]
         acc[...] += dot(a, w2c)
-        du = (dot(dy, w2c, NT) * ga).astype(bf16)
         t2 = dot(dyt, a)
         t1 = dot(n2t, du)
         for k in range(ns):
@@ -454,6 +457,18 @@
             dn2[...] = d
         else:
             dn2[...] += d
+
+    work = [first(c) for c in range(1)]
+    mids = []
+    for c in range(n + 1):
+        if c + 1 < n:
+            work.append(first(c + 1))
+        if c < n:
+            a, ga = gelu_both(work[c][2] + b1[:, c * FC : (c + 1) * FC])
+            mids.append((a.astype(bf16), (work[c][3] * ga).astype(bf16)))
+        if c >= 1:
+            last(c - 1)
+    n = pl.num_programs(0)
     for g in range(G):
         mask = (i * G + g < live[0]).astype(f32)
         out_o[g] = (acc[g * TP : g * TP + WT, :] * mask).astype(bf16)
@@ -522,7 +537,7 @@
             V((NG, FF, TL), bf16),
             pltpu.SemaphoreType.DMA,
         ],
-        compiler_params=params(),
+        compiler_params=params(36),
         cost_estimate=cost(44),
         name="mlp",
     )(me, live, tok, cot, attn, *bufs, vec, b1)
@@ -536,7 +551,7 @@
     cores = 2 if nb > 1 else 1
     dc_o, small_o = refs[:2]
     outs = refs[2 : 2 + cores]
-    bdq, bda, gq, gb, gt, wq, rs, ex, sem = refs[2 + cores :]
+    gq, gb, gt, wq, rs, ex, sem = refs[2 + cores :]
     i = pl.program_id(0)
     n = pl.num_programs(0)
 
@@ -544,34 +559,44 @@
     def _():
         for m in copies_a(geo, bufs, me, wq, sem):
             m.start()
-        for ref in (bdq, bda, gq, gb, gt):
+        for ref in (gq, gb, gt):
             ref[...] = jnp.zeros_like(ref)
         for m in copies_a(geo, bufs, me, wq, sem):
             m.wait()
 
     def window(g, carry):
         rows = pl.ds(pl.multiple_of(g * TP, 16), TP)
+        cols = [slice(j * TL, (j + 1) * TL) for j in range(NG)]
+        ks = [k[rows, c] for c in cols]
+        vs = [v[rows, c] for c in cols]
+        bqs = [spread(q[rows, c]) for c in cols]
+        bas = [spread(da[rows, c]) for c in cols]
+        dps = [dot(vs[i], bas[i], NT) for i in range(2)]
+        dqs, dks, dvs, dss = [], [], [], []
+        pts = []
+        for j in range(NG + 1):
+            if j + 2 < NG:
+                dps.append(dot(vs[j + 2], bas[j + 2], NT))
+            if j < NG:
+                pts.append(p[g, j])
+                pf = pts[j].astype(f32)
+                t = pf * dps[j]
+                dss.append((t - pf * jnp.sum(t, 0, keepdims=True)).astype(bf16))
+            if 0 <= j - 0 < NG:
+                i = j - 0
+                dvs.append(dot(pts[i], bas[i]).astype(bf16))
+            if 0 <= j - 1 < NG:
+                i = j - 1
+                dks.append(dot(dss[i], bqs[i]).astype(bf16))
+                dqs.append((diag_t(dot(ks[i], dss[i], TN)).T[:TP] * SCALE).astype(bf16))
         for j in range(NG):
-            cols = slice(j * TL, (j + 1) * TL)
-            qg, kg, vg, dg = q[rows, cols], k[rows, cols], v[rows, cols], da[rows, cols]
-            bq, ba = bdq.at[j], bda.at[j]
-            fill_blocks(bq, qg)
-            fill_blocks(ba, dg)
-            pt = p[g, j]
-            pf = pt.astype(f32)
-            dp = dot(vg, ba[...], NT)
-            t = pf * dp
-            ds = (t - pf * jnp.sum(t, 0, keepdims=True)).astype(bf16)
-            gt[j] += ds.astype(f32)
-            dv = dot(pt, ba[...])
-            dk = dot(ds, bq[...])
-            dq = diag_t(dot(kg, ds, TN)).T[:TP] * SCALE
-            dc_o[rows, j * TL : (j + 1) * TL] = dq.astype(bf16)
-            dc_o[rows, D + j * TL : D + (j + 1) * TL] = dk.astype(bf16)
-            dc_o[rows, 2 * D + j * TL : 2 * D + (j + 1) * TL] = dv.astype(bf16)
+            gt[j] += dss[j].astype(f32)
+            dc_o[rows, j * TL : (j + 1) * TL] = dqs[j]
+            dc_o[rows, D + j * TL : D + (j + 1) * TL] = dks[j]
+            dc_o[rows, 2 * D + j * TL : 2 * D + (j + 1) * TL] = dvs[j]
         return carry
 
-    lax.fori_loop(0, G, window, 0)
+    lax.fori_loop(0, G, window, 0, unroll=G)
     xt = xh[...].T
     for c in range(3):
         cols = slice(c * D, (c + 1) * D)
@@ -648,8 +673,6 @@
         out_specs=[pl.BlockSpec((G * TP, 3 * D), lambda i: (i, 0)), whole((24, D))] + [whole(gshape)] * cores,
         out_shape=[S((R, 3 * D), bf16), S((24, D), f32)] + [S(gshape, bf16)] * cores,
         scratch_shapes=[
-            V((NG, GH * TL, TL), bf16),
-            V((NG, GH * TL, TL), bf16),
             V((3 * NG, D, TL), f32),
             V((1, 3 * D), f32),
             V((NG, TP, GH * TL), f32),
@@ -658,7 +681,7 @@
             V((geo.nz, EXTRA, TL), f32),
             pltpu.SemaphoreType.DMA,
         ],
-        compiler_params=params(),
+        compiler_params=params(32),
         cost_estimate=cost(30),
         name="attn_bwd",
     )(me, q, k, v, p, da, xh, vec, gv2, gb1, place, *bufs)
@@ -702,7 +725,7 @@
         out_specs=win,
         out_shape=S(tok.shape, bf16),
         scratch_shapes=[V((G * TP, D), f32), V((3 * NG, D, TL), bf16), pltpu.SemaphoreType.DMA],
-        compiler_params=params(),
+        compiler_params=params(24),
         cost_estimate=cost(10),
         name="input_bwd",
     )(me, tok, dc, dx1, vec, *bufs)

time: 198 us -> 177 us (0.89)
  Pallas kernels: 124 us -> 98.6 us
  local copies, waits for them, and re-layouts: 14.5 us -> 18.9 us
  waiting for transfers between devices: 14.1 us -> 17.4 us
  other arithmetic: 4.59 us -> 1.67 us
    pallas_call x1, Pallas kernels: 32.6 us -> 18.5 us  [attn_fwd(): pl.pallas_call(functools.partial(attn_fwd_body, geo, G, vec is not None),...]
    pallas_call x1, Pallas kernels: 33.7 us -> 24.2 us  [attn_bwd(): pl.pallas_call(functools.partial(attn_bwd_body, geo, G), grid=(B // G,),...]
    unnamed x67 -> x61, local copies, waits for them, and re-layouts: 14.4 us -> 18.8 us
    ppermute x34, waiting for transfers between devices: 14.1 us -> 17.4 us  [swap(): return lax.ppermute(x, axis, [(i, i ^ d) for i in range(size)])]
    pallas_call x1, Pallas kernels: 9.79 us -> 7.5 us  [input_bwd(): pl.pallas_call(functools.partial(input_bwd_body, geo, G), grid=(B // G,),...]
  transfers between devices with their start and end apart: 34 -> 34, of which waited for: 10 -> 15; matrix products, arithmetic and copies ran while one was open for 5% -> 4% of each run, Pallas kernels for 40% -> 30%
where the time goes in v3:
time: 177 us
  Pallas kernels  98.6 us (56%)
  starting transfers between devices  38.5 us (22%)
  local copies, waits for them, and re-layouts  18.9 us (11%)
  waiting for transfers between devices  17.4 us (10%)
    pallas_call x1, Pallas kernels, mlp(): pl.pallas_call(functools.partial(mlp_body, geo, G, FC), grid=(B // G,), i...  42 us
    ppermute x34, starting transfers between devices, swap(): return lax.ppermute(x, axis, [(i, i ^ d) for i in range(size)])  38.5 us
    pallas_call x1, Pallas kernels, attn_bwd(): pl.pallas_call(functools.partial(attn_bwd_body, geo, G), grid=(B // G,),...  24.2 us
    unnamed x61, local copies, waits for them, and re-layouts  18.8 us
    pallas_call x1, Pallas kernels, attn_fwd(): pl.pallas_call(functools.partial(attn_fwd_body, geo, G, vec is not None),...  18.5 us
    ppermute x34, waiting for transfers between devices, swap(): return lax.ppermute(x, axis, [(i, i ^ d) for i in range(size)])  17.4 us
    pallas_call x1, Pallas kernels, input_bwd(): pl.pallas_call(functools.partial(input_bwd_body, geo, G), grid=(B // G,),...  7.5 us
  transfers between devices with their start and end apart: 34, of which 15 were waited for; matrix products, arithmetic and copies ran while one was open for 4% of the time, Pallas kernels for 30%

profile of v3, /device:TPU:0, one launch (start us, length us, event | category | flops | bytes accessed | tf_op | source)
XLA Modules:
  0.0 176.8 jit_solution(7539113138952368009)
XLA Ops:
  2.2 5.1 %collective-permute-start.2 = (bf16[224,128]{1,0:T(8,128)(2,1)}, bf16[224,128]{1,0:T(8,128)(2,1)S(1)}, u32[]{:S(2)}, u32[]{:S(2)}) collective-permute-start(bf16[224,128]{1,0:T(8,128)(2,1)} %pack.2), channel_id=1, source_target_pairs={{0,24},{8,16},{16,8},{24,0},{1,25},{9,17},{17,9},{25,1},{2,26},{10... | collective-permute-start | bytes 172040 | tf_op jit(solution)/shard_map/ppermute | solution.py:803
  9.9 2.6 %collective-permute-done.1 = bf16[224,128]{1,0:T(8,128)(2,1)S(1)} collective-permute-done((bf16[224,128]{1,0:T(8,128)(2,1)}, bf16[224,128]{1,0:T(8,128)(2,1)S(1)}, u32[]{:S(2)}, u32[]{:S(2)}) %collective-permute-start.1) | collective-permute-done | bytes 57376 | tf_op jit(solution)/shard_map/ppermute | solution.py:803
  12.6 2.7 %collective-permute-start.12 = (bf16[576,128]{1,0:T(8,128)(2,1)}, bf16[576,128]{1,0:T(8,128)(2,1)S(1)}, u32[]{:S(2)}, u32[]{:S(2)}) collective-permute-start(bf16[576,128]{1,0:T(8,128)(2,1)} %pack.3), channel_id=1, source_target_pairs={{0,24},{8,16},{16,8},{24,0},{1,25},{9,17},{17,9},{25,1},{2,26},{10... | collective-permute-start | bytes 442376 | tf_op jit(solution)/shard_map/ppermute | solution.py:803
  15.4 1.7 collective-permute-start.10
  17.1 2.5 %collective-permute-start.8 = (bf16[4,224,128]{2,1,0:T(8,128)(2,1)S(1)}, bf16[4,224,128]{2,1,0:T(8,128)(2,1)S(1)}, u32[]{:S(2)}, u32[]{:S(2)}) collective-permute-start(bf16[4,224,128]{2,1,0:T(8,128)(2,1)S(1)} %pad_maximum_fusion.1.refs_3_.refs_11_.refs_5_), channel_id=1, source_target_pairs={{0,6},{1,7},{2,4},{3,5},{4,2},{5,3},{6,0},{7,1},{8,14},{9,15},{10,... | collective-permute-start | bytes 688136 | tf_op jit(solution)/shard_map/ppermute | solution.py:803
  25.1 2.4 %copy.21.refs_1_.refs_2_ = bf16[16,100,512]{2,1,0:T(8,128)(2,1)S(1)} copy(bf16[16,100,512]{2,0,1:T(8,128)(2,1)} %param.11) | data formatting | bytes 3276800 | tf_op args[0]
  30.6 1.9 %collective-permute-start.15 = (bf16[4,576,128]{2,1,0:T(8,128)(2,1)S(1)}, bf16[4,576,128]{2,1,0:T(8,128)(2,1)S(1)}, u32[]{:S(2)}, u32[]{:S(2)}) collective-permute-start(bf16[4,576,128]{2,1,0:T(8,128)(2,1)S(1)} %pad_maximum_fusion.refs_5_), channel_id=1, source_target_pairs={{0,6},{1,7},{2,4},{3,5},{4,2},{5,3},{6,0},{7,1},{8,14},{9,15},{10,... | collective-permute-start | bytes 1769480 | tf_op jit(solution)/shard_map/ppermute | solution.py:803
  34.1 18.5 %attn_fwd.1 = (bf16[1792,512]{1,0:T(8,128)(2,1)S(1)}, bf16[1792,512]{1,0:T(8,128)(2,1)S(1)}, bf16[1792,512]{1,0:T(8,128)(2,1)S(1)}, bf16[1792,512]{1,0:T(8,128)(...) custom-call(s32[2]{0:T(128)S(1)} %pad_add_fusion.refs_0_, ...), custom_call_target="tpu_custom_call" | custom-call | flops 32999999488 | bytes 30000000 | tf_op jit(solution)/shard_map/attn_fwd/pallas_call | solution.py:350
  52.6 2.9 %copy-done.5 = bf16[16,4,112,512]{3,2,1,0:T(8,128)(2,1)} copy-done((bf16[16,4,112,512]{3,2,1,0:T(8,128)(2,1)}, bf16[16,4,112,512]{3,2,1,0:T(8,128)(2,1)S(1)}, u32[]{:S(2)}) %copy-start.5) | copy-done | bytes 7340056
  64.3 42.0 %mlp.1 = (bf16[16,100,512]{2,1,0:T(8,128)(2,1)S(1)}, f32[1792,512]{1,0:T(8,128)}, bf16[1792,512]{1,0:T(8,128)(2,1)S(1)}, f32[8,512]{1,0:T(8,128)S(1)}, f32[1,204...) custom-call(s32[2]{0:T(128)S(1)} %pad_add_fusion.refs_0_, ...), custom_call_target="tpu_custom_call" | custom-call | flops 48399998976 | bytes 44000000 | tf_op jit(solution)/shard_map/mlp/pallas_call | solution.py:518
  106.5 4.4 %collective-permute-done.20 = bf16[4,4,576,128]{3,2,1,0:T(8,128)(2,1)S(1)} collective-permute-done((bf16[4,4,576,128]{3,2,1,0:T(8,128)(2,1)S(1)}, bf16[4,4,576,128]{3,2,1,0:T(8,128)(2,1)S(1)}, u32[]{:S(2)}, u32[]{:S(2)}) %collective-permute-start.20) | collective-permute-done | bytes 2359328 | tf_op jit(solution)/shard_map/ppermute | solution.py:803
  111.7 1.7 collective-permute-start.23
  116.7 24.2 %attn_bwd.1 = (bf16[1792,1536]{1,0:T(8,128)(2,1)S(1)}, f32[24,512]{1,0:T(8,128)}, bf16[4,4,224,128]{3,2,1,0:T(8,128)(2,1)S(1)}, bf16[4,4,224,128]{3,2,1,0:T(8,128)(2,1)S(1)}) custom-call(s32[2]{0:T(128)S(1)} %pad_add_fusion.refs_0_, bf16[1792,512]{1,0:T(8,128)(2,1)S(1)} %copy-done.9, bf16[1792,512]{1,0:T(8,128)(2,1)S(1)} %copy-done.11, ...), custom_call_target="tpu_custom_call" | custom-call | flops 32999999488 | bytes 30000000 | tf_op jit(solution)/shard_map/attn_bwd/pallas_call | solution.py:667
  141.4 2.1 %collective-permute-start.30 = (bf16[576,128]{1,0:T(8,128)(2,1)S(1)}, bf16[576,128]{1,0:T(8,128)(2,1)S(1)}, u32[]{:S(2)}, u32[]{:S(2)}) collective-permute-start(bf16[576,128]{1,0:T(8,128)(2,1)S(1)} %get-tuple-element.110), channel_id=1, source_target_pairs={{0,24},{8,16},{16,8},{24,0},{1,25},{9,17},{17,9},{25,1},{2,26},{10... | collective-permute-start | bytes 442376 | tf_op jit(solution)/shard_map/ppermute | solution.py:803
  143.5 3.8 %collective-permute-start.29 = (bf16[576,128]{1,0:T(8,128)(2,1)S(1)}, bf16[576,128]{1,0:T(8,128)(2,1)S(1)}, u32[]{:S(2)}, u32[]{:S(2)}) collective-permute-start(bf16[576,128]{1,0:T(8,128)(2,1)S(1)} %get-tuple-element.111), channel_id=1, source_target_pairs={{0,16},{8,24},{16,0},{24,8},{1,17},{9,25},{17,1},{25,9},{2,18},{10... | collective-permute-start | bytes 442376 | tf_op jit(solution)/shard_map/ppermute | solution.py:803
  151.1 7.5 %input_bwd.1 = bf16[16,100,512]{2,1,0:T(8,128)(2,1)S(1)} custom-call(s32[2]{0:T(128)S(1)} %pad_add_fusion.refs_0_, bf16[16,100,512]{2,1,0:T(8,128)(2,1)S(1)} %copy.21.refs_1_.refs_2_, bf16[1792,1536]{1,0:T(8,128)(2,1)S(1)} %get-tuple-element.76.refs_2_, f32[1792,512]{1,0:T(8,128)S(1)} %copy-done.2, f32[8,512]{1,0:T(8,128)S(1)} %get-tuple-element.58.refs_13_.refs_7_.refs_4_, ...), custom_call_target="tpu_custom_call" | custom-call | flops 11000000512 | bytes 10000000 | tf_op jit(solution)/shard_map/input_bwd/pallas_call | solution.py:720
  159.2 1.6 collective-permute-done.26
  161.1 2.2 %collective-permute-start.33 = (bf16[352,128]{1,0:T(8,128)(2,1)S(1)}, bf16[352,128]{1,0:T(8,128)(2,1)S(1)}, u32[]{:S(2)}, u32[]{:S(2)}) collective-permute-start(bf16[352,128]{1,0:T(8,128)(2,1)S(1)} %get-tuple-element.116), channel_id=1, source_target_pairs={{0,24},{8,16},{16,8},{24,0},{1,25},{9,17},{17,9},{25,1},{2,26},{10... | collective-permute-start | bytes 270344 | tf_op jit(solution)/shard_map/ppermute | solution.py:803
  163.4 2.2 %collective-permute-start.31 = (bf16[352,128]{1,0:T(8,128)(2,1)S(1)}, bf16[352,128]{1,0:T(8,128)(2,1)S(1)}, u32[]{:S(2)}, u32[]{:S(2)}) collective-permute-start(bf16[352,128]{1,0:T(8,128)(2,1)S(1)} %get-tuple-element.118), channel_id=1, source_target_pairs={{0,8},{8,0},{16,24},{24,16},{1,9},{9,1},{17,25},{25,17},{2,10},{10... | collective-permute-start | bytes 270344 | tf_op jit(solution)/shard_map/ppermute | solution.py:803
  165.5 1.7 copy.24
  167.2 1.7 copy.25
  169.0 2.7 %collective-permute-done.32.refs_7_ = bf16[352,128]{1,0:T(8,128)(2,1)S(1)} collective-permute-done((bf16[352,128]{1,0:T(8,128)(2,1)S(1)}, bf16[352,128]{1,0:T(8,128)(2,1)S(1)}, u32[]{:S(2)}, u32[]{:S(2)}) %collective-permute-start.32) | collective-permute-done | bytes 90144 | tf_op jit(solution)/shard_map/ppermute | solution.py:803
  172.9 2.3 %finish.1 = (f32[64,384]{1,0:T(8,128)}, f32[64,128]{1,0:T(8,128)}, f32[64,512]{1,0:T(8,128)}, f32[256,128]{1,0:T(8,128)}, f32[8,16]{1,0:T(8,128)}, /*index=5*/f32[1,64]{1,0:T(1,128)}, f32[361,16]{1,0:T(8,128)}) custom-call(s32[2]{0:T(128)} %copy-done.1, bf16[4,224,128]{2,1,0:T(8,128)(2,1)} %copy-done.18, bf16[4,576,128]{2,1,0:T(8,128)(2,1)} %copy-done.16, ...), custom_call_target="tpu_custom_call" | custom-call | flops 3300000000 | bytes 3000000 | tf_op jit(solution)/shard_map/finish/pallas_call | solution.py:782
  175.2 1.6 copy.26
  (125 shorter events, 33.1 us)
Async XLA Ops:
  2.2 7.8 %collective-permute-start.2 = (bf16[224,128]{1,0:T(8,128)(2,1)}, bf16[224,128]{1,0:T(8,128)(2,1)S(1)}, u32[]{:S(2)}, u32[]{:S(2)}) collective-permute-start(bf16[224,128]{1,0:T(8,128)(2,1)} %pack.2), channel_id=1, source_target_pairs={{0,24},{8,16},{16,8},{24,0},{1,25},{9,17},{17,9},{25,1},{2,26},{10... | collective-permute-start | bytes 172040 | tf_op jit(solution)/shard_map/ppermute | solution.py:803
  7.3 5.3 %collective-permute-start.1 = (bf16[224,128]{1,0:T(8,128)(2,1)}, bf16[224,128]{1,0:T(8,128)(2,1)S(1)}, u32[]{:S(2)}, u32[]{:S(2)}) collective-permute-start(bf16[224,128]{1,0:T(8,128)(2,1)} %pack.2), channel_id=1, source_target_pairs={{0,16},{8,24},{16,0},{24,8},{1,17},{9,25},{17,1},{25,9},{2,18},{10... | collective-permute-start | bytes 172040 | tf_op jit(solution)/shard_map/ppermute | solution.py:803
  12.6 8.9 %collective-permute-start.12 = (bf16[576,128]{1,0:T(8,128)(2,1)}, bf16[576,128]{1,0:T(8,128)(2,1)S(1)}, u32[]{:S(2)}, u32[]{:S(2)}) collective-permute-start(bf16[576,128]{1,0:T(8,128)(2,1)} %pack.3), channel_id=1, source_target_pairs={{0,24},{8,16},{16,8},{24,0},{1,25},{9,17},{17,9},{25,1},{2,26},{10... | collective-permute-start | bytes 442376 | tf_op jit(solution)/shard_map/ppermute | solution.py:803
  15.3 12.2 %collective-permute-start.11 = (bf16[576,128]{1,0:T(8,128)(2,1)}, bf16[576,128]{1,0:T(8,128)(2,1)S(1)}, u32[]{:S(2)}, u32[]{:S(2)}) collective-permute-start(bf16[576,128]{1,0:T(8,128)(2,1)} %pack.3), channel_id=1, source_target_pairs={{0,16},{8,24},{16,0},{24,8},{1,17},{9,25},{17,1},{25,9},{2,18},{10... | collective-permute-start | bytes 442376 | tf_op jit(solution)/shard_map/ppermute | solution.py:803
  15.4 14.0 %collective-permute-start.10 = (bf16[576,128]{1,0:T(8,128)(2,1)}, bf16[576,128]{1,0:T(8,128)(2,1)S(1)}, u32[]{:S(2)}, u32[]{:S(2)}) collective-permute-start(bf16[576,128]{1,0:T(8,128)(2,1)} %pack.3), channel_id=1, source_target_pairs={{0,8},{8,0},{16,24},{24,16},{1,9},{9,1},{17,25},{25,17},{2,10},{10... | collective-permute-start | bytes 442376 | tf_op jit(solution)/shard_map/ppermute | solution.py:803
  17.1 10.5 %collective-permute-start.8 = (bf16[4,224,128]{2,1,0:T(8,128)(2,1)S(1)}, bf16[4,224,128]{2,1,0:T(8,128)(2,1)S(1)}, u32[]{:S(2)}, u32[]{:S(2)}) collective-permute-start(bf16[4,224,128]{2,1,0:T(8,128)(2,1)S(1)} %pad_maximum_fusion.1.refs_3_.refs_11_.refs_5_), channel_id=1, source_target_pairs={{0,6},{1,7},{2,4},{3,5},{4,2},{5,3},{6,0},{7,1},{8,14},{9,15},{10,... | collective-permute-start | bytes 688136 | tf_op jit(solution)/shard_map/ppermute | solution.py:803
  19.6 9.1 %collective-permute-start.6 = (bf16[4,224,128]{2,1,0:T(8,128)(2,1)S(1)}, bf16[4,224,128]{2,1,0:T(8,128)(2,1)S(1)}, u32[]{:S(2)}, u32[]{:S(2)}) collective-permute-start(bf16[4,224,128]{2,1,0:T(8,128)(2,1)S(1)} %pad_maximum_fusion.1.refs_3_.refs_11_.refs_5_), channel_id=1, source_target_pairs={{0,4},{1,5},{2,6},{3,7},{4,0},{5,1},{6,2},{7,3},{8,12},{9,13},{10,... | collective-permute-start | bytes 688136 | tf_op jit(solution)/shard_map/ppermute | solution.py:803
  21.5 7.4 %collective-permute-start.4 = (bf16[4,224,128]{2,1,0:T(8,128)(2,1)S(1)}, bf16[4,224,128]{2,1,0:T(8,128)(2,1)S(1)}, u32[]{:S(2)}, u32[]{:S(2)}) collective-permute-start(bf16[4,224,128]{2,1,0:T(8,128)(2,1)S(1)} %pad_maximum_fusion.1.refs_3_.refs_11_.refs_5_), channel_id=1, source_target_pairs={{0,2},{1,3},{2,0},{3,1},{4,6},{5,7},{6,4},{7,5},{8,10},{9,11},{10,... | collective-permute-start | bytes 688136 | tf_op jit(solution)/shard_map/ppermute | solution.py:803
  30.6 28.8 %collective-permute-start.15 = (bf16[4,576,128]{2,1,0:T(8,128)(2,1)S(1)}, bf16[4,576,128]{2,1,0:T(8,128)(2,1)S(1)}, u32[]{:S(2)}, u32[]{:S(2)}) collective-permute-start(bf16[4,576,128]{2,1,0:T(8,128)(2,1)S(1)} %pad_maximum_fusion.refs_5_), channel_id=1, source_target_pairs={{0,6},{1,7},{2,4},{3,5},{4,2},{5,3},{6,0},{7,1},{8,14},{9,15},{10,... | collective-permute-start | bytes 1769480 | tf_op jit(solution)/shard_map/ppermute | solution.py:803
  32.5 27.0 %collective-permute-start.14 = (bf16[4,576,128]{2,1,0:T(8,128)(2,1)S(1)}, bf16[4,576,128]{2,1,0:T(8,128)(2,1)S(1)}, u32[]{:S(2)}, u32[]{:S(2)}) collective-permute-start(bf16[4,576,128]{2,1,0:T(8,128)(2,1)S(1)} %pad_maximum_fusion.refs_5_), channel_id=1, source_target_pairs={{0,4},{1,5},{2,6},{3,7},{4,0},{5,1},{6,2},{7,3},{8,12},{9,13},{10,... | collective-permute-start | bytes 1769480 | tf_op jit(solution)/shard_map/ppermute | solution.py:803
  33.6 26.1 %collective-permute-start.13 = (bf16[4,576,128]{2,1,0:T(8,128)(2,1)S(1)}, bf16[4,576,128]{2,1,0:T(8,128)(2,1)S(1)}, u32[]{:S(2)}, u32[]{:S(2)}) collective-permute-start(bf16[4,576,128]{2,1,0:T(8,128)(2,1)S(1)} %pad_maximum_fusion.refs_5_), channel_id=1, source_target_pairs={{0,2},{1,3},{2,0},{3,1},{4,6},{5,7},{6,4},{7,5},{8,10},{9,11},{10,... | collective-permute-start | bytes 1769480 | tf_op jit(solution)/shard_map/ppermute | solution.py:803
  111.7 29.2 %collective-permute-start.23 = (bf16[4,576,128]{2,1,0:T(8,128)(2,1)S(1)}, bf16[4,576,128]{2,1,0:T(8,128)(2,1)S(1)}, u32[]{:S(2)}, u32[]{:S(2)}) collective-permute-start(bf16[4,576,128]{2,1,0:T(8,128)(2,1)S(1)} %get-tuple-element.102), channel_id=1, source_target_pairs={{0,6},{1,7},{2,4},{3,5},{4,2},{5,3},{6,0},{7,1},{8,14},{9,15},{10,... | collective-permute-start | bytes 1769480 | tf_op jit(solution)/shard_map/ppermute | solution.py:803
  113.4 27.5 %collective-permute-start.22 = (bf16[4,576,128]{2,1,0:T(8,128)(2,1)S(1)}, bf16[4,576,128]{2,1,0:T(8,128)(2,1)S(1)}, u32[]{:S(2)}, u32[]{:S(2)}) collective-permute-start(bf16[4,576,128]{2,1,0:T(8,128)(2,1)S(1)} %get-tuple-element.103), channel_id=1, source_target_pairs={{0,4},{1,5},{2,6},{3,7},{4,0},{5,1},{6,2},{7,3},{8,12},{9,13},{10,... | collective-permute-start | bytes 1769480 | tf_op jit(solution)/shard_map/ppermute | solution.py:803
  114.6 26.4 %collective-permute-start.21 = (bf16[4,576,128]{2,1,0:T(8,128)(2,1)S(1)}, bf16[4,576,128]{2,1,0:T(8,128)(2,1)S(1)}, u32[]{:S(2)}, u32[]{:S(2)}) collective-permute-start(bf16[4,576,128]{2,1,0:T(8,128)(2,1)S(1)} %get-tuple-element.104), channel_id=1, source_target_pairs={{0,2},{1,3},{2,0},{3,1},{4,6},{5,7},{6,4},{7,5},{8,10},{9,11},{10,... | collective-permute-start | bytes 1769480 | tf_op jit(solution)/shard_map/ppermute | solution.py:803
  140.9 6.4 %collective-permute-start.24 = (bf16[4,4,224,128]{3,2,1,0:T(8,128)(2,1)S(1)}, bf16[4,4,224,128]{3,2,1,0:T(8,128)(2,1)S(1)}, u32[]{:S(2)}, u32[]{:S(2)}) collective-permute-start(bf16[4,4,224,128]{3,2,1,0:T(8,128)(2,1)S(1)} %get-tuple-element.75), channel_id=1, source_target_pairs={{0,1},{1,0},{2,3},{3,2},{4,5},{5,4},{6,7},{7,6},{8,9},{9,8},{10,11... | collective-permute-start | bytes 2752520 | tf_op jit(solution)/shard_map/ppermute | solution.py:803
  141.4 22.0 %collective-permute-start.30 = (bf16[576,128]{1,0:T(8,128)(2,1)S(1)}, bf16[576,128]{1,0:T(8,128)(2,1)S(1)}, u32[]{:S(2)}, u32[]{:S(2)}) collective-permute-start(bf16[576,128]{1,0:T(8,128)(2,1)S(1)} %get-tuple-element.110), channel_id=1, source_target_pairs={{0,24},{8,16},{16,8},{24,0},{1,25},{9,17},{17,9},{25,1},{2,26},{10... | collective-permute-start | bytes 442376 | tf_op jit(solution)/shard_map/ppermute | solution.py:803
  143.5 25.4 %collective-permute-start.29 = (bf16[576,128]{1,0:T(8,128)(2,1)S(1)}, bf16[576,128]{1,0:T(8,128)(2,1)S(1)}, u32[]{:S(2)}, u32[]{:S(2)}) collective-permute-start(bf16[576,128]{1,0:T(8,128)(2,1)S(1)} %get-tuple-element.111), channel_id=1, source_target_pairs={{0,16},{8,24},{16,0},{24,8},{1,17},{9,25},{17,1},{25,9},{2,18},{10... | collective-permute-start | bytes 442376 | tf_op jit(solution)/shard_map/ppermute | solution.py:803
  147.5 11.1 %collective-permute-start.27 = (bf16[4,224,128]{2,1,0:T(8,128)(2,1)S(1)}, bf16[4,224,128]{2,1,0:T(8,128)(2,1)S(1)}, u32[]{:S(2)}, u32[]{:S(2)}) collective-permute-start(bf16[4,224,128]{2,1,0:T(8,128)(2,1)S(1)} %get-tuple-element.106), channel_id=1, source_target_pairs={{0,6},{1,7},{2,4},{3,5},{4,2},{5,3},{6,0},{7,1},{8,14},{9,15},{10,... | collective-permute-start | bytes 688136 | tf_op jit(solution)/shard_map/ppermute | solution.py:803
  149.0 11.9 %collective-permute-start.26 = (bf16[4,224,128]{2,1,0:T(8,128)(2,1)S(1)}, bf16[4,224,128]{2,1,0:T(8,128)(2,1)S(1)}, u32[]{:S(2)}, u32[]{:S(2)}) collective-permute-start(bf16[4,224,128]{2,1,0:T(8,128)(2,1)S(1)} %get-tuple-element.107), channel_id=1, source_target_pairs={{0,4},{1,5},{2,6},{3,7},{4,0},{5,1},{6,2},{7,3},{8,12},{9,13},{10,... | collective-permute-start | bytes 688136 | tf_op jit(solution)/shard_map/ppermute | solution.py:803
  149.6 11.3 %collective-permute-start.25 = (bf16[4,224,128]{2,1,0:T(8,128)(2,1)S(1)}, bf16[4,224,128]{2,1,0:T(8,128)(2,1)S(1)}, u32[]{:S(2)}, u32[]{:S(2)}) collective-permute-start(bf16[4,224,128]{2,1,0:T(8,128)(2,1)S(1)} %get-tuple-element.108), channel_id=1, source_target_pairs={{0,2},{1,3},{2,0},{3,1},{4,6},{5,7},{6,4},{7,5},{8,10},{9,11},{10,... | collective-permute-start | bytes 688136 | tf_op jit(solution)/shard_map/ppermute | solution.py:803
  158.6 10.3 %collective-permute-start.28 = (bf16[576,128]{1,0:T(8,128)(2,1)S(1)}, bf16[576,128]{1,0:T(8,128)(2,1)S(1)}, u32[]{:S(2)}, u32[]{:S(2)}) collective-permute-start(bf16[576,128]{1,0:T(8,128)(2,1)S(1)} %get-tuple-element.112), channel_id=1, source_target_pairs={{0,8},{8,0},{16,24},{24,16},{1,9},{9,1},{17,25},{25,17},{2,10},{10... | collective-permute-start | bytes 442376 | tf_op jit(solution)/shard_map/ppermute | solution.py:803
  161.1 7.9 %collective-permute-start.33 = (bf16[352,128]{1,0:T(8,128)(2,1)S(1)}, bf16[352,128]{1,0:T(8,128)(2,1)S(1)}, u32[]{:S(2)}, u32[]{:S(2)}) collective-permute-start(bf16[352,128]{1,0:T(8,128)(2,1)S(1)} %get-tuple-element.116), channel_id=1, source_target_pairs={{0,24},{8,16},{16,8},{24,0},{1,25},{9,17},{17,9},{25,1},{2,26},{10... | collective-permute-start | bytes 270344 | tf_op jit(solution)/shard_map/ppermute | solution.py:803
  163.2 8.4 %collective-permute-start.32 = (bf16[352,128]{1,0:T(8,128)(2,1)S(1)}, bf16[352,128]{1,0:T(8,128)(2,1)S(1)}, u32[]{:S(2)}, u32[]{:S(2)}) collective-permute-start(bf16[352,128]{1,0:T(8,128)(2,1)S(1)} %get-tuple-element.117), channel_id=1, source_target_pairs={{0,16},{8,24},{16,0},{24,8},{1,17},{9,25},{17,1},{25,9},{2,18},{10... | collective-permute-start | bytes 270344 | tf_op jit(solution)/shard_map/ppermute | solution.py:803
  163.4 8.3 %collective-permute-start.31 = (bf16[352,128]{1,0:T(8,128)(2,1)S(1)}, bf16[352,128]{1,0:T(8,128)(2,1)S(1)}, u32[]{:S(2)}, u32[]{:S(2)}) collective-permute-start(bf16[352,128]{1,0:T(8,128)(2,1)S(1)} %get-tuple-element.118), channel_id=1, source_target_pairs={{0,8},{8,0},{16,24},{24,16},{1,9},{9,1},{17,25},{25,17},{2,10},{10... | collective-permute-start | bytes 270344 | tf_op jit(solution)/shard_map/ppermute | solution.py:803
  (38 other events, 358.4 us)

commit v4 on v3

--- a/solution.py
+++ b/solution.py
@@ -78,7 +78,8 @@
         self.cq, self.cp, self.c1 = 3 * D // nz // TL, D // nz // TL, FF // nz // TL
         self.r2 = FF // nw
         self.rows_a = self.cq * self.r
-        self.rows_b = self.cp * self.r + self.c1 * self.r + self.cp * self.r2
+        self.blocks = self.c1 + 5 * self.cp
+        self.cores = 2 if nw > 1 else 1
 
 
 def slabs(x):
@@ -88,41 +89,44 @@
 def pack_body(count, *refs):
     srcs, out = refs[:count], refs[count]
     rest = refs[count + 1 :]
-    stage, flat, sem = rest[: len(srcs)], rest[-2], rest[-1]
+    stage, flat, sem = rest[:count], rest[-2], rest[-1]
     moves = [pltpu.make_async_copy(x, y, sem.at[i]) for i, (x, y) in enumerate(zip(srcs, stage))]
     for m in moves:
         m.start()
+    parts = []
+    r = flat.shape[-2]
     at = 0
     for m, w in zip(moves, stage):
         m.wait()
         if w.dtype == f32:
             part = [p.astype(f32) for p in three(w[...])]
-            part = [jnp.concatenate([p, jnp.zeros((p.shape[0], TL - p.shape[1]), f32)], 1) for p in part]
-            part = jnp.concatenate(part, 0)
-            if part.shape[0] == 24:
-                kept = part
-                continue
-            part = jnp.concatenate([kept, part, jnp.zeros((EXTRA - 27, TL), f32)], 0)
-            flat[at : at + EXTRA, :] = part.astype(bf16)
-            at += EXTRA
+            parts += [jnp.concatenate([p, jnp.zeros((p.shape[0], TL - p.shape[1]), f32)], 1) for p in part]
             continue
         for i in range(0, w.shape[1], TL):
-            flat[at : at + w.shape[0], :] = w[:, i : i + TL]
-            at += w.shape[0]
+            if len(flat.shape) == 2:
+                flat[at : at + w.shape[0], :] = w[:, i : i + TL]
+                at += w.shape[0]
+                continue
+            for k in range(0, w.shape[0], r):
+                flat[at] = w[k : k + r, i : i + TL]
+                at += 1
+    if parts:
+        used = sum(p.shape[0] for p in parts)
+        flat[at : at + EXTRA, :] = jnp.concatenate(parts + [jnp.zeros((EXTRA - used, TL), f32)], 0).astype(bf16)
     last = pltpu.make_async_copy(flat, out, sem.at[count])
     last.start()
     last.wait()
 
 
-def pack(rows, *arrays):
+def pack(shape, *arrays):
     V = pltpu.VMEM
     return pl.pallas_call(
         functools.partial(pack_body, len(arrays)),
         in_specs=[anyspace()] * len(arrays),
         out_specs=anyspace(),
-        out_shape=jax.ShapeDtypeStruct((rows, TL), bf16),
+        out_shape=jax.ShapeDtypeStruct(shape, bf16),
         scratch_shapes=[V(x.shape, x.dtype) for x in arrays]
-        + [V((rows, TL), bf16), pltpu.SemaphoreType.DMA((len(arrays) + 1,))],
+        + [V(shape, bf16), pltpu.SemaphoreType.DMA((len(arrays) + 1,))],
         compiler_params=pltpu.CompilerParams(vmem_limit_bytes=60 * 2**20),
         cost_estimate=cost(2),
         name="pack",
@@ -149,19 +153,16 @@
 def copies_b(geo, bufs, me, wp, w1, w2, sem):
     out = []
     for d in range(geo.nw):
-        row = pl.multiple_of((me[0] ^ d) * geo.r, geo.r)
-        row2 = pl.multiple_of((me[0] ^ d) * geo.r2, geo.r2)
+        w = me[0] ^ d
+        row = pl.multiple_of(w * geo.r, geo.r)
         for e in range(geo.nz):
             z = me[1] ^ e
-            at = 0
-            for w, n, r, to in ((wp, geo.cp, geo.r, row), (w1, geo.c1, geo.r, row), (w2, geo.cp, geo.r2, row2)):
-                for i in range(n):
-                    out.append(
-                        pltpu.make_async_copy(
-                            bufs[d].at[e, pl.ds(at, r), :], w.at[z * n + i, pl.ds(to, r), :], sem
-                        )
-                    )
-                    at += r
+            for ref, at, n in ((wp, 0, geo.cp), (w1, geo.cp, geo.c1)):
+                src = bufs[d].at[e, pl.ds(at, n)]
+                out.append(pltpu.make_async_copy(src, ref.at[pl.ds(z * n, n), pl.ds(row, geo.r), :], sem))
+            for i in range(geo.cp):
+                src = bufs[d].at[e, pl.ds(geo.cp + geo.c1 + 4 * i, 4)]
+                out.append(pltpu.make_async_copy(src, w2.at[z * geo.cp + i, pl.ds(w * 4, 4)], sem))
     return out
 
 
@@ -214,12 +215,9 @@
             base = (j * GH + h) * 16
             for half in range(2):
                 rs[half, base : base + WS, :] = total[:, half * TL : (half + 1) * TL]
-    out = jnp.zeros((HEADS, TT), f32)
-    for cj in range(WS):
-        parts = jnp.concatenate([p for p in three(strided(rs, cj, HEADS, 16))], 0)
-        z = dot(parts, place[cj], NT)
-        out = out + (z[:HEADS] + z[HEADS : 2 * HEADS] + z[2 * HEADS :])
-    return out
+    columns = jnp.concatenate([strided(rs, cj, HEADS, 16) for cj in range(WS)], 1)
+    z = dot(jnp.concatenate(three(columns), 0), jnp.concatenate([place[cj] for cj in range(WS)], 1), NT)
+    return z[:HEADS] + z[HEADS : 2 * HEADS] + z[2 * HEADS :]
 
 
 def norm(x):
@@ -382,7 +380,7 @@
 
 
 def scatter_out(geo, me, blocks, outs):
-    cores = len(outs)
+    cores = geo.cores
     for c in range(cores):
         for xy in range(geo.nw // cores):
             w = me[0] ^ (xy * cores + c)
@@ -391,7 +389,7 @@
                 at = 0
                 for ref, pick in blocks:
                     for part in pick(ref, w, z):
-                        outs[c][xy, e, at : at + part.shape[0], :] = part.astype(bf16)
+                        outs[c * (geo.nw // cores) + xy][e, at : at + part.shape[0], :] = part.astype(bf16)
                         at += part.shape[0]
 
 
@@ -402,9 +400,8 @@
     vec, b1 = refs[5 + nb : 7 + nb]
     refs = refs[7 + nb :]
     out_o, dx1_o, da_o, gv_o, gb1_o = refs[:5]
-    cores = 2 if nb > 1 else 1
-    outs = refs[5 : 5 + cores]
-    xs, dys, gp, g1, g2, gv, gb1, acc, dn2, wp, w1, w2, sem = refs[5 + cores :]
+    outs = refs[5 : 5 + geo.nw]
+    xs, dys, gp, g1, g2, gv, gb1, acc, dn2, wp, w1, w2, sem = refs[5 + geo.nw :]
     i = pl.program_id(0)
     n = pl.num_programs(0)
 
@@ -438,7 +435,7 @@
     def first(c):
         cols = slice(c * FC, (c + 1) * FC)
         w1c = wide(w1, c * ns, ns)
-        w2c = jnp.concatenate([w2[z, cols, :] for z in range(NG)], 1)
+        w2c = jnp.concatenate([w2[z, cols.start // geo.r : cols.stop // geo.r].reshape(FC, TL) for z in range(NG)], 1)
         return w1c, w2c, dot(n2, w1c), dot(dy, w2c, NT)
 
     def last(c):
@@ -512,16 +509,15 @@
     blk = pl.BlockSpec((M, D), lambda i: (i, 0))
     win = pl.BlockSpec((G, WT, D), lambda i: (i, 0, 0))
     S = jax.ShapeDtypeStruct
-    cores = 2 if geo.nw > 1 else 1
-    gshape = (geo.nw // cores, geo.nz, geo.rows_b, TL)
+    gshape = (geo.nz, geo.blocks * geo.r, TL)
     V = pltpu.VMEM
     return pl.pallas_call(
         functools.partial(mlp_body, geo, G, FC),
         grid=(B // G,),
         in_specs=[smem(), smem(), win, win, blk] + [anyspace()] * len(bufs) + [whole(vec.shape), whole(b1.shape)],
-        out_specs=[win, blk, blk, whole((8, D)), whole((1, FF))] + [whole(gshape)] * cores,
+        out_specs=[win, blk, blk, whole((8, D)), whole((1, FF))] + [whole(gshape)] * geo.nw,
         out_shape=[S(tok.shape, bf16), S((R, D), f32), S((R, D), bf16), S((8, D), f32), S((1, FF), f32)]
-        + [S(gshape, bf16)] * cores,
+        + [S(gshape, bf16)] * geo.nw,
         scratch_shapes=[
             V((M, D), f32),
             V((M, D), f32),
@@ -534,7 +530,7 @@
             V((M, D), f32),
             V((NG, D, TL), bf16),
             V((FF // TL, D, TL), bf16),
-            V((NG, FF, TL), bf16),
+            V((NG, FF // geo.r, geo.r, TL), bf16),
             pltpu.SemaphoreType.DMA,
         ],
         compiler_params=params(36),
@@ -548,10 +544,9 @@
     me, q, k, v, p, da, xh, vec, gv2, gb1, place = refs[:11]
     bufs = refs[11 : 11 + nb]
     refs = refs[11 + nb :]
-    cores = 2 if nb > 1 else 1
     dc_o, small_o = refs[:2]
-    outs = refs[2 : 2 + cores]
-    gq, gb, gt, wq, rs, ex, sem = refs[2 + cores :]
+    outs = refs[2 : 2 + geo.nw]
+    gq, gb, gt, wq, rs, ex, sem = refs[2 + geo.nw :]
     i = pl.program_id(0)
     n = pl.num_programs(0)
 
@@ -609,23 +604,21 @@
     @pl.when(i == n - 1)
     def _():
         sums = gb[...]
-        ones = jnp.ones((8, D), bf16)
-        gain = jnp.zeros((8, D), f32)
-        shift = jnp.zeros((8, D), f32)
-        for c in range(3):
-            w = wide(wq, c * NG, NG)
-            prod = wide(gq, c * NG, NG) * w.astype(f32)
-            for part in three(prod)[:2]:
-                gain = gain + dot(ones, part, NT)
-            part = [x.astype(f32) for x in three(sums[:, c * D : (c + 1) * D])]
-            part = jnp.concatenate(part + [jnp.zeros((5, D), f32)], 0).astype(bf16)
-            shift = shift + dot(part, w, NT)
         g_col = jnp.broadcast_to(vec[0:1, :], (TL, D)).T
         s_col = jnp.broadcast_to(vec[1:2, :], (TL, D)).T
+        gain = jnp.zeros((D, TL), f32)
+        shift = jnp.zeros((D, TL), f32)
         for s in range(3 * NG):
-            gq[s] = gq[s] * g_col + s_col * sums[:, s * TL : (s + 1) * TL]
-        small_o[0:1, :] = gain[0:1]
-        small_o[1:2, :] = shift[0:1] + shift[1:2] + shift[2:3]
+            part = gq[s]
+            w = wq[s].astype(f32)
+            total = sums[:, s * TL : (s + 1) * TL]
+            gain = gain + part * w
+            shift = shift + w * total
+            gq[s] = part * g_col + s_col * total
+        gain = jnp.sum(gain.T, 0, keepdims=True)
+        shift = jnp.sum(shift.T, 0, keepdims=True)
+        small_o[0:1, :] = gain
+        small_o[1:2, :] = shift
         small_o[2:3, :] = sums[:, :D]
         small_o[3:4, :] = sums[:, 2 * D :]
         small_o[4:8, :] = gv2[4:8, :]
@@ -662,16 +655,15 @@
     blk = pl.BlockSpec((G * TP, D), lambda i: (i, 0))
     S = jax.ShapeDtypeStruct
     V = pltpu.VMEM
-    cores = 2 if geo.nw > 1 else 1
-    gshape = (geo.nw // cores, geo.nz, geo.rows_a + (EXTRA if cores == 2 else 0), TL)
+    gshape = (geo.nz, geo.rows_a + (EXTRA if geo.cores == 2 else 0), TL)
     return pl.pallas_call(
         functools.partial(attn_bwd_body, geo, G),
         grid=(B // G,),
         in_specs=[smem(), blk, blk, blk, pl.BlockSpec((G, NG, TP, GH * TL), lambda i: (i, 0, 0, 0)), blk, blk]
         + [whole(x.shape) for x in (vec, gv2, gb1, place)]
         + [anyspace()] * len(bufs),
-        out_specs=[pl.BlockSpec((G * TP, 3 * D), lambda i: (i, 0)), whole((24, D))] + [whole(gshape)] * cores,
-        out_shape=[S((R, 3 * D), bf16), S((24, D), f32)] + [S(gshape, bf16)] * cores,
+        out_specs=[pl.BlockSpec((G * TP, 3 * D), lambda i: (i, 0)), whole((24, D))] + [whole(gshape)] * geo.nw,
+        out_shape=[S((R, 3 * D), bf16), S((24, D), f32)] + [S(gshape, bf16)] * geo.nw,
         scratch_shapes=[
             V((3 * NG, D, TL), f32),
             V((1, 3 * D), f32),
@@ -773,7 +765,7 @@
         for k in range(TT // TL):
             tab[me[1] ^ e, :, k * TL : (k + 1) * TL] = t[lo + k * nh : lo + (k + 1) * nh]
     full = jnp.concatenate([tab[z] for z in range(nz)], 0)
-    tab_o[...] = full.T[:TABLE]
+    tab_o[...] = full[:, :TABLE]
 
 
 def finish(geo, nw, nz, me, low_a, low_b, got_b, got_a):
@@ -790,10 +782,10 @@
             S((geo.r2, geo.cp * TL), f32),
             S((8, D // (nw * nz)), f32),
             S((1, FF // (nw * nz)), f32),
-            S((TABLE, HEADS), f32),
+            S((HEADS, TABLE), f32),
         ],
         scratch_shapes=[pltpu.VMEM((nz, HEADS // nz, TT), f32)],
-        compiler_params=pltpu.CompilerParams(vmem_limit_bytes=60 * 2**20),
+        compiler_params=pltpu.CompilerParams(vmem_limit_bytes=12 * 2**20),
         cost_estimate=cost(3),
         name="finish",
     )(me, low_a, low_b, *got_b, *got_a)
@@ -819,8 +811,12 @@
     return [y for x in planes for y in (x, swap(x, "win", nw, 1))]
 
 
-def sum_core(keep, got, nw):
-    return [(keep[d].astype(f32) + got[d].astype(f32)).astype(bf16) for d in range(nw // 2)]
+def sum_core(parts, nw):
+    n = nw // 2
+    out = [None] * n
+    for d in reversed(range(n)):
+        out[d] = (parts[d].astype(f32) + swap(parts[n + d], "win", nw, 1).astype(f32)).astype(bf16)
+    return out
 
 
 def swap_xy(sums, nw):
@@ -857,29 +853,30 @@
     if fast:
         geo = Geometry(nw, nz)
         me = jnp.stack([lax.axis_index("win"), lax.axis_index("fsdp")]).astype(jnp.int32)
-        buf_a = pack(geo.rows_a + EXTRA, w_qkv, vectors, fc1_bias.reshape(1, -1))
-        buf_b = pack(geo.rows_b, w_proj, w_fc1, w_fc2)
+        buf_a = pack((geo.rows_a + EXTRA, TL), w_qkv, vectors, fc1_bias.reshape(1, -1))
+        buf_b = pack((geo.blocks, geo.r, TL), w_proj, w_fc1, w_fc2)
         mine_a = gather_z(buf_a, nz)
         pb = bias(table, place)
         planes_a = gather_xy(mine_a, nw)
         mine_b = gather_z(after(buf_b, mine_a), nz)
         bufs_a = gather_core(planes_a, nw)
-        planes_b = gather_xy(after(mine_b, *bufs_a), nw)
+        planes_b = gather_xy(mine_b, nw)
+        own_core = swap(planes_b[0], "win", nw, 1)
         xh, q, k, v, p, att, vec, b1 = attn_fwd(geo, me, tokens, pb, bufs_a)
-        planes_b = lax.optimization_barrier((*planes_b, att))[:-1]
-        bufs_b = gather_core(planes_b, nw)
-        out, dx1, da, gv2, gb1, keep_b, send_b = mlp(geo, me, live, tokens, cotangent, att, bufs_b, vec, b1)
-        sums_b = sum_core(keep_b, swap(send_b, "win", nw, 1), nw)
+        rest = lax.optimization_barrier((*planes_b[1:], att))[:-1]
+        bufs_b = [planes_b[0], own_core] + gather_core(rest, nw)
+        out, dx1, da, gv2, gb1, *gw = mlp(geo, me, live, tokens, cotangent, att, bufs_b, vec, b1)
+        sums_b = sum_core(gw, nw)
         parts_b = swap_xy(sums_b, nw)
-        da = after(da, *sums_b)
-        dc, _, keep_a, send_a = attn_bwd(geo, me, q, k, v, p, da, xh, vec, gv2, gb1, place, bufs_a)
-        *parts_b, send_a = lax.optimization_barrier((*parts_b, send_a))
+        gv2 = after(gv2, *sums_b)
+        dc, _, *gq = attn_bwd(geo, me, q, k, v, p, da, xh, vec, gv2, gb1, place, bufs_a)
+        res = lax.optimization_barrier((*parts_b, *gq))
+        parts_b, gq = res[: len(parts_b)], res[len(parts_b) :]
         low_b = sum_xy(parts_b)
-        sums_a = sum_core(keep_a, swap(send_a, "win", nw, 1), nw)
+        sums_a = sum_core(gq, nw)
         parts_a = swap_xy(sums_a, nw)
         own_b = swap_z(low_b, nz)
-        dc = after(dc, *sums_a)
-        grad_tokens = input_bwd(geo, me, tokens, dc, dx1, vec, bufs_a)
+        grad_tokens = input_bwd(geo, me, tokens, dc, dx1, after(vec, *sums_a), bufs_a)
         parts_a = lax.optimization_barrier((*parts_a, grad_tokens))[:-1]
         low_a = sum_xy(parts_a)
         tail = low_a[:, geo.rows_a :].reshape(nz * EXTRA, TL)
@@ -888,6 +885,7 @@
             geo, nw, nz, me, low_a, low_b, own_b, own_a
         )
         grad_bias = grad_bias.reshape(-1)
+        grad_table = grad_table.T
     else:
         geo = Geometry(1, 1)
         me = jnp.zeros((2,), jnp.int32)
@@ -896,7 +894,7 @@
             return lax.all_gather(lax.all_gather(w, "fsdp", axis=1, tiled=True), "win", axis=0, tiled=True)
 
         bufs_a = [slabs(full(w_qkv))[None]]
-        bufs_b = [jnp.concatenate([slabs(full(w)) for w in (w_proj, w_fc1, w_fc2)], 0)[None]]
+        bufs_b = [jnp.concatenate([slabs(full(w)) for w in (w_proj, w_fc1, w_fc2)], 0).reshape(1, geo.blocks, D, TL)]
         vec = lax.all_gather(vectors, both, axis=1, tiled=True)
         b1 = lax.all_gather(fc1_bias, both, axis=0, tiled=True).reshape(1, -1)
         pb = bias(table, place)
@@ -909,8 +907,8 @@
             g = lax.psum_scatter(g.astype(bf16), "win", scatter_dimension=0, tiled=True)
             return lax.psum_scatter(g, "fsdp", scatter_dimension=1, tiled=True).astype(f32)
 
-        grad_qkv = down(unslab(gq[0, 0], geo.cq))
-        grad_proj, grad_one, grad_two = [down(g) for g in split_b(geo, gw[0, 0])]
+        grad_qkv = down(unslab(gq[0], geo.cq))
+        grad_proj, grad_one, grad_two = [down(g) for g in split_b(geo, gw[0])]
         small = lax.psum(small, both)
         grad_vectors = lax.dynamic_slice_in_dim(small[:8], dev * own, own, 1)
         grad_bias = lax.dynamic_slice_in_dim(small[8:, TT:].reshape(FF), dev * own1, own1, 0)

time: 177 us -> 167 us (0.944)
  waiting for transfers between devices: 17.4 us -> 11.4 us
  Pallas kernels: 98.6 us -> 95 us
    ppermute x34 -> x40, waiting for transfers between devices: 17.4 us -> 11.4 us  [swap(): return lax.ppermute(x, axis, [(i, i ^ d) for i in range(size)])]
    pallas_call x1, Pallas kernels: 42 us -> 39.6 us  [mlp(): pl.pallas_call(functools.partial(mlp_body, geo, G, FC), grid=(B // G,), i...]
    unnamed x61 -> x46, local copies, waits for them, and re-layouts: 18.8 us -> 17.2 us
    ppermute x34 -> x40, starting transfers between devices: 38.5 us -> 40 us  [swap(): return lax.ppermute(x, axis, [(i, i ^ d) for i in range(size)])]
  transfers between devices with their start and end apart: 34 -> 40, of which waited for: 15 -> 11; matrix products, arithmetic and copies ran while one was open for 4% -> 5% of each run, Pallas kernels for 30% -> 32%
where the time goes in v4:
time: 167 us
  Pallas kernels  95 us (57%)
  starting transfers between devices  40 us (24%)
  local copies, waits for them, and re-layouts  17.2 us (10%)
  waiting for transfers between devices  11.4 us (7%)
  between operations  1.74 us (1%)
    ppermute x40, starting transfers between devices, swap(): return lax.ppermute(x, axis, [(i, i ^ d) for i in range(size)])  40 us
    pallas_call x1, Pallas kernels, mlp(): pl.pallas_call(functools.partial(mlp_body, geo, G, FC), grid=(B // G,), i...  39.6 us
    pallas_call x1, Pallas kernels, attn_bwd(): pl.pallas_call(functools.partial(attn_bwd_body, geo, G), grid=(B // G,),...  23.8 us
    pallas_call x1, Pallas kernels, attn_fwd(): pl.pallas_call(functools.partial(attn_fwd_body, geo, G, vec is not None),...  18.6 us
    unnamed x46, local copies, waits for them, and re-layouts  17.2 us
    ppermute x40, waiting for transfers between devices, swap(): return lax.ppermute(x, axis, [(i, i ^ d) for i in range(size)])  11.4 us
    pallas_call x1, Pallas kernels, input_bwd(): pl.pallas_call(functools.partial(input_bwd_body, geo, G), grid=(B // G,),...  7.52 us
  transfers between devices with their start and end apart: 40, of which 11 were waited for; matrix products, arithmetic and copies ran while one was open for 5% of the time, Pallas kernels for 32%

profile of v4, /device:TPU:0, one launch (start us, length us, event | category | flops | bytes accessed | tf_op | source)
XLA Modules:
  0.0 166.9 jit_solution(1556319270904925223)
XLA Ops:
  0.6 1.5 pack.2
  2.2 5.1 %collective-permute-start.2 = (bf16[224,128]{1,0:T(8,128)(2,1)}, bf16[224,128]{1,0:T(8,128)(2,1)S(1)}, u32[]{:S(2)}, u32[]{:S(2)}) collective-permute-start(bf16[224,128]{1,0:T(8,128)(2,1)} %pack.2), channel_id=1, source_target_pairs={{0,24},{8,16},{16,8},{24,0},{1,25},{9,17},{17,9},{25,1},{2,26},{10... | collective-permute-start | bytes 172040 | tf_op jit(solution)/shard_map/ppermute | solution.py:795
  7.9 1.6 pack.3
  9.9 2.6 %collective-permute-done.1 = bf16[224,128]{1,0:T(8,128)(2,1)S(1)} collective-permute-done((bf16[224,128]{1,0:T(8,128)(2,1)}, bf16[224,128]{1,0:T(8,128)(2,1)S(1)}, u32[]{:S(2)}, u32[]{:S(2)}) %collective-permute-start.1) | collective-permute-done | bytes 57376 | tf_op jit(solution)/shard_map/ppermute | solution.py:795
  12.6 2.7 %collective-permute-start.12 = (bf16[9,64,128]{2,1,0:T(8,128)(2,1)}, bf16[9,64,128]{2,1,0:T(8,128)(2,1)S(1)}, u32[]{:S(2)}, u32[]{:S(2)}) collective-permute-start(bf16[9,64,128]{2,1,0:T(8,128)(2,1)} %pack.3), channel_id=1, source_target_pairs={{0,24},{8,16},{16,8},{24,0},{1,25},{9,17},{17,9},{25,1},{2,26},{10... | collective-permute-start | bytes 442376 | tf_op jit(solution)/shard_map/ppermute | solution.py:795
  15.4 1.7 %collective-permute-start.10 = (bf16[9,64,128]{2,1,0:T(8,128)(2,1)}, bf16[9,64,128]{2,1,0:T(8,128)(2,1)S(1)}, u32[]{:S(2)}, u32[]{:S(2)}) collective-permute-start(bf16[9,64,128]{2,1,0:T(8,128)(2,1)} %pack.3), channel_id=1, source_target_pairs={{0,8},{8,0},{16,24},{24,16},{1,9},{9,1},{17,25},{25,17},{2,10},{10... | collective-permute-start | bytes 442376 | tf_op jit(solution)/shard_map/ppermute | solution.py:795
  17.1 2.5 %collective-permute-start.8 = (bf16[4,224,128]{2,1,0:T(8,128)(2,1)S(1)}, bf16[4,224,128]{2,1,0:T(8,128)(2,1)S(1)}, u32[]{:S(2)}, u32[]{:S(2)}) collective-permute-start(bf16[4,224,128]{2,1,0:T(8,128)(2,1)S(1)} %pad_maximum_fusion.1.refs_3_.refs_11_.refs_5_), channel_id=1, source_target_pairs={{0,6},{1,7},{2,4},{3,5},{4,2},{5,3},{6,0},{7,1},{8,14},{9,15},{10,... | collective-permute-start | bytes 688136 | tf_op jit(solution)/shard_map/ppermute | solution.py:795
  21.5 1.5 collective-permute-start.4
  25.1 2.4 %copy.21.refs_1_.refs_2_ = bf16[16,100,512]{2,1,0:T(8,128)(2,1)S(1)} copy(bf16[16,100,512]{2,0,1:T(8,128)(2,1)} %param.11) | data formatting | bytes 3276800 | tf_op args[0]
  29.4 1.8 %collective-permute-start.16 = (bf16[4,9,64,128]{3,2,1,0:T(8,128)(2,1)S(1)}, bf16[4,9,64,128]{3,2,1,0:T(8,128)(2,1)S(1)}, u32[]{:S(2)}, u32[]{:S(2)}) collective-permute-start(bf16[4,9,64,128]{3,2,1,0:T(8,128)(2,1)S(1)} %pad_maximum_fusion.refs_5_), channel_id=1, source_target_pairs={{0,6},{1,7},{2,4},{3,5},{4,2},{5,3},{6,0},{7,1},{8,14},{9,15},{10,... | collective-permute-start | bytes 1769480 | tf_op jit(solution)/shard_map/ppermute | solution.py:795
  33.0 18.6 %attn_fwd.1 = (bf16[1792,512]{1,0:T(8,128)(2,1)S(1)}, bf16[1792,512]{1,0:T(8,128)(2,1)S(1)}, bf16[1792,512]{1,0:T(8,128)(2,1)S(1)}, bf16[1792,512]{1,0:T(8,128)(...) custom-call(s32[2]{0:T(128)S(1)} %pad_add_fusion.refs_0_, ...), custom_call_target="tpu_custom_call" | custom-call | flops 32999999488 | bytes 30000000 | tf_op jit(solution)/shard_map/attn_fwd/pallas_call | solution.py:348
  51.6 2.9 %copy-done.4 = bf16[16,4,112,512]{3,2,1,0:T(8,128)(2,1)} copy-done((bf16[16,4,112,512]{3,2,1,0:T(8,128)(2,1)}, bf16[16,4,112,512]{3,2,1,0:T(8,128)(2,1)S(1)}, u32[]{:S(2)}) %copy-start.4) | copy-done | bytes 7340056
  63.6 39.6 %mlp.1 = (bf16[16,100,512]{2,1,0:T(8,128)(2,1)S(1)}, f32[1792,512]{1,0:T(8,128)}, bf16[1792,512]{1,0:T(8,128)(2,1)S(1)}, f32[8,512]{1,0:T(8,128)S(1)}, f32[1,204...) custom-call(s32[2]{0:T(128)S(1)} %pad_add_fusion.refs_0_, ...), custom_call_target="tpu_custom_call" | custom-call | flops 48399998976 | bytes 44000000 | tf_op jit(solution)/shard_map/mlp/pallas_call | solution.py:514
  105.4 1.7 collective-permute-start.24
  109.8 1.5 copy-done.14
  111.3 23.8 %attn_bwd.1 = (bf16[1792,1536]{1,0:T(8,128)(2,1)S(1)}, f32[24,512]{1,0:T(8,128)}, bf16[4,224,128]{2,1,0:T(8,128)(2,1)S(1)}, bf16[4,224,128]{2,1,0:T(8,128)(2,1)S...) custom-call(s32[2]{0:T(128)S(1)} %pad_add_fusion.refs_0_, ...), custom_call_target="tpu_custom_call" | custom-call | flops 32999999488 | bytes 30000000 | tf_op jit(solution)/shard_map/attn_bwd/pallas_call | solution.py:659
  136.6 2.1 %collective-permute-start.36 = (bf16[576,128]{1,0:T(8,128)(2,1)S(1)}, bf16[576,128]{1,0:T(8,128)(2,1)S(1)}, u32[]{:S(2)}, u32[]{:S(2)}) collective-permute-start(bf16[576,128]{1,0:T(8,128)(2,1)S(1)} %get-tuple-element.136), channel_id=1, source_target_pairs={{0,24},{8,16},{16,8},{24,0},{1,25},{9,17},{17,9},{25,1},{2,26},{10... | collective-permute-start | bytes 442376 | tf_op jit(solution)/shard_map/ppermute | solution.py:795
  138.8 3.4 %collective-permute-start.35 = (bf16[576,128]{1,0:T(8,128)(2,1)S(1)}, bf16[576,128]{1,0:T(8,128)(2,1)S(1)}, u32[]{:S(2)}, u32[]{:S(2)}) collective-permute-start(bf16[576,128]{1,0:T(8,128)(2,1)S(1)} %get-tuple-element.137), channel_id=1, source_target_pairs={{0,16},{8,24},{16,0},{24,8},{1,17},{9,25},{17,1},{25,9},{2,18},{10... | collective-permute-start | bytes 442376 | tf_op jit(solution)/shard_map/ppermute | solution.py:795
  146.2 7.5 %input_bwd.1 = bf16[16,100,512]{2,1,0:T(8,128)(2,1)S(1)} custom-call(s32[2]{0:T(128)S(1)} %pad_add_fusion.refs_0_, bf16[16,100,512]{2,1,0:T(8,128)(2,1)S(1)} %copy.21.refs_1_.refs_2_, bf16[1792,1536]{1,0:T(8,128)(2,1)S(1)} %get-tuple-element.93.refs_2_, f32[1792,512]{1,0:T(8,128)S(1)} %copy-done.1, f32[8,512]{1,0:T(8,128)S(1)} %get-tuple-element.111.refs_13_.refs_7_.refs_4_, ...), custom_call_target="tpu_custom_call" | custom-call | flops 11000000512 | bytes 10000000 | tf_op jit(solution)/shard_map/input_bwd/pallas_call | solution.py:712
  155.5 2.2 %collective-permute-start.39 = (bf16[352,128]{1,0:T(8,128)(2,1)S(1)}, bf16[352,128]{1,0:T(8,128)(2,1)S(1)}, u32[]{:S(2)}, u32[]{:S(2)}) collective-permute-start(bf16[352,128]{1,0:T(8,128)(2,1)S(1)} %get-tuple-element.142), channel_id=1, source_target_pairs={{0,24},{8,16},{16,8},{24,0},{1,25},{9,17},{17,9},{25,1},{2,26},{10... | collective-permute-start | bytes 270344 | tf_op jit(solution)/shard_map/ppermute | solution.py:795
  157.7 2.3 %collective-permute-start.37 = (bf16[352,128]{1,0:T(8,128)(2,1)S(1)}, bf16[352,128]{1,0:T(8,128)(2,1)S(1)}, u32[]{:S(2)}, u32[]{:S(2)}) collective-permute-start(bf16[352,128]{1,0:T(8,128)(2,1)S(1)} %get-tuple-element.144), channel_id=1, source_target_pairs={{0,8},{8,0},{16,24},{24,16},{1,9},{9,1},{17,25},{25,17},{2,10},{10... | collective-permute-start | bytes 270344 | tf_op jit(solution)/shard_map/ppermute | solution.py:795
  159.9 1.7 %copy.24 = bf16[16,100,512]{2,0,1:T(8,128)(2,1)} copy(bf16[16,100,512]{2,1,0:T(8,128)(2,1)S(1)} %get-tuple-element.127) | data formatting | bytes 3276800
  161.6 1.7 %copy.25 = bf16[16,100,512]{2,0,1:T(8,128)(2,1)} copy(bf16[16,100,512]{2,1,0:T(8,128)(2,1)S(1)} %input_bwd.1) | data formatting | bytes 3276800
  163.3 2.2 %collective-permute-done.38.refs_7_ = bf16[352,128]{1,0:T(8,128)(2,1)S(1)} collective-permute-done((bf16[352,128]{1,0:T(8,128)(2,1)S(1)}, bf16[352,128]{1,0:T(8,128)(2,1)S(1)}, u32[]{:S(2)}, u32[]{:S(2)}) %collective-permute-start.38) | collective-permute-done | bytes 90144 | tf_op jit(solution)/shard_map/ppermute | solution.py:795
  (128 shorter events, 30.5 us)
Async XLA Ops:
  2.2 7.8 %collective-permute-start.2 = (bf16[224,128]{1,0:T(8,128)(2,1)}, bf16[224,128]{1,0:T(8,128)(2,1)S(1)}, u32[]{:S(2)}, u32[]{:S(2)}) collective-permute-start(bf16[224,128]{1,0:T(8,128)(2,1)} %pack.2), channel_id=1, source_target_pairs={{0,24},{8,16},{16,8},{24,0},{1,25},{9,17},{17,9},{25,1},{2,26},{10... | collective-permute-start | bytes 172040 | tf_op jit(solution)/shard_map/ppermute | solution.py:795
  12.6 8.9 %collective-permute-start.12 = (bf16[9,64,128]{2,1,0:T(8,128)(2,1)}, bf16[9,64,128]{2,1,0:T(8,128)(2,1)S(1)}, u32[]{:S(2)}, u32[]{:S(2)}) collective-permute-start(bf16[9,64,128]{2,1,0:T(8,128)(2,1)} %pack.3), channel_id=1, source_target_pairs={{0,24},{8,16},{16,8},{24,0},{1,25},{9,17},{17,9},{25,1},{2,26},{10... | collective-permute-start | bytes 442376 | tf_op jit(solution)/shard_map/ppermute | solution.py:795
  15.3 12.2 %collective-permute-start.11 = (bf16[9,64,128]{2,1,0:T(8,128)(2,1)}, bf16[9,64,128]{2,1,0:T(8,128)(2,1)S(1)}, u32[]{:S(2)}, u32[]{:S(2)}) collective-permute-start(bf16[9,64,128]{2,1,0:T(8,128)(2,1)} %pack.3), channel_id=1, source_target_pairs={{0,16},{8,24},{16,0},{24,8},{1,17},{9,25},{17,1},{25,9},{2,18},{10... | collective-permute-start | bytes 442376 | tf_op jit(solution)/shard_map/ppermute | solution.py:795
  15.4 14.0 %collective-permute-start.10 = (bf16[9,64,128]{2,1,0:T(8,128)(2,1)}, bf16[9,64,128]{2,1,0:T(8,128)(2,1)S(1)}, u32[]{:S(2)}, u32[]{:S(2)}) collective-permute-start(bf16[9,64,128]{2,1,0:T(8,128)(2,1)} %pack.3), channel_id=1, source_target_pairs={{0,8},{8,0},{16,24},{24,16},{1,9},{9,1},{17,25},{25,17},{2,10},{10... | collective-permute-start | bytes 442376 | tf_op jit(solution)/shard_map/ppermute | solution.py:795
  17.1 10.4 %collective-permute-start.8 = (bf16[4,224,128]{2,1,0:T(8,128)(2,1)S(1)}, bf16[4,224,128]{2,1,0:T(8,128)(2,1)S(1)}, u32[]{:S(2)}, u32[]{:S(2)}) collective-permute-start(bf16[4,224,128]{2,1,0:T(8,128)(2,1)S(1)} %pad_maximum_fusion.1.refs_3_.refs_11_.refs_5_), channel_id=1, source_target_pairs={{0,6},{1,7},{2,4},{3,5},{4,2},{5,3},{6,0},{7,1},{8,14},{9,15},{10,... | collective-permute-start | bytes 688136 | tf_op jit(solution)/shard_map/ppermute | solution.py:795
  19.6 9.1 %collective-permute-start.6 = (bf16[4,224,128]{2,1,0:T(8,128)(2,1)S(1)}, bf16[4,224,128]{2,1,0:T(8,128)(2,1)S(1)}, u32[]{:S(2)}, u32[]{:S(2)}) collective-permute-start(bf16[4,224,128]{2,1,0:T(8,128)(2,1)S(1)} %pad_maximum_fusion.1.refs_3_.refs_11_.refs_5_), channel_id=1, source_target_pairs={{0,4},{1,5},{2,6},{3,7},{4,0},{5,1},{6,2},{7,3},{8,12},{9,13},{10,... | collective-permute-start | bytes 688136 | tf_op jit(solution)/shard_map/ppermute | solution.py:795
  29.4 30.2 %collective-permute-start.16 = (bf16[4,9,64,128]{3,2,1,0:T(8,128)(2,1)S(1)}, bf16[4,9,64,128]{3,2,1,0:T(8,128)(2,1)S(1)}, u32[]{:S(2)}, u32[]{:S(2)}) collective-permute-start(bf16[4,9,64,128]{3,2,1,0:T(8,128)(2,1)S(1)} %pad_maximum_fusion.refs_5_), channel_id=1, source_target_pairs={{0,6},{1,7},{2,4},{3,5},{4,2},{5,3},{6,0},{7,1},{8,14},{9,15},{10,... | collective-permute-start | bytes 1769480 | tf_op jit(solution)/shard_map/ppermute | solution.py:795
  31.3 28.4 %collective-permute-start.15 = (bf16[4,9,64,128]{3,2,1,0:T(8,128)(2,1)S(1)}, bf16[4,9,64,128]{3,2,1,0:T(8,128)(2,1)S(1)}, u32[]{:S(2)}, u32[]{:S(2)}) collective-permute-start(bf16[4,9,64,128]{3,2,1,0:T(8,128)(2,1)S(1)} %pad_maximum_fusion.refs_5_), channel_id=1, source_target_pairs={{0,4},{1,5},{2,6},{3,7},{4,0},{5,1},{6,2},{7,3},{8,12},{9,13},{10,... | collective-permute-start | bytes 1769480 | tf_op jit(solution)/shard_map/ppermute | solution.py:795
  32.6 27.1 %collective-permute-start.14 = (bf16[4,9,64,128]{3,2,1,0:T(8,128)(2,1)S(1)}, bf16[4,9,64,128]{3,2,1,0:T(8,128)(2,1)S(1)}, u32[]{:S(2)}, u32[]{:S(2)}) collective-permute-start(bf16[4,9,64,128]{3,2,1,0:T(8,128)(2,1)S(1)} %pad_maximum_fusion.refs_5_), channel_id=1, source_target_pairs={{0,2},{1,3},{2,0},{3,1},{4,6},{5,7},{6,4},{7,5},{8,10},{9,11},{10,... | collective-permute-start | bytes 1769480 | tf_op jit(solution)/shard_map/ppermute | solution.py:795
  33.0 29.3 %collective-permute-start.13 = (bf16[4,9,64,128]{3,2,1,0:T(8,128)(2,1)S(1)}, bf16[4,9,64,128]{3,2,1,0:T(8,128)(2,1)S(1)}, u32[]{:S(2)}, u32[]{:S(2)}) collective-permute-start(bf16[4,9,64,128]{3,2,1,0:T(8,128)(2,1)S(1)} %pad_maximum_fusion.refs_5_), channel_id=1, source_target_pairs={{0,1},{1,0},{2,3},{3,2},{4,5},{5,4},{6,7},{7,6},{8,9},{9,8},{10,11... | collective-permute-start | bytes 1769480 | tf_op jit(solution)/shard_map/ppermute | solution.py:795
  105.4 29.7 %collective-permute-start.24 = (bf16[4,576,128]{2,1,0:T(8,128)(2,1)S(1)}, bf16[4,576,128]{2,1,0:T(8,128)(2,1)S(1)}, u32[]{:S(2)}, u32[]{:S(2)}) collective-permute-start(bf16[4,576,128]{2,1,0:T(8,128)(2,1)S(1)} %add_convert_fusion.3), channel_id=1, source_target_pairs={{0,2},{1,3},{2,0},{3,1},{4,6},{5,7},{6,4},{7,5},{8,10},{9,11},{10,... | collective-permute-start | bytes 1769480 | tf_op jit(solution)/shard_map/ppermute | solution.py:795
  107.2 28.0 %collective-permute-start.25 = (bf16[4,576,128]{2,1,0:T(8,128)(2,1)S(1)}, bf16[4,576,128]{2,1,0:T(8,128)(2,1)S(1)}, u32[]{:S(2)}, u32[]{:S(2)}) collective-permute-start(bf16[4,576,128]{2,1,0:T(8,128)(2,1)S(1)} %add_convert_fusion.2), channel_id=1, source_target_pairs={{0,4},{1,5},{2,6},{3,7},{4,0},{5,1},{6,2},{7,3},{8,12},{9,13},{10,... | collective-permute-start | bytes 1769480 | tf_op jit(solution)/shard_map/ppermute | solution.py:795
  108.2 27.0 %collective-permute-start.26 = (bf16[4,576,128]{2,1,0:T(8,128)(2,1)S(1)}, bf16[4,576,128]{2,1,0:T(8,128)(2,1)S(1)}, u32[]{:S(2)}, u32[]{:S(2)}) collective-permute-start(bf16[4,576,128]{2,1,0:T(8,128)(2,1)S(1)} %add_convert_fusion.1), channel_id=1, source_target_pairs={{0,6},{1,7},{2,4},{3,5},{4,2},{5,3},{6,0},{7,1},{8,14},{9,15},{10,... | collective-permute-start | bytes 1769480 | tf_op jit(solution)/shard_map/ppermute | solution.py:795
  135.3 9.5 %collective-permute-start.27 = (bf16[4,224,128]{2,1,0:T(8,128)(2,1)S(1)}, bf16[4,224,128]{2,1,0:T(8,128)(2,1)S(1)}, u32[]{:S(2)}, u32[]{:S(2)}) collective-permute-start(bf16[4,224,128]{2,1,0:T(8,128)(2,1)S(1)} %get-tuple-element.104), channel_id=1, source_target_pairs={{0,1},{1,0},{2,3},{3,2},{4,5},{5,4},{6,7},{7,6},{8,9},{9,8},{10,11... | collective-permute-start | bytes 688136 | tf_op jit(solution)/shard_map/ppermute | solution.py:795
  135.8 7.7 %collective-permute-start.30 = (bf16[4,224,128]{2,1,0:T(8,128)(2,1)S(1)}, bf16[4,224,128]{2,1,0:T(8,128)(2,1)S(1)}, u32[]{:S(2)}, u32[]{:S(2)}) collective-permute-start(bf16[4,224,128]{2,1,0:T(8,128)(2,1)S(1)} %get-tuple-element.110), channel_id=1, source_target_pairs={{0,1},{1,0},{2,3},{3,2},{4,5},{5,4},{6,7},{7,6},{8,9},{9,8},{10,11... | collective-permute-start | bytes 688136 | tf_op jit(solution)/shard_map/ppermute | solution.py:795
  136.6 21.0 %collective-permute-start.36 = (bf16[576,128]{1,0:T(8,128)(2,1)S(1)}, bf16[576,128]{1,0:T(8,128)(2,1)S(1)}, u32[]{:S(2)}, u32[]{:S(2)}) collective-permute-start(bf16[576,128]{1,0:T(8,128)(2,1)S(1)} %get-tuple-element.136), channel_id=1, source_target_pairs={{0,24},{8,16},{16,8},{24,0},{1,25},{9,17},{17,9},{25,1},{2,26},{10... | collective-permute-start | bytes 442376 | tf_op jit(solution)/shard_map/ppermute | solution.py:795
  138.8 24.5 %collective-permute-start.35 = (bf16[576,128]{1,0:T(8,128)(2,1)S(1)}, bf16[576,128]{1,0:T(8,128)(2,1)S(1)}, u32[]{:S(2)}, u32[]{:S(2)}) collective-permute-start(bf16[576,128]{1,0:T(8,128)(2,1)S(1)} %get-tuple-element.137), channel_id=1, source_target_pairs={{0,16},{8,24},{16,0},{24,8},{1,17},{9,25},{17,1},{25,9},{2,18},{10... | collective-permute-start | bytes 442376 | tf_op jit(solution)/shard_map/ppermute | solution.py:795
  142.3 11.4 %collective-permute-start.31 = (bf16[4,224,128]{2,1,0:T(8,128)(2,1)S(1)}, bf16[4,224,128]{2,1,0:T(8,128)(2,1)S(1)}, u32[]{:S(2)}, u32[]{:S(2)}) collective-permute-start(bf16[4,224,128]{2,1,0:T(8,128)(2,1)S(1)} %add_convert_fusion.8), channel_id=1, source_target_pairs={{0,2},{1,3},{2,0},{3,1},{4,6},{5,7},{6,4},{7,5},{8,10},{9,11},{10,... | collective-permute-start | bytes 688136 | tf_op jit(solution)/shard_map/ppermute | solution.py:795
  143.5 10.3 %collective-permute-start.32 = (bf16[4,224,128]{2,1,0:T(8,128)(2,1)S(1)}, bf16[4,224,128]{2,1,0:T(8,128)(2,1)S(1)}, u32[]{:S(2)}, u32[]{:S(2)}) collective-permute-start(bf16[4,224,128]{2,1,0:T(8,128)(2,1)S(1)} %add_convert_fusion.7), channel_id=1, source_target_pairs={{0,4},{1,5},{2,6},{3,7},{4,0},{5,1},{6,2},{7,3},{8,12},{9,13},{10,... | collective-permute-start | bytes 688136 | tf_op jit(solution)/shard_map/ppermute | solution.py:795
  144.8 10.5 %collective-permute-start.33 = (bf16[4,224,128]{2,1,0:T(8,128)(2,1)S(1)}, bf16[4,224,128]{2,1,0:T(8,128)(2,1)S(1)}, u32[]{:S(2)}, u32[]{:S(2)}) collective-permute-start(bf16[4,224,128]{2,1,0:T(8,128)(2,1)S(1)} %add_convert_fusion.6), channel_id=1, source_target_pairs={{0,6},{1,7},{2,4},{3,5},{4,2},{5,3},{6,0},{7,1},{8,14},{9,15},{10,... | collective-permute-start | bytes 688136 | tf_op jit(solution)/shard_map/ppermute | solution.py:795
  153.7 9.6 %collective-permute-start.34 = (bf16[576,128]{1,0:T(8,128)(2,1)S(1)}, bf16[576,128]{1,0:T(8,128)(2,1)S(1)}, u32[]{:S(2)}, u32[]{:S(2)}) collective-permute-start(bf16[576,128]{1,0:T(8,128)(2,1)S(1)} %get-tuple-element.138), channel_id=1, source_target_pairs={{0,8},{8,0},{16,24},{24,16},{1,9},{9,1},{17,25},{25,17},{2,10},{10... | collective-permute-start | bytes 442376 | tf_op jit(solution)/shard_map/ppermute | solution.py:795
  155.5 7.9 %collective-permute-start.39 = (bf16[352,128]{1,0:T(8,128)(2,1)S(1)}, bf16[352,128]{1,0:T(8,128)(2,1)S(1)}, u32[]{:S(2)}, u32[]{:S(2)}) collective-permute-start(bf16[352,128]{1,0:T(8,128)(2,1)S(1)} %get-tuple-element.142), channel_id=1, source_target_pairs={{0,24},{8,16},{16,8},{24,0},{1,25},{9,17},{17,9},{25,1},{2,26},{10... | collective-permute-start | bytes 270344 | tf_op jit(solution)/shard_map/ppermute | solution.py:795
  157.6 7.9 %collective-permute-start.38 = (bf16[352,128]{1,0:T(8,128)(2,1)S(1)}, bf16[352,128]{1,0:T(8,128)(2,1)S(1)}, u32[]{:S(2)}, u32[]{:S(2)}) collective-permute-start(bf16[352,128]{1,0:T(8,128)(2,1)S(1)} %get-tuple-element.143), channel_id=1, source_target_pairs={{0,16},{8,24},{16,0},{24,8},{1,17},{9,25},{17,1},{25,9},{2,18},{10... | collective-permute-start | bytes 270344 | tf_op jit(solution)/shard_map/ppermute | solution.py:795
  157.7 7.9 %collective-permute-start.37 = (bf16[352,128]{1,0:T(8,128)(2,1)S(1)}, bf16[352,128]{1,0:T(8,128)(2,1)S(1)}, u32[]{:S(2)}, u32[]{:S(2)}) collective-permute-start(bf16[352,128]{1,0:T(8,128)(2,1)S(1)} %get-tuple-element.144), channel_id=1, source_target_pairs={{0,8},{8,0},{16,24},{24,16},{1,9},{9,1},{17,25},{25,17},{2,10},{10... | collective-permute-start | bytes 270344 | tf_op jit(solution)/shard_map/ppermute | solution.py:795
  (37 other events, 241.5 us)

commit v5 on v4

--- a/solution.py
+++ b/solution.py
@@ -533,7 +533,7 @@
             V((NG, FF // geo.r, geo.r, TL), bf16),
             pltpu.SemaphoreType.DMA,
         ],
-        compiler_params=params(36),
+        compiler_params=params(40),
         cost_estimate=cost(44),
         name="mlp",
     )(me, live, tok, cot, attn, *bufs, vec, b1)
@@ -858,7 +858,7 @@
         mine_a = gather_z(buf_a, nz)
         pb = bias(table, place)
         planes_a = gather_xy(mine_a, nw)
-        mine_b = gather_z(after(buf_b, mine_a), nz)
+        mine_b = gather_z(buf_b, nz)
         bufs_a = gather_core(planes_a, nw)
         planes_b = gather_xy(mine_b, nw)
         own_core = swap(planes_b[0], "win", nw, 1)
@@ -875,7 +875,8 @@
         low_b = sum_xy(parts_b)
         sums_a = sum_core(gq, nw)
         parts_a = swap_xy(sums_a, nw)
-        own_b = swap_z(low_b, nz)
+        held = after(low_b, *sums_a)
+        own_b = [swap((low_b if e == nz - 1 else held)[e], "fsdp", nz, e) for e in range(1, nz)]
         grad_tokens = input_bwd(geo, me, tokens, dc, dx1, after(vec, *sums_a), bufs_a)
         parts_a = lax.optimization_barrier((*parts_a, grad_tokens))[:-1]
         low_a = sum_xy(parts_a)

time: 167 us -> 163 us (0.976)
  waiting for transfers between devices: 11.4 us -> 7.28 us
    ppermute x40, waiting for transfers between devices: 11.4 us -> 7.28 us  [swap(): return lax.ppermute(x, axis, [(i, i ^ d) for i in range(size)])]
    unnamed x46 -> x38, local copies, waits for them, and re-layouts: 17.2 us -> 16.2 us
  transfers between devices with their start and end apart: 40 -> 40, of which waited for: 11 -> 10; matrix products, arithmetic and copies ran while one was open for 5% -> 5% of each run, Pallas kernels for 32% -> 32%
where the time goes in v5:
time: 163 us
  Pallas kernels  95.4 us (59%)
  starting transfers between devices  40.6 us (25%)
  local copies, waits for them, and re-layouts  16.3 us (10%)
  waiting for transfers between devices  7.28 us (4%)
  between operations  1.67 us (1%)
    ppermute x40, starting transfers between devices, swap(): return lax.ppermute(x, axis, [(i, i ^ d) for i in range(size)])  40.6 us
    pallas_call x1, Pallas kernels, mlp(): pl.pallas_call(functools.partial(mlp_body, geo, G, FC), grid=(B // G,), i...  40.1 us
    pallas_call x1, Pallas kernels, attn_bwd(): pl.pallas_call(functools.partial(attn_bwd_body, geo, G), grid=(B // G,),...  23.7 us
    pallas_call x1, Pallas kernels, attn_fwd(): pl.pallas_call(functools.partial(attn_fwd_body, geo, G, vec is not None),...  18.7 us
    unnamed x38, local copies, waits for them, and re-layouts  16.2 us
    pallas_call x1, Pallas kernels, input_bwd(): pl.pallas_call(functools.partial(input_bwd_body, geo, G), grid=(B // G,),...  7.41 us
    ppermute x40, waiting for transfers between devices, swap(): return lax.ppermute(x, axis, [(i, i ^ d) for i in range(size)])  7.28 us
  transfers between devices with their start and end apart: 40, of which 10 were waited for; matrix products, arithmetic and copies ran while one was open for 5% of the time, Pallas kernels for 32%

profile of v5, /device:TPU:0, one launch (start us, length us, event | category | flops | bytes accessed | tf_op | source)
XLA Modules:
  0.0 162.8 jit_solution(5999432242498030010)
XLA Ops:
  0.6 1.5 pack.2
  2.2 5.1 %collective-permute-start.2 = (bf16[224,128]{1,0:T(8,128)(2,1)}, bf16[224,128]{1,0:T(8,128)(2,1)S(1)}, u32[]{:S(2)}, u32[]{:S(2)}) collective-permute-start(bf16[224,128]{1,0:T(8,128)(2,1)} %pack.2), channel_id=1, source_target_pairs={{0,24},{8,16},{16,8},{24,0},{1,25},{9,17},{17,9},{25,1},{2,26},{10... | collective-permute-start | bytes 172040 | tf_op jit(solution)/shard_map/ppermute | solution.py:795
  7.9 1.6 pack.3
  9.5 3.8 %collective-permute-start.12 = (bf16[9,64,128]{2,1,0:T(8,128)(2,1)}, bf16[9,64,128]{2,1,0:T(8,128)(2,1)S(1)}, u32[]{:S(2)}, u32[]{:S(2)}) collective-permute-start(bf16[9,64,128]{2,1,0:T(8,128)(2,1)} %pack.3), channel_id=1, source_target_pairs={{0,24},{8,16},{16,8},{24,0},{1,25},{9,17},{17,9},{25,1},{2,26},{10... | collective-permute-start | bytes 442376 | tf_op jit(solution)/shard_map/ppermute | solution.py:795
  14.1 2.7 %collective-permute-start.8 = (bf16[4,224,128]{2,1,0:T(8,128)(2,1)S(1)}, bf16[4,224,128]{2,1,0:T(8,128)(2,1)S(1)}, u32[]{:S(2)}, u32[]{:S(2)}) collective-permute-start(bf16[4,224,128]{2,1,0:T(8,128)(2,1)S(1)} %pad_maximum_fusion.1.refs_3_.refs_11_.refs_5_), channel_id=1, source_target_pairs={{0,6},{1,7},{2,4},{3,5},{4,2},{5,3},{6,0},{7,1},{8,14},{9,15},{10,... | collective-permute-start | bytes 688136 | tf_op jit(solution)/shard_map/ppermute | solution.py:795
  18.5 1.6 %collective-permute-start.4 = (bf16[4,224,128]{2,1,0:T(8,128)(2,1)S(1)}, bf16[4,224,128]{2,1,0:T(8,128)(2,1)S(1)}, u32[]{:S(2)}, u32[]{:S(2)}) collective-permute-start(bf16[4,224,128]{2,1,0:T(8,128)(2,1)S(1)} %pad_maximum_fusion.1.refs_3_.refs_11_.refs_5_), channel_id=1, source_target_pairs={{0,2},{1,3},{2,0},{3,1},{4,6},{5,7},{6,4},{7,5},{8,10},{9,11},{10,... | collective-permute-start | bytes 688136 | tf_op jit(solution)/shard_map/ppermute | solution.py:795
  22.2 2.4 %copy.21.refs_1_.refs_2_ = bf16[16,100,512]{2,1,0:T(8,128)(2,1)S(1)} copy(bf16[16,100,512]{2,0,1:T(8,128)(2,1)} %param.11) | data formatting | bytes 3276800 | tf_op args[0]
  26.6 2.3 %collective-permute-start.16 = (bf16[4,9,64,128]{3,2,1,0:T(8,128)(2,1)S(1)}, bf16[4,9,64,128]{3,2,1,0:T(8,128)(2,1)S(1)}, u32[]{:S(2)}, u32[]{:S(2)}) collective-permute-start(bf16[4,9,64,128]{3,2,1,0:T(8,128)(2,1)S(1)} %pad_maximum_fusion.refs_5_), channel_id=1, source_target_pairs={{0,6},{1,7},{2,4},{3,5},{4,2},{5,3},{6,0},{7,1},{8,14},{9,15},{10,... | collective-permute-start | bytes 1769480 | tf_op jit(solution)/shard_map/ppermute | solution.py:795
  30.2 18.7 %attn_fwd.1 = (bf16[1792,512]{1,0:T(8,128)(2,1)S(1)}, bf16[1792,512]{1,0:T(8,128)(2,1)S(1)}, bf16[1792,512]{1,0:T(8,128)(2,1)S(1)}, bf16[1792,512]{1,0:T(8,128)(...) custom-call(s32[2]{0:T(128)S(1)} %pad_add_fusion.refs_0_, ...), custom_call_target="tpu_custom_call" | custom-call | flops 32999999488 | bytes 30000000 | tf_op jit(solution)/shard_map/attn_fwd/pallas_call | solution.py:348
  48.9 2.9 %copy-done.4 = bf16[16,4,112,512]{3,2,1,0:T(8,128)(2,1)} copy-done((bf16[16,4,112,512]{3,2,1,0:T(8,128)(2,1)}, bf16[16,4,112,512]{3,2,1,0:T(8,128)(2,1)S(1)}, u32[]{:S(2)}) %copy-start.4) | copy-done | bytes 7340056
  59.4 40.1 %mlp.1 = (bf16[16,100,512]{2,1,0:T(8,128)(2,1)S(1)}, f32[1792,512]{1,0:T(8,128)}, bf16[1792,512]{1,0:T(8,128)(2,1)}, f32[8,512]{1,0:T(8,128)S(1)}, f32[1,2048]{1...) custom-call(s32[2]{0:T(128)S(1)} %pad_add_fusion.refs_0_, ...), custom_call_target="tpu_custom_call" | custom-call | flops 48399998976 | bytes 44000000 | tf_op jit(solution)/shard_map/mlp/pallas_call | solution.py:514
  101.8 1.6 collective-permute-start.24
  103.5 1.5 collective-permute-start.25
  106.5 1.5 copy-done.11
  108.0 23.7 %attn_bwd.1 = (bf16[1792,1536]{1,0:T(8,128)(2,1)S(1)}, f32[24,512]{1,0:T(8,128)}, bf16[4,224,128]{2,1,0:T(8,128)(2,1)S(1)}, bf16[4,224,128]{2,1,0:T(8,128)(2,1)S...) custom-call(s32[2]{0:T(128)S(1)} %pad_add_fusion.refs_0_, ...), custom_call_target="tpu_custom_call" | custom-call | flops 32999999488 | bytes 30000000 | tf_op jit(solution)/shard_map/attn_bwd/pallas_call | solution.py:659
  133.2 3.3 %collective-permute-start.36 = (bf16[576,128]{1,0:T(8,128)(2,1)S(1)}, bf16[576,128]{1,0:T(8,128)(2,1)S(1)}, u32[]{:S(2)}, u32[]{:S(2)}) collective-permute-start(bf16[576,128]{1,0:T(8,128)(2,1)S(1)} %slice_bitcast_fusion), channel_id=1, source_target_pairs={{0,24},{8,16},{16,8},{24,0},{1,25},{9,17},{17,9},{25,1},{2,26},{10... | collective-permute-start | bytes 442376 | tf_op jit(solution)/shard_map/ppermute | solution.py:795
  139.0 1.4 collective-permute-start.33
  140.5 2.5 %collective-permute-start.35 = (bf16[576,128]{1,0:T(8,128)(2,1)S(1)}, bf16[576,128]{1,0:T(8,128)(2,1)S(1)}, u32[]{:S(2)}, u32[]{:S(2)}) collective-permute-start(bf16[576,128]{1,0:T(8,128)(2,1)S(1)} %get-tuple-element.136), channel_id=1, source_target_pairs={{0,16},{8,24},{16,0},{24,8},{1,17},{9,25},{17,1},{25,9},{2,18},{10... | collective-permute-start | bytes 442376 | tf_op jit(solution)/shard_map/ppermute | solution.py:795
  143.0 7.4 %input_bwd.1 = bf16[16,100,512]{2,1,0:T(8,128)(2,1)S(1)} custom-call(s32[2]{0:T(128)S(1)} %pad_add_fusion.refs_0_, bf16[16,100,512]{2,1,0:T(8,128)(2,1)S(1)} %copy.21.refs_1_.refs_2_, bf16[1792,1536]{1,0:T(8,128)(2,1)S(1)} %get-tuple-element.92.refs_2_, f32[1792,512]{1,0:T(8,128)S(1)} %copy-done.1, f32[8,512]{1,0:T(8,128)S(1)} %get-tuple-element.110.refs_13_.refs_7_.refs_4_, ...), custom_call_target="tpu_custom_call" | custom-call | flops 11000000512 | bytes 10000000 | tf_op jit(solution)/shard_map/input_bwd/pallas_call | solution.py:712
  150.9 2.4 %collective-permute-start.39 = (bf16[352,128]{1,0:T(8,128)(2,1)S(1)}, bf16[352,128]{1,0:T(8,128)(2,1)S(1)}, u32[]{:S(2)}, u32[]{:S(2)}) collective-permute-start(bf16[352,128]{1,0:T(8,128)(2,1)S(1)} %get-tuple-element.141), channel_id=1, source_target_pairs={{0,24},{8,16},{16,8},{24,0},{1,25},{9,17},{17,9},{25,1},{2,26},{10... | collective-permute-start | bytes 270344 | tf_op jit(solution)/shard_map/ppermute | solution.py:795
  155.4 1.7 %copy.24 = bf16[16,100,512]{2,0,1:T(8,128)(2,1)} copy(bf16[16,100,512]{2,1,0:T(8,128)(2,1)S(1)} %get-tuple-element.127) | data formatting | bytes 3276800
  157.1 1.7 %copy.25 = bf16[16,100,512]{2,0,1:T(8,128)(2,1)} copy(bf16[16,100,512]{2,1,0:T(8,128)(2,1)S(1)} %input_bwd.1) | data formatting | bytes 3276800
  159.8 1.7 %collective-permute-done.38.refs_7_ = bf16[352,128]{1,0:T(8,128)(2,1)S(1)} collective-permute-done((bf16[352,128]{1,0:T(8,128)(2,1)S(1)}, bf16[352,128]{1,0:T(8,128)(2,1)S(1)}, u32[]{:S(2)}, u32[]{:S(2)}) %collective-permute-start.38) | collective-permute-done | bytes 90144 | tf_op jit(solution)/shard_map/ppermute | solution.py:795
  161.4 1.4 finish.1
  (121 shorter events, 26.8 us)
Async XLA Ops:
  2.2 11.2 %collective-permute-start.2 = (bf16[224,128]{1,0:T(8,128)(2,1)}, bf16[224,128]{1,0:T(8,128)(2,1)S(1)}, u32[]{:S(2)}, u32[]{:S(2)}) collective-permute-start(bf16[224,128]{1,0:T(8,128)(2,1)} %pack.2), channel_id=1, source_target_pairs={{0,24},{8,16},{16,8},{24,0},{1,25},{9,17},{17,9},{25,1},{2,26},{10... | collective-permute-start | bytes 172040 | tf_op jit(solution)/shard_map/ppermute | solution.py:795
  9.5 9.0 %collective-permute-start.12 = (bf16[9,64,128]{2,1,0:T(8,128)(2,1)}, bf16[9,64,128]{2,1,0:T(8,128)(2,1)S(1)}, u32[]{:S(2)}, u32[]{:S(2)}) collective-permute-start(bf16[9,64,128]{2,1,0:T(8,128)(2,1)} %pack.3), channel_id=1, source_target_pairs={{0,24},{8,16},{16,8},{24,0},{1,25},{9,17},{17,9},{25,1},{2,26},{10... | collective-permute-start | bytes 442376 | tf_op jit(solution)/shard_map/ppermute | solution.py:795
  13.3 11.9 %collective-permute-start.11 = (bf16[9,64,128]{2,1,0:T(8,128)(2,1)}, bf16[9,64,128]{2,1,0:T(8,128)(2,1)S(1)}, u32[]{:S(2)}, u32[]{:S(2)}) collective-permute-start(bf16[9,64,128]{2,1,0:T(8,128)(2,1)} %pack.3), channel_id=1, source_target_pairs={{0,16},{8,24},{16,0},{24,8},{1,17},{9,25},{17,1},{25,9},{2,18},{10... | collective-permute-start | bytes 442376 | tf_op jit(solution)/shard_map/ppermute | solution.py:795
  13.4 13.2 %collective-permute-start.10 = (bf16[9,64,128]{2,1,0:T(8,128)(2,1)}, bf16[9,64,128]{2,1,0:T(8,128)(2,1)S(1)}, u32[]{:S(2)}, u32[]{:S(2)}) collective-permute-start(bf16[9,64,128]{2,1,0:T(8,128)(2,1)} %pack.3), channel_id=1, source_target_pairs={{0,8},{8,0},{16,24},{24,16},{1,9},{9,1},{17,25},{25,17},{2,10},{10... | collective-permute-start | bytes 442376 | tf_op jit(solution)/shard_map/ppermute | solution.py:795
  14.1 11.1 %collective-permute-start.8 = (bf16[4,224,128]{2,1,0:T(8,128)(2,1)S(1)}, bf16[4,224,128]{2,1,0:T(8,128)(2,1)S(1)}, u32[]{:S(2)}, u32[]{:S(2)}) collective-permute-start(bf16[4,224,128]{2,1,0:T(8,128)(2,1)S(1)} %pad_maximum_fusion.1.refs_3_.refs_11_.refs_5_), channel_id=1, source_target_pairs={{0,6},{1,7},{2,4},{3,5},{4,2},{5,3},{6,0},{7,1},{8,14},{9,15},{10,... | collective-permute-start | bytes 688136 | tf_op jit(solution)/shard_map/ppermute | solution.py:795
  16.8 9.2 %collective-permute-start.6 = (bf16[4,224,128]{2,1,0:T(8,128)(2,1)S(1)}, bf16[4,224,128]{2,1,0:T(8,128)(2,1)S(1)}, u32[]{:S(2)}, u32[]{:S(2)}) collective-permute-start(bf16[4,224,128]{2,1,0:T(8,128)(2,1)S(1)} %pad_maximum_fusion.1.refs_3_.refs_11_.refs_5_), channel_id=1, source_target_pairs={{0,4},{1,5},{2,6},{3,7},{4,0},{5,1},{6,2},{7,3},{8,12},{9,13},{10,... | collective-permute-start | bytes 688136 | tf_op jit(solution)/shard_map/ppermute | solution.py:795
  18.5 7.7 %collective-permute-start.4 = (bf16[4,224,128]{2,1,0:T(8,128)(2,1)S(1)}, bf16[4,224,128]{2,1,0:T(8,128)(2,1)S(1)}, u32[]{:S(2)}, u32[]{:S(2)}) collective-permute-start(bf16[4,224,128]{2,1,0:T(8,128)(2,1)S(1)} %pad_maximum_fusion.1.refs_3_.refs_11_.refs_5_), channel_id=1, source_target_pairs={{0,2},{1,3},{2,0},{3,1},{4,6},{5,7},{6,4},{7,5},{8,10},{9,11},{10,... | collective-permute-start | bytes 688136 | tf_op jit(solution)/shard_map/ppermute | solution.py:795
  26.6 29.0 %collective-permute-start.16 = (bf16[4,9,64,128]{3,2,1,0:T(8,128)(2,1)S(1)}, bf16[4,9,64,128]{3,2,1,0:T(8,128)(2,1)S(1)}, u32[]{:S(2)}, u32[]{:S(2)}) collective-permute-start(bf16[4,9,64,128]{3,2,1,0:T(8,128)(2,1)S(1)} %pad_maximum_fusion.refs_5_), channel_id=1, source_target_pairs={{0,6},{1,7},{2,4},{3,5},{4,2},{5,3},{6,0},{7,1},{8,14},{9,15},{10,... | collective-permute-start | bytes 1769480 | tf_op jit(solution)/shard_map/ppermute | solution.py:795
  28.9 26.7 %collective-permute-start.15 = (bf16[4,9,64,128]{3,2,1,0:T(8,128)(2,1)S(1)}, bf16[4,9,64,128]{3,2,1,0:T(8,128)(2,1)S(1)}, u32[]{:S(2)}, u32[]{:S(2)}) collective-permute-start(bf16[4,9,64,128]{3,2,1,0:T(8,128)(2,1)S(1)} %pad_maximum_fusion.refs_5_), channel_id=1, source_target_pairs={{0,4},{1,5},{2,6},{3,7},{4,0},{5,1},{6,2},{7,3},{8,12},{9,13},{10,... | collective-permute-start | bytes 1769480 | tf_op jit(solution)/shard_map/ppermute | solution.py:795
  29.6 26.0 %collective-permute-start.14 = (bf16[4,9,64,128]{3,2,1,0:T(8,128)(2,1)S(1)}, bf16[4,9,64,128]{3,2,1,0:T(8,128)(2,1)S(1)}, u32[]{:S(2)}, u32[]{:S(2)}) collective-permute-start(bf16[4,9,64,128]{3,2,1,0:T(8,128)(2,1)S(1)} %pad_maximum_fusion.refs_5_), channel_id=1, source_target_pairs={{0,2},{1,3},{2,0},{3,1},{4,6},{5,7},{6,4},{7,5},{8,10},{9,11},{10,... | collective-permute-start | bytes 1769480 | tf_op jit(solution)/shard_map/ppermute | solution.py:795
  30.2 28.0 %collective-permute-start.13 = (bf16[4,9,64,128]{3,2,1,0:T(8,128)(2,1)S(1)}, bf16[4,9,64,128]{3,2,1,0:T(8,128)(2,1)S(1)}, u32[]{:S(2)}, u32[]{:S(2)}) collective-permute-start(bf16[4,9,64,128]{3,2,1,0:T(8,128)(2,1)S(1)} %pad_maximum_fusion.refs_5_), channel_id=1, source_target_pairs={{0,1},{1,0},{2,3},{3,2},{4,5},{5,4},{6,7},{7,6},{8,9},{9,8},{10,11... | collective-permute-start | bytes 1769480 | tf_op jit(solution)/shard_map/ppermute | solution.py:795
  101.8 29.9 %collective-permute-start.24 = (bf16[4,576,128]{2,1,0:T(8,128)(2,1)S(1)}, bf16[4,576,128]{2,1,0:T(8,128)(2,1)S(1)}, u32[]{:S(2)}, u32[]{:S(2)}) collective-permute-start(bf16[4,576,128]{2,1,0:T(8,128)(2,1)S(1)} %add_convert_fusion.3), channel_id=1, source_target_pairs={{0,2},{1,3},{2,0},{3,1},{4,6},{5,7},{6,4},{7,5},{8,10},{9,11},{10,... | collective-permute-start | bytes 1769480 | tf_op jit(solution)/shard_map/ppermute | solution.py:795
  103.5 28.2 %collective-permute-start.25 = (bf16[4,576,128]{2,1,0:T(8,128)(2,1)S(1)}, bf16[4,576,128]{2,1,0:T(8,128)(2,1)S(1)}, u32[]{:S(2)}, u32[]{:S(2)}) collective-permute-start(bf16[4,576,128]{2,1,0:T(8,128)(2,1)S(1)} %add_convert_fusion.2), channel_id=1, source_target_pairs={{0,4},{1,5},{2,6},{3,7},{4,0},{5,1},{6,2},{7,3},{8,12},{9,13},{10,... | collective-permute-start | bytes 1769480 | tf_op jit(solution)/shard_map/ppermute | solution.py:795
  105.1 26.6 %collective-permute-start.26 = (bf16[4,576,128]{2,1,0:T(8,128)(2,1)S(1)}, bf16[4,576,128]{2,1,0:T(8,128)(2,1)S(1)}, u32[]{:S(2)}, u32[]{:S(2)}) collective-permute-start(bf16[4,576,128]{2,1,0:T(8,128)(2,1)S(1)} %add_convert_fusion.1), channel_id=1, source_target_pairs={{0,6},{1,7},{2,4},{3,5},{4,2},{5,3},{6,0},{7,1},{8,14},{9,15},{10,... | collective-permute-start | bytes 1769480 | tf_op jit(solution)/shard_map/ppermute | solution.py:795
  131.7 8.7 %collective-permute-start.27 = (bf16[4,224,128]{2,1,0:T(8,128)(2,1)S(1)}, bf16[4,224,128]{2,1,0:T(8,128)(2,1)S(1)}, u32[]{:S(2)}, u32[]{:S(2)}) collective-permute-start(bf16[4,224,128]{2,1,0:T(8,128)(2,1)S(1)} %get-tuple-element.103), channel_id=1, source_target_pairs={{0,1},{1,0},{2,3},{3,2},{4,5},{5,4},{6,7},{7,6},{8,9},{9,8},{10,11... | collective-permute-start | bytes 688136 | tf_op jit(solution)/shard_map/ppermute | solution.py:795
  133.2 21.1 %collective-permute-start.36 = (bf16[576,128]{1,0:T(8,128)(2,1)S(1)}, bf16[576,128]{1,0:T(8,128)(2,1)S(1)}, u32[]{:S(2)}, u32[]{:S(2)}) collective-permute-start(bf16[576,128]{1,0:T(8,128)(2,1)S(1)} %slice_bitcast_fusion), channel_id=1, source_target_pairs={{0,24},{8,16},{16,8},{24,0},{1,25},{9,17},{17,9},{25,1},{2,26},{10... | collective-permute-start | bytes 442376 | tf_op jit(solution)/shard_map/ppermute | solution.py:795
  136.6 13.8 %collective-permute-start.31 = (bf16[4,224,128]{2,1,0:T(8,128)(2,1)S(1)}, bf16[4,224,128]{2,1,0:T(8,128)(2,1)S(1)}, u32[]{:S(2)}, u32[]{:S(2)}) collective-permute-start(bf16[4,224,128]{2,1,0:T(8,128)(2,1)S(1)} %add_convert_fusion.8), channel_id=1, source_target_pairs={{0,2},{1,3},{2,0},{3,1},{4,6},{5,7},{6,4},{7,5},{8,10},{9,11},{10,... | collective-permute-start | bytes 688136 | tf_op jit(solution)/shard_map/ppermute | solution.py:795
  138.0 12.7 %collective-permute-start.32 = (bf16[4,224,128]{2,1,0:T(8,128)(2,1)S(1)}, bf16[4,224,128]{2,1,0:T(8,128)(2,1)S(1)}, u32[]{:S(2)}, u32[]{:S(2)}) collective-permute-start(bf16[4,224,128]{2,1,0:T(8,128)(2,1)S(1)} %add_convert_fusion.7), channel_id=1, source_target_pairs={{0,4},{1,5},{2,6},{3,7},{4,0},{5,1},{6,2},{7,3},{8,12},{9,13},{10,... | collective-permute-start | bytes 688136 | tf_op jit(solution)/shard_map/ppermute | solution.py:795
  139.0 11.8 %collective-permute-start.33 = (bf16[4,224,128]{2,1,0:T(8,128)(2,1)S(1)}, bf16[4,224,128]{2,1,0:T(8,128)(2,1)S(1)}, u32[]{:S(2)}, u32[]{:S(2)}) collective-permute-start(bf16[4,224,128]{2,1,0:T(8,128)(2,1)S(1)} %add_convert_fusion.6), channel_id=1, source_target_pairs={{0,6},{1,7},{2,4},{3,5},{4,2},{5,3},{6,0},{7,1},{8,14},{9,15},{10,... | collective-permute-start | bytes 688136 | tf_op jit(solution)/shard_map/ppermute | solution.py:795
  140.5 18.3 %collective-permute-start.35 = (bf16[576,128]{1,0:T(8,128)(2,1)S(1)}, bf16[576,128]{1,0:T(8,128)(2,1)S(1)}, u32[]{:S(2)}, u32[]{:S(2)}) collective-permute-start(bf16[576,128]{1,0:T(8,128)(2,1)S(1)} %get-tuple-element.136), channel_id=1, source_target_pairs={{0,16},{8,24},{16,0},{24,8},{1,17},{9,25},{17,1},{25,9},{2,18},{10... | collective-permute-start | bytes 442376 | tf_op jit(solution)/shard_map/ppermute | solution.py:795
  150.4 9.3 %collective-permute-start.34 = (bf16[576,128]{1,0:T(8,128)(2,1)S(1)}, bf16[576,128]{1,0:T(8,128)(2,1)S(1)}, u32[]{:S(2)}, u32[]{:S(2)}) collective-permute-start(bf16[576,128]{1,0:T(8,128)(2,1)S(1)} %get-tuple-element.137), channel_id=1, source_target_pairs={{0,8},{8,0},{16,24},{24,16},{1,9},{9,1},{17,25},{25,17},{2,10},{10... | collective-permute-start | bytes 442376 | tf_op jit(solution)/shard_map/ppermute | solution.py:795
  150.9 8.8 %collective-permute-start.39 = (bf16[352,128]{1,0:T(8,128)(2,1)S(1)}, bf16[352,128]{1,0:T(8,128)(2,1)S(1)}, u32[]{:S(2)}, u32[]{:S(2)}) collective-permute-start(bf16[352,128]{1,0:T(8,128)(2,1)S(1)} %get-tuple-element.141), channel_id=1, source_target_pairs={{0,24},{8,16},{16,8},{24,0},{1,25},{9,17},{17,9},{25,1},{2,26},{10... | collective-permute-start | bytes 270344 | tf_op jit(solution)/shard_map/ppermute | solution.py:795
  153.3 8.1 %collective-permute-start.38 = (bf16[352,128]{1,0:T(8,128)(2,1)S(1)}, bf16[352,128]{1,0:T(8,128)(2,1)S(1)}, u32[]{:S(2)}, u32[]{:S(2)}) collective-permute-start(bf16[352,128]{1,0:T(8,128)(2,1)S(1)} %get-tuple-element.142), channel_id=1, source_target_pairs={{0,16},{8,24},{16,0},{24,8},{1,17},{9,25},{17,1},{25,9},{2,18},{10... | collective-permute-start | bytes 270344 | tf_op jit(solution)/shard_map/ppermute | solution.py:795
  154.2 7.2 %collective-permute-start.37 = (bf16[352,128]{1,0:T(8,128)(2,1)S(1)}, bf16[352,128]{1,0:T(8,128)(2,1)S(1)}, u32[]{:S(2)}, u32[]{:S(2)}) collective-permute-start(bf16[352,128]{1,0:T(8,128)(2,1)S(1)} %get-tuple-element.143), channel_id=1, source_target_pairs={{0,8},{8,0},{16,24},{24,16},{1,9},{9,1},{17,25},{25,17},{2,10},{10... | collective-permute-start | bytes 270344 | tf_op jit(solution)/shard_map/ppermute | solution.py:795
  (33 other events, 184.8 us)

commit v6 on v5

--- a/solution.py
+++ b/solution.py
@@ -556,8 +556,6 @@
             m.start()
         for ref in (gq, gb, gt):
             ref[...] = jnp.zeros_like(ref)
-        for m in copies_a(geo, bufs, me, wq, sem):
-            m.wait()
 
     def window(g, carry):
         rows = pl.ds(pl.multiple_of(g * TP, 16), TP)
@@ -603,6 +601,8 @@
 
     @pl.when(i == n - 1)
     def _():
+        for m in copies_a(geo, bufs, me, wq, sem):
+            m.wait()
         sums = gb[...]
         g_col = jnp.broadcast_to(vec[0:1, :], (TL, D)).T
         s_col = jnp.broadcast_to(vec[1:2, :], (TL, D)).T

time: 163 us -> 163 us (level)
  no operation moved by 1% of the time
where the time goes in v6:
time: 163 us
  Pallas kernels  95.5 us (59%)
  starting transfers between devices  40.6 us (25%)
  local copies, waits for them, and re-layouts  16.3 us (10%)
  waiting for transfers between devices  7.27 us (4%)
  between operations  1.67 us (1%)
    ppermute x40, starting transfers between devices, swap(): return lax.ppermute(x, axis, [(i, i ^ d) for i in range(size)])  40.6 us
    pallas_call x1, Pallas kernels, mlp(): pl.pallas_call(functools.partial(mlp_body, geo, G, FC), grid=(B // G,), i...  40.1 us
    pallas_call x1, Pallas kernels, attn_bwd(): pl.pallas_call(functools.partial(attn_bwd_body, geo, G), grid=(B // G,),...  23.7 us
    pallas_call x1, Pallas kernels, attn_fwd(): pl.pallas_call(functools.partial(attn_fwd_body, geo, G, vec is not None),...  18.7 us
    unnamed x38, local copies, waits for them, and re-layouts  16.2 us
    pallas_call x1, Pallas kernels, input_bwd(): pl.pallas_call(functools.partial(input_bwd_body, geo, G), grid=(B // G,),...  7.41 us
    ppermute x40, waiting for transfers between devices, swap(): return lax.ppermute(x, axis, [(i, i ^ d) for i in range(size)])  7.27 us
  transfers between devices with their start and end apart: 40, of which 10 were waited for; matrix products, arithmetic and copies ran while one was open for 5% of the time, Pallas kernels for 32%

profile of v6, /device:TPU:0, one launch (start us, length us, event | category | flops | bytes accessed | tf_op | source)
XLA Modules:
  0.0 162.8 jit_solution(5267386352673785488)
XLA Ops:
  0.6 1.5 pack.2
  2.2 5.1 %collective-permute-start.2 = (bf16[224,128]{1,0:T(8,128)(2,1)}, bf16[224,128]{1,0:T(8,128)(2,1)S(1)}, u32[]{:S(2)}, u32[]{:S(2)}) collective-permute-start(bf16[224,128]{1,0:T(8,128)(2,1)} %pack.2), channel_id=1, source_target_pairs={{0,24},{8,16},{16,8},{24,0},{1,25},{9,17},{17,9},{25,1},{2,26},{10... | collective-permute-start | bytes 172040 | tf_op jit(solution)/shard_map/ppermute | solution.py:795
  7.9 1.6 pack.3
  9.5 3.8 %collective-permute-start.12 = (bf16[9,64,128]{2,1,0:T(8,128)(2,1)}, bf16[9,64,128]{2,1,0:T(8,128)(2,1)S(1)}, u32[]{:S(2)}, u32[]{:S(2)}) collective-permute-start(bf16[9,64,128]{2,1,0:T(8,128)(2,1)} %pack.3), channel_id=1, source_target_pairs={{0,24},{8,16},{16,8},{24,0},{1,25},{9,17},{17,9},{25,1},{2,26},{10... | collective-permute-start | bytes 442376 | tf_op jit(solution)/shard_map/ppermute | solution.py:795
  14.1 2.7 %collective-permute-start.8 = (bf16[4,224,128]{2,1,0:T(8,128)(2,1)S(1)}, bf16[4,224,128]{2,1,0:T(8,128)(2,1)S(1)}, u32[]{:S(2)}, u32[]{:S(2)}) collective-permute-start(bf16[4,224,128]{2,1,0:T(8,128)(2,1)S(1)} %pad_maximum_fusion.1.refs_3_.refs_11_.refs_5_), channel_id=1, source_target_pairs={{0,6},{1,7},{2,4},{3,5},{4,2},{5,3},{6,0},{7,1},{8,14},{9,15},{10,... | collective-permute-start | bytes 688136 | tf_op jit(solution)/shard_map/ppermute | solution.py:795
  18.5 1.6 %collective-permute-start.4 = (bf16[4,224,128]{2,1,0:T(8,128)(2,1)S(1)}, bf16[4,224,128]{2,1,0:T(8,128)(2,1)S(1)}, u32[]{:S(2)}, u32[]{:S(2)}) collective-permute-start(bf16[4,224,128]{2,1,0:T(8,128)(2,1)S(1)} %pad_maximum_fusion.1.refs_3_.refs_11_.refs_5_), channel_id=1, source_target_pairs={{0,2},{1,3},{2,0},{3,1},{4,6},{5,7},{6,4},{7,5},{8,10},{9,11},{10,... | collective-permute-start | bytes 688136 | tf_op jit(solution)/shard_map/ppermute | solution.py:795
  22.2 2.4 %copy.21.refs_1_.refs_2_ = bf16[16,100,512]{2,1,0:T(8,128)(2,1)S(1)} copy(bf16[16,100,512]{2,0,1:T(8,128)(2,1)} %param.11) | data formatting | bytes 3276800 | tf_op args[0]
  26.6 2.3 %collective-permute-start.16 = (bf16[4,9,64,128]{3,2,1,0:T(8,128)(2,1)S(1)}, bf16[4,9,64,128]{3,2,1,0:T(8,128)(2,1)S(1)}, u32[]{:S(2)}, u32[]{:S(2)}) collective-permute-start(bf16[4,9,64,128]{3,2,1,0:T(8,128)(2,1)S(1)} %pad_maximum_fusion.refs_5_), channel_id=1, source_target_pairs={{0,6},{1,7},{2,4},{3,5},{4,2},{5,3},{6,0},{7,1},{8,14},{9,15},{10,... | collective-permute-start | bytes 1769480 | tf_op jit(solution)/shard_map/ppermute | solution.py:795
  30.2 18.7 %attn_fwd.1 = (bf16[1792,512]{1,0:T(8,128)(2,1)S(1)}, bf16[1792,512]{1,0:T(8,128)(2,1)S(1)}, bf16[1792,512]{1,0:T(8,128)(2,1)S(1)}, bf16[1792,512]{1,0:T(8,128)(...) custom-call(s32[2]{0:T(128)S(1)} %pad_add_fusion.refs_0_, ...), custom_call_target="tpu_custom_call" | custom-call | flops 32999999488 | bytes 30000000 | tf_op jit(solution)/shard_map/attn_fwd/pallas_call | solution.py:348
  48.9 2.9 %copy-done.4 = bf16[16,4,112,512]{3,2,1,0:T(8,128)(2,1)} copy-done((bf16[16,4,112,512]{3,2,1,0:T(8,128)(2,1)}, bf16[16,4,112,512]{3,2,1,0:T(8,128)(2,1)S(1)}, u32[]{:S(2)}) %copy-start.4) | copy-done | bytes 7340056
  59.4 40.1 %mlp.1 = (bf16[16,100,512]{2,1,0:T(8,128)(2,1)S(1)}, f32[1792,512]{1,0:T(8,128)}, bf16[1792,512]{1,0:T(8,128)(2,1)}, f32[8,512]{1,0:T(8,128)S(1)}, f32[1,2048]{1...) custom-call(s32[2]{0:T(128)S(1)} %pad_add_fusion.refs_0_, ...), custom_call_target="tpu_custom_call" | custom-call | flops 48399998976 | bytes 44000000 | tf_op jit(solution)/shard_map/mlp/pallas_call | solution.py:514
  101.8 1.6 collective-permute-start.24
  103.5 1.5 collective-permute-start.25
  106.5 1.5 copy-done.11
  108.0 23.7 %attn_bwd.1 = (bf16[1792,1536]{1,0:T(8,128)(2,1)S(1)}, f32[24,512]{1,0:T(8,128)}, bf16[4,224,128]{2,1,0:T(8,128)(2,1)S(1)}, bf16[4,224,128]{2,1,0:T(8,128)(2,1)S...) custom-call(s32[2]{0:T(128)S(1)} %pad_add_fusion.refs_0_, ...), custom_call_target="tpu_custom_call" | custom-call | flops 32999999488 | bytes 30000000 | tf_op jit(solution)/shard_map/attn_bwd/pallas_call | solution.py:659
  133.2 3.3 %collective-permute-start.36 = (bf16[576,128]{1,0:T(8,128)(2,1)S(1)}, bf16[576,128]{1,0:T(8,128)(2,1)S(1)}, u32[]{:S(2)}, u32[]{:S(2)}) collective-permute-start(bf16[576,128]{1,0:T(8,128)(2,1)S(1)} %slice_bitcast_fusion), channel_id=1, source_target_pairs={{0,24},{8,16},{16,8},{24,0},{1,25},{9,17},{17,9},{25,1},{2,26},{10... | collective-permute-start | bytes 442376 | tf_op jit(solution)/shard_map/ppermute | solution.py:795
  139.0 1.4 collective-permute-start.33
  140.5 2.5 %collective-permute-start.35 = (bf16[576,128]{1,0:T(8,128)(2,1)S(1)}, bf16[576,128]{1,0:T(8,128)(2,1)S(1)}, u32[]{:S(2)}, u32[]{:S(2)}) collective-permute-start(bf16[576,128]{1,0:T(8,128)(2,1)S(1)} %get-tuple-element.136), channel_id=1, source_target_pairs={{0,16},{8,24},{16,0},{24,8},{1,17},{9,25},{17,1},{25,9},{2,18},{10... | collective-permute-start | bytes 442376 | tf_op jit(solution)/shard_map/ppermute | solution.py:795
  143.0 7.4 %input_bwd.1 = bf16[16,100,512]{2,1,0:T(8,128)(2,1)S(1)} custom-call(s32[2]{0:T(128)S(1)} %pad_add_fusion.refs_0_, bf16[16,100,512]{2,1,0:T(8,128)(2,1)S(1)} %copy.21.refs_1_.refs_2_, bf16[1792,1536]{1,0:T(8,128)(2,1)S(1)} %get-tuple-element.92.refs_2_, f32[1792,512]{1,0:T(8,128)S(1)} %copy-done.1, f32[8,512]{1,0:T(8,128)S(1)} %get-tuple-element.110.refs_13_.refs_7_.refs_4_, ...), custom_call_target="tpu_custom_call" | custom-call | flops 11000000512 | bytes 10000000 | tf_op jit(solution)/shard_map/input_bwd/pallas_call | solution.py:712
  150.9 2.4 %collective-permute-start.39 = (bf16[352,128]{1,0:T(8,128)(2,1)S(1)}, bf16[352,128]{1,0:T(8,128)(2,1)S(1)}, u32[]{:S(2)}, u32[]{:S(2)}) collective-permute-start(bf16[352,128]{1,0:T(8,128)(2,1)S(1)} %get-tuple-element.141), channel_id=1, source_target_pairs={{0,24},{8,16},{16,8},{24,0},{1,25},{9,17},{17,9},{25,1},{2,26},{10... | collective-permute-start | bytes 270344 | tf_op jit(solution)/shard_map/ppermute | solution.py:795
  155.4 1.7 %copy.24 = bf16[16,100,512]{2,0,1:T(8,128)(2,1)} copy(bf16[16,100,512]{2,1,0:T(8,128)(2,1)S(1)} %get-tuple-element.127) | data formatting | bytes 3276800
  157.1 1.7 %copy.25 = bf16[16,100,512]{2,0,1:T(8,128)(2,1)} copy(bf16[16,100,512]{2,1,0:T(8,128)(2,1)S(1)} %input_bwd.1) | data formatting | bytes 3276800
  159.8 1.7 %collective-permute-done.38.refs_7_ = bf16[352,128]{1,0:T(8,128)(2,1)S(1)} collective-permute-done((bf16[352,128]{1,0:T(8,128)(2,1)S(1)}, bf16[352,128]{1,0:T(8,128)(2,1)S(1)}, u32[]{:S(2)}, u32[]{:S(2)}) %collective-permute-start.38) | collective-permute-done | bytes 90144 | tf_op jit(solution)/shard_map/ppermute | solution.py:795
  161.4 1.4 finish.1
  (121 shorter events, 26.8 us)
Async XLA Ops:
  2.2 11.2 %collective-permute-start.2 = (bf16[224,128]{1,0:T(8,128)(2,1)}, bf16[224,128]{1,0:T(8,128)(2,1)S(1)}, u32[]{:S(2)}, u32[]{:S(2)}) collective-permute-start(bf16[224,128]{1,0:T(8,128)(2,1)} %pack.2), channel_id=1, source_target_pairs={{0,24},{8,16},{16,8},{24,0},{1,25},{9,17},{17,9},{25,1},{2,26},{10... | collective-permute-start | bytes 172040 | tf_op jit(solution)/shard_map/ppermute | solution.py:795
  9.5 9.0 %collective-permute-start.12 = (bf16[9,64,128]{2,1,0:T(8,128)(2,1)}, bf16[9,64,128]{2,1,0:T(8,128)(2,1)S(1)}, u32[]{:S(2)}, u32[]{:S(2)}) collective-permute-start(bf16[9,64,128]{2,1,0:T(8,128)(2,1)} %pack.3), channel_id=1, source_target_pairs={{0,24},{8,16},{16,8},{24,0},{1,25},{9,17},{17,9},{25,1},{2,26},{10... | collective-permute-start | bytes 442376 | tf_op jit(solution)/shard_map/ppermute | solution.py:795
  13.3 11.9 %collective-permute-start.11 = (bf16[9,64,128]{2,1,0:T(8,128)(2,1)}, bf16[9,64,128]{2,1,0:T(8,128)(2,1)S(1)}, u32[]{:S(2)}, u32[]{:S(2)}) collective-permute-start(bf16[9,64,128]{2,1,0:T(8,128)(2,1)} %pack.3), channel_id=1, source_target_pairs={{0,16},{8,24},{16,0},{24,8},{1,17},{9,25},{17,1},{25,9},{2,18},{10... | collective-permute-start | bytes 442376 | tf_op jit(solution)/shard_map/ppermute | solution.py:795
  13.4 13.2 %collective-permute-start.10 = (bf16[9,64,128]{2,1,0:T(8,128)(2,1)}, bf16[9,64,128]{2,1,0:T(8,128)(2,1)S(1)}, u32[]{:S(2)}, u32[]{:S(2)}) collective-permute-start(bf16[9,64,128]{2,1,0:T(8,128)(2,1)} %pack.3), channel_id=1, source_target_pairs={{0,8},{8,0},{16,24},{24,16},{1,9},{9,1},{17,25},{25,17},{2,10},{10... | collective-permute-start | bytes 442376 | tf_op jit(solution)/shard_map/ppermute | solution.py:795
  14.1 11.1 %collective-permute-start.8 = (bf16[4,224,128]{2,1,0:T(8,128)(2,1)S(1)}, bf16[4,224,128]{2,1,0:T(8,128)(2,1)S(1)}, u32[]{:S(2)}, u32[]{:S(2)}) collective-permute-start(bf16[4,224,128]{2,1,0:T(8,128)(2,1)S(1)} %pad_maximum_fusion.1.refs_3_.refs_11_.refs_5_), channel_id=1, source_target_pairs={{0,6},{1,7},{2,4},{3,5},{4,2},{5,3},{6,0},{7,1},{8,14},{9,15},{10,... | collective-permute-start | bytes 688136 | tf_op jit(solution)/shard_map/ppermute | solution.py:795
  16.8 9.2 %collective-permute-start.6 = (bf16[4,224,128]{2,1,0:T(8,128)(2,1)S(1)}, bf16[4,224,128]{2,1,0:T(8,128)(2,1)S(1)}, u32[]{:S(2)}, u32[]{:S(2)}) collective-permute-start(bf16[4,224,128]{2,1,0:T(8,128)(2,1)S(1)} %pad_maximum_fusion.1.refs_3_.refs_11_.refs_5_), channel_id=1, source_target_pairs={{0,4},{1,5},{2,6},{3,7},{4,0},{5,1},{6,2},{7,3},{8,12},{9,13},{10,... | collective-permute-start | bytes 688136 | tf_op jit(solution)/shard_map/ppermute | solution.py:795
  18.5 7.7 %collective-permute-start.4 = (bf16[4,224,128]{2,1,0:T(8,128)(2,1)S(1)}, bf16[4,224,128]{2,1,0:T(8,128)(2,1)S(1)}, u32[]{:S(2)}, u32[]{:S(2)}) collective-permute-start(bf16[4,224,128]{2,1,0:T(8,128)(2,1)S(1)} %pad_maximum_fusion.1.refs_3_.refs_11_.refs_5_), channel_id=1, source_target_pairs={{0,2},{1,3},{2,0},{3,1},{4,6},{5,7},{6,4},{7,5},{8,10},{9,11},{10,... | collective-permute-start | bytes 688136 | tf_op jit(solution)/shard_map/ppermute | solution.py:795
  26.6 29.0 %collective-permute-start.16 = (bf16[4,9,64,128]{3,2,1,0:T(8,128)(2,1)S(1)}, bf16[4,9,64,128]{3,2,1,0:T(8,128)(2,1)S(1)}, u32[]{:S(2)}, u32[]{:S(2)}) collective-permute-start(bf16[4,9,64,128]{3,2,1,0:T(8,128)(2,1)S(1)} %pad_maximum_fusion.refs_5_), channel_id=1, source_target_pairs={{0,6},{1,7},{2,4},{3,5},{4,2},{5,3},{6,0},{7,1},{8,14},{9,15},{10,... | collective-permute-start | bytes 1769480 | tf_op jit(solution)/shard_map/ppermute | solution.py:795
  28.9 26.7 %collective-permute-start.15 = (bf16[4,9,64,128]{3,2,1,0:T(8,128)(2,1)S(1)}, bf16[4,9,64,128]{3,2,1,0:T(8,128)(2,1)S(1)}, u32[]{:S(2)}, u32[]{:S(2)}) collective-permute-start(bf16[4,9,64,128]{3,2,1,0:T(8,128)(2,1)S(1)} %pad_maximum_fusion.refs_5_), channel_id=1, source_target_pairs={{0,4},{1,5},{2,6},{3,7},{4,0},{5,1},{6,2},{7,3},{8,12},{9,13},{10,... | collective-permute-start | bytes 1769480 | tf_op jit(solution)/shard_map/ppermute | solution.py:795
  29.6 26.0 %collective-permute-start.14 = (bf16[4,9,64,128]{3,2,1,0:T(8,128)(2,1)S(1)}, bf16[4,9,64,128]{3,2,1,0:T(8,128)(2,1)S(1)}, u32[]{:S(2)}, u32[]{:S(2)}) collective-permute-start(bf16[4,9,64,128]{3,2,1,0:T(8,128)(2,1)S(1)} %pad_maximum_fusion.refs_5_), channel_id=1, source_target_pairs={{0,2},{1,3},{2,0},{3,1},{4,6},{5,7},{6,4},{7,5},{8,10},{9,11},{10,... | collective-permute-start | bytes 1769480 | tf_op jit(solution)/shard_map/ppermute | solution.py:795
  30.2 28.0 %collective-permute-start.13 = (bf16[4,9,64,128]{3,2,1,0:T(8,128)(2,1)S(1)}, bf16[4,9,64,128]{3,2,1,0:T(8,128)(2,1)S(1)}, u32[]{:S(2)}, u32[]{:S(2)}) collective-permute-start(bf16[4,9,64,128]{3,2,1,0:T(8,128)(2,1)S(1)} %pad_maximum_fusion.refs_5_), channel_id=1, source_target_pairs={{0,1},{1,0},{2,3},{3,2},{4,5},{5,4},{6,7},{7,6},{8,9},{9,8},{10,11... | collective-permute-start | bytes 1769480 | tf_op jit(solution)/shard_map/ppermute | solution.py:795
  101.8 29.9 %collective-permute-start.24 = (bf16[4,576,128]{2,1,0:T(8,128)(2,1)S(1)}, bf16[4,576,128]{2,1,0:T(8,128)(2,1)S(1)}, u32[]{:S(2)}, u32[]{:S(2)}) collective-permute-start(bf16[4,576,128]{2,1,0:T(8,128)(2,1)S(1)} %add_convert_fusion.3), channel_id=1, source_target_pairs={{0,2},{1,3},{2,0},{3,1},{4,6},{5,7},{6,4},{7,5},{8,10},{9,11},{10,... | collective-permute-start | bytes 1769480 | tf_op jit(solution)/shard_map/ppermute | solution.py:795
  103.5 28.2 %collective-permute-start.25 = (bf16[4,576,128]{2,1,0:T(8,128)(2,1)S(1)}, bf16[4,576,128]{2,1,0:T(8,128)(2,1)S(1)}, u32[]{:S(2)}, u32[]{:S(2)}) collective-permute-start(bf16[4,576,128]{2,1,0:T(8,128)(2,1)S(1)} %add_convert_fusion.2), channel_id=1, source_target_pairs={{0,4},{1,5},{2,6},{3,7},{4,0},{5,1},{6,2},{7,3},{8,12},{9,13},{10,... | collective-permute-start | bytes 1769480 | tf_op jit(solution)/shard_map/ppermute | solution.py:795
  105.1 26.6 %collective-permute-start.26 = (bf16[4,576,128]{2,1,0:T(8,128)(2,1)S(1)}, bf16[4,576,128]{2,1,0:T(8,128)(2,1)S(1)}, u32[]{:S(2)}, u32[]{:S(2)}) collective-permute-start(bf16[4,576,128]{2,1,0:T(8,128)(2,1)S(1)} %add_convert_fusion.1), channel_id=1, source_target_pairs={{0,6},{1,7},{2,4},{3,5},{4,2},{5,3},{6,0},{7,1},{8,14},{9,15},{10,... | collective-permute-start | bytes 1769480 | tf_op jit(solution)/shard_map/ppermute | solution.py:795
  131.8 8.6 %collective-permute-start.27 = (bf16[4,224,128]{2,1,0:T(8,128)(2,1)S(1)}, bf16[4,224,128]{2,1,0:T(8,128)(2,1)S(1)}, u32[]{:S(2)}, u32[]{:S(2)}) collective-permute-start(bf16[4,224,128]{2,1,0:T(8,128)(2,1)S(1)} %get-tuple-element.103), channel_id=1, source_target_pairs={{0,1},{1,0},{2,3},{3,2},{4,5},{5,4},{6,7},{7,6},{8,9},{9,8},{10,11... | collective-permute-start | bytes 688136 | tf_op jit(solution)/shard_map/ppermute | solution.py:795
  133.2 21.1 %collective-permute-start.36 = (bf16[576,128]{1,0:T(8,128)(2,1)S(1)}, bf16[576,128]{1,0:T(8,128)(2,1)S(1)}, u32[]{:S(2)}, u32[]{:S(2)}) collective-permute-start(bf16[576,128]{1,0:T(8,128)(2,1)S(1)} %slice_bitcast_fusion), channel_id=1, source_target_pairs={{0,24},{8,16},{16,8},{24,0},{1,25},{9,17},{17,9},{25,1},{2,26},{10... | collective-permute-start | bytes 442376 | tf_op jit(solution)/shard_map/ppermute | solution.py:795
  136.6 13.9 %collective-permute-start.31 = (bf16[4,224,128]{2,1,0:T(8,128)(2,1)S(1)}, bf16[4,224,128]{2,1,0:T(8,128)(2,1)S(1)}, u32[]{:S(2)}, u32[]{:S(2)}) collective-permute-start(bf16[4,224,128]{2,1,0:T(8,128)(2,1)S(1)} %add_convert_fusion.8), channel_id=1, source_target_pairs={{0,2},{1,3},{2,0},{3,1},{4,6},{5,7},{6,4},{7,5},{8,10},{9,11},{10,... | collective-permute-start | bytes 688136 | tf_op jit(solution)/shard_map/ppermute | solution.py:795
  138.0 12.7 %collective-permute-start.32 = (bf16[4,224,128]{2,1,0:T(8,128)(2,1)S(1)}, bf16[4,224,128]{2,1,0:T(8,128)(2,1)S(1)}, u32[]{:S(2)}, u32[]{:S(2)}) collective-permute-start(bf16[4,224,128]{2,1,0:T(8,128)(2,1)S(1)} %add_convert_fusion.7), channel_id=1, source_target_pairs={{0,4},{1,5},{2,6},{3,7},{4,0},{5,1},{6,2},{7,3},{8,12},{9,13},{10,... | collective-permute-start | bytes 688136 | tf_op jit(solution)/shard_map/ppermute | solution.py:795
  139.0 11.8 %collective-permute-start.33 = (bf16[4,224,128]{2,1,0:T(8,128)(2,1)S(1)}, bf16[4,224,128]{2,1,0:T(8,128)(2,1)S(1)}, u32[]{:S(2)}, u32[]{:S(2)}) collective-permute-start(bf16[4,224,128]{2,1,0:T(8,128)(2,1)S(1)} %add_convert_fusion.6), channel_id=1, source_target_pairs={{0,6},{1,7},{2,4},{3,5},{4,2},{5,3},{6,0},{7,1},{8,14},{9,15},{10,... | collective-permute-start | bytes 688136 | tf_op jit(solution)/shard_map/ppermute | solution.py:795
  140.5 18.3 %collective-permute-start.35 = (bf16[576,128]{1,0:T(8,128)(2,1)S(1)}, bf16[576,128]{1,0:T(8,128)(2,1)S(1)}, u32[]{:S(2)}, u32[]{:S(2)}) collective-permute-start(bf16[576,128]{1,0:T(8,128)(2,1)S(1)} %get-tuple-element.136), channel_id=1, source_target_pairs={{0,16},{8,24},{16,0},{24,8},{1,17},{9,25},{17,1},{25,9},{2,18},{10... | collective-permute-start | bytes 442376 | tf_op jit(solution)/shard_map/ppermute | solution.py:795
  150.4 9.3 %collective-permute-start.34 = (bf16[576,128]{1,0:T(8,128)(2,1)S(1)}, bf16[576,128]{1,0:T(8,128)(2,1)S(1)}, u32[]{:S(2)}, u32[]{:S(2)}) collective-permute-start(bf16[576,128]{1,0:T(8,128)(2,1)S(1)} %get-tuple-element.137), channel_id=1, source_target_pairs={{0,8},{8,0},{16,24},{24,16},{1,9},{9,1},{17,25},{25,17},{2,10},{10... | collective-permute-start | bytes 442376 | tf_op jit(solution)/shard_map/ppermute | solution.py:795
  150.9 8.8 %collective-permute-start.39 = (bf16[352,128]{1,0:T(8,128)(2,1)S(1)}, bf16[352,128]{1,0:T(8,128)(2,1)S(1)}, u32[]{:S(2)}, u32[]{:S(2)}) collective-permute-start(bf16[352,128]{1,0:T(8,128)(2,1)S(1)} %get-tuple-element.141), channel_id=1, source_target_pairs={{0,24},{8,16},{16,8},{24,0},{1,25},{9,17},{17,9},{25,1},{2,26},{10... | collective-permute-start | bytes 270344 | tf_op jit(solution)/shard_map/ppermute | solution.py:795
  153.3 8.1 %collective-permute-start.38 = (bf16[352,128]{1,0:T(8,128)(2,1)S(1)}, bf16[352,128]{1,0:T(8,128)(2,1)S(1)}, u32[]{:S(2)}, u32[]{:S(2)}) collective-permute-start(bf16[352,128]{1,0:T(8,128)(2,1)S(1)} %get-tuple-element.142), channel_id=1, source_target_pairs={{0,16},{8,24},{16,0},{24,8},{1,17},{9,25},{17,1},{25,9},{2,18},{10... | collective-permute-start | bytes 270344 | tf_op jit(solution)/shard_map/ppermute | solution.py:795
  154.3 7.2 %collective-permute-start.37 = (bf16[352,128]{1,0:T(8,128)(2,1)S(1)}, bf16[352,128]{1,0:T(8,128)(2,1)S(1)}, u32[]{:S(2)}, u32[]{:S(2)}) collective-permute-start(bf16[352,128]{1,0:T(8,128)(2,1)S(1)} %get-tuple-element.143), channel_id=1, source_target_pairs={{0,8},{8,0},{16,24},{24,16},{1,9},{9,1},{17,25},{25,17},{2,10},{10... | collective-permute-start | bytes 270344 | tf_op jit(solution)/shard_map/ppermute | solution.py:795
  (33 other events, 184.8 us)

commit v7 on v6

--- a/solution.py
+++ b/solution.py
@@ -533,7 +533,7 @@
             V((NG, FF // geo.r, geo.r, TL), bf16),
             pltpu.SemaphoreType.DMA,
         ],
-        compiler_params=params(40),
+        compiler_params=params(44),
         cost_estimate=cost(44),
         name="mlp",
     )(me, live, tok, cot, attn, *bufs, vec, b1)

time: 163 us -> 163 us (level)
  local copies, waits for them, and re-layouts: 16.3 us -> 14.3 us
  waiting for transfers between devices: 7.27 us -> 9.18 us
    unnamed x38 -> x40, local copies, waits for them, and re-layouts: 16.2 us -> 14.2 us
    ppermute x40, waiting for transfers between devices: 7.27 us -> 9.18 us  [swap(): return lax.ppermute(x, axis, [(i, i ^ d) for i in range(size)])]
  transfers between devices with their start and end apart: 40 -> 40, of which waited for: 10 -> 10; matrix products, arithmetic and copies ran while one was open for 5% -> 6% of each run, Pallas kernels for 32% -> 32%
where the time goes in v7:
time: 163 us
  Pallas kernels  96.1 us (59%)
  starting transfers between devices  40 us (25%)
  local copies, waits for them, and re-layouts  14.3 us (9%)
  waiting for transfers between devices  9.18 us (6%)
  between operations  1.67 us (1%)
    pallas_call x1, Pallas kernels, mlp(): pl.pallas_call(functools.partial(mlp_body, geo, G, FC), grid=(B // G,), i...  40.5 us
    ppermute x40, starting transfers between devices, swap(): return lax.ppermute(x, axis, [(i, i ^ d) for i in range(size)])  40 us
    pallas_call x1, Pallas kernels, attn_bwd(): pl.pallas_call(functools.partial(attn_bwd_body, geo, G), grid=(B // G,),...  24 us
    pallas_call x1, Pallas kernels, attn_fwd(): pl.pallas_call(functools.partial(attn_fwd_body, geo, G, vec is not None),...  18.7 us
    unnamed x40, local copies, waits for them, and re-layouts  14.2 us
    ppermute x40, waiting for transfers between devices, swap(): return lax.ppermute(x, axis, [(i, i ^ d) for i in range(size)])  9.18 us
    pallas_call x1, Pallas kernels, input_bwd(): pl.pallas_call(functools.partial(input_bwd_body, geo, G), grid=(B // G,),...  7.4 us
  transfers between devices with their start and end apart: 40, of which 10 were waited for; matrix products, arithmetic and copies ran while one was open for 6% of the time, Pallas kernels for 32%

profile of v7, /device:TPU:0, one launch (start us, length us, event | category | flops | bytes accessed | tf_op | source)
XLA Modules:
  0.0 162.8 jit_solution(11987589335208214115)
XLA Ops:
  0.6 1.5 pack.2
  2.2 5.1 %collective-permute-start.2 = (bf16[224,128]{1,0:T(8,128)(2,1)}, bf16[224,128]{1,0:T(8,128)(2,1)S(1)}, u32[]{:S(2)}, u32[]{:S(2)}) collective-permute-start(bf16[224,128]{1,0:T(8,128)(2,1)} %pack.2), channel_id=1, source_target_pairs={{0,24},{8,16},{16,8},{24,0},{1,25},{9,17},{17,9},{25,1},{2,26},{10... | collective-permute-start | bytes 172040 | tf_op jit(solution)/shard_map/ppermute | solution.py:795
  7.9 1.6 pack.3
  9.5 3.8 %collective-permute-start.12 = (bf16[9,64,128]{2,1,0:T(8,128)(2,1)}, bf16[9,64,128]{2,1,0:T(8,128)(2,1)S(1)}, u32[]{:S(2)}, u32[]{:S(2)}) collective-permute-start(bf16[9,64,128]{2,1,0:T(8,128)(2,1)} %pack.3), channel_id=1, source_target_pairs={{0,24},{8,16},{16,8},{24,0},{1,25},{9,17},{17,9},{25,1},{2,26},{10... | collective-permute-start | bytes 442376 | tf_op jit(solution)/shard_map/ppermute | solution.py:795
  14.1 2.7 %collective-permute-start.8 = (bf16[4,224,128]{2,1,0:T(8,128)(2,1)S(1)}, bf16[4,224,128]{2,1,0:T(8,128)(2,1)S(1)}, u32[]{:S(2)}, u32[]{:S(2)}) collective-permute-start(bf16[4,224,128]{2,1,0:T(8,128)(2,1)S(1)} %pad_maximum_fusion.1.refs_3_.refs_11_.refs_5_), channel_id=1, source_target_pairs={{0,6},{1,7},{2,4},{3,5},{4,2},{5,3},{6,0},{7,1},{8,14},{9,15},{10,... | collective-permute-start | bytes 688136 | tf_op jit(solution)/shard_map/ppermute | solution.py:795
  18.5 1.6 %collective-permute-start.4 = (bf16[4,224,128]{2,1,0:T(8,128)(2,1)S(1)}, bf16[4,224,128]{2,1,0:T(8,128)(2,1)S(1)}, u32[]{:S(2)}, u32[]{:S(2)}) collective-permute-start(bf16[4,224,128]{2,1,0:T(8,128)(2,1)S(1)} %pad_maximum_fusion.1.refs_3_.refs_11_.refs_5_), channel_id=1, source_target_pairs={{0,2},{1,3},{2,0},{3,1},{4,6},{5,7},{6,4},{7,5},{8,10},{9,11},{10,... | collective-permute-start | bytes 688136 | tf_op jit(solution)/shard_map/ppermute | solution.py:795
  22.2 2.4 %copy.21.refs_1_.refs_2_ = bf16[16,100,512]{2,1,0:T(8,128)(2,1)S(1)} copy(bf16[16,100,512]{2,0,1:T(8,128)(2,1)} %param.11) | data formatting | bytes 3276800 | tf_op args[0]
  26.6 2.3 %collective-permute-start.16 = (bf16[4,9,64,128]{3,2,1,0:T(8,128)(2,1)S(1)}, bf16[4,9,64,128]{3,2,1,0:T(8,128)(2,1)S(1)}, u32[]{:S(2)}, u32[]{:S(2)}) collective-permute-start(bf16[4,9,64,128]{3,2,1,0:T(8,128)(2,1)S(1)} %pad_maximum_fusion.refs_5_), channel_id=1, source_target_pairs={{0,6},{1,7},{2,4},{3,5},{4,2},{5,3},{6,0},{7,1},{8,14},{9,15},{10,... | collective-permute-start | bytes 1769480 | tf_op jit(solution)/shard_map/ppermute | solution.py:795
  30.2 18.7 %attn_fwd.1 = (bf16[1792,512]{1,0:T(8,128)(2,1)S(1)}, bf16[1792,512]{1,0:T(8,128)(2,1)S(1)}, bf16[1792,512]{1,0:T(8,128)(2,1)S(1)}, bf16[1792,512]{1,0:T(8,128)(...) custom-call(s32[2]{0:T(128)S(1)} %pad_add_fusion.refs_0_, ...), custom_call_target="tpu_custom_call" | custom-call | flops 32999999488 | bytes 30000000 | tf_op jit(solution)/shard_map/attn_fwd/pallas_call | solution.py:348
  48.9 2.9 %copy-done.6 = bf16[16,4,112,512]{3,2,1,0:T(8,128)(2,1)} copy-done((bf16[16,4,112,512]{3,2,1,0:T(8,128)(2,1)}, bf16[16,4,112,512]{3,2,1,0:T(8,128)(2,1)S(1)}, u32[]{:S(2)}) %copy-start.6) | copy-done | bytes 7340056
  54.2 1.4 collective-permute-done.15.refs_9_
  56.9 2.1 %copy.22.refs_3_ = bf16[16,100,512]{2,1,0:T(8,128)(2,1)} copy(bf16[16,100,512]{2,0,1:T(8,128)(2,1)S(1)} %copy-done.14) | data formatting | bytes 3276800 | tf_op args[9]
  59.4 40.5 %mlp.1 = (bf16[16,100,512]{2,1,0:T(8,128)(2,1)}, f32[1792,512]{1,0:T(8,128)}, bf16[1792,512]{1,0:T(8,128)(2,1)}, f32[8,512]{1,0:T(8,128)S(1)}, f32[1,2048]{1,0:T...) custom-call(s32[2]{0:T(128)S(1)} %pad_add_fusion.refs_0_, ...), custom_call_target="tpu_custom_call" | custom-call | flops 48399998976 | bytes 44000000 | tf_op jit(solution)/shard_map/mlp/pallas_call | solution.py:514
  102.1 1.4 collective-permute-start.24
  106.4 24.0 %attn_bwd.1 = (bf16[1792,1536]{1,0:T(8,128)(2,1)S(1)}, f32[24,512]{1,0:T(8,128)}, bf16[4,224,128]{2,1,0:T(8,128)(2,1)S(1)}, bf16[4,224,128]{2,1,0:T(8,128)(2,1)S...) custom-call(s32[2]{0:T(128)S(1)} %pad_add_fusion.refs_0_, ...), custom_call_target="tpu_custom_call" | custom-call | flops 32999999488 | bytes 30000000 | tf_op jit(solution)/shard_map/attn_bwd/pallas_call | solution.py:659
  130.4 1.4 collective-permute-done.25
  133.1 3.5 %collective-permute-start.36 = (bf16[576,128]{1,0:T(8,128)(2,1)S(1)}, bf16[576,128]{1,0:T(8,128)(2,1)S(1)}, u32[]{:S(2)}, u32[]{:S(2)}) collective-permute-start(bf16[576,128]{1,0:T(8,128)(2,1)S(1)} %slice_bitcast_fusion), channel_id=1, source_target_pairs={{0,24},{8,16},{16,8},{24,0},{1,25},{9,17},{17,9},{25,1},{2,26},{10... | collective-permute-start | bytes 442376 | tf_op jit(solution)/shard_map/ppermute | solution.py:795
  139.0 1.6 collective-permute-start.33
  140.7 2.3 %collective-permute-start.35 = (bf16[576,128]{1,0:T(8,128)(2,1)S(1)}, bf16[576,128]{1,0:T(8,128)(2,1)S(1)}, u32[]{:S(2)}, u32[]{:S(2)}) collective-permute-start(bf16[576,128]{1,0:T(8,128)(2,1)S(1)} %get-tuple-element.136), channel_id=1, source_target_pairs={{0,16},{8,24},{16,0},{24,8},{1,17},{9,25},{17,1},{25,9},{2,18},{10... | collective-permute-start | bytes 442376 | tf_op jit(solution)/shard_map/ppermute | solution.py:795
  142.9 7.4 %input_bwd.1 = bf16[16,100,512]{2,1,0:T(8,128)(2,1)S(1)} custom-call(s32[2]{0:T(128)S(1)} %pad_add_fusion.refs_0_, bf16[16,100,512]{2,1,0:T(8,128)(2,1)S(1)} %copy-done.1, bf16[1792,1536]{1,0:T(8,128)(2,1)S(1)} %get-tuple-element.92.refs_2_, f32[1792,512]{1,0:T(8,128)S(1)} %copy-done.3, f32[8,512]{1,0:T(8,128)S(1)} %get-tuple-element.110.refs_13_.refs_7_.refs_4_, ...), custom_call_target="tpu_custom_call" | custom-call | flops 11000000512 | bytes 10000000 | tf_op jit(solution)/shard_map/input_bwd/pallas_call | solution.py:712
  150.9 2.4 %collective-permute-start.39 = (bf16[352,128]{1,0:T(8,128)(2,1)S(1)}, bf16[352,128]{1,0:T(8,128)(2,1)S(1)}, u32[]{:S(2)}, u32[]{:S(2)}) collective-permute-start(bf16[352,128]{1,0:T(8,128)(2,1)S(1)} %get-tuple-element.141), channel_id=1, source_target_pairs={{0,24},{8,16},{16,8},{24,0},{1,25},{9,17},{17,9},{25,1},{2,26},{10... | collective-permute-start | bytes 270344 | tf_op jit(solution)/shard_map/ppermute | solution.py:795
  155.3 1.7 %copy.24 = bf16[16,100,512]{2,0,1:T(8,128)(2,1)} copy(bf16[16,100,512]{2,1,0:T(8,128)(2,1)S(1)} %copy-done.13) | data formatting | bytes 3276800
  157.0 1.7 %copy.25 = bf16[16,100,512]{2,0,1:T(8,128)(2,1)} copy(bf16[16,100,512]{2,1,0:T(8,128)(2,1)S(1)} %input_bwd.1) | data formatting | bytes 3276800
  159.7 1.6 collective-permute-done.38.refs_7_
  (123 shorter events, 25.5 us)
Async XLA Ops:
  2.2 11.2 %collective-permute-start.2 = (bf16[224,128]{1,0:T(8,128)(2,1)}, bf16[224,128]{1,0:T(8,128)(2,1)S(1)}, u32[]{:S(2)}, u32[]{:S(2)}) collective-permute-start(bf16[224,128]{1,0:T(8,128)(2,1)} %pack.2), channel_id=1, source_target_pairs={{0,24},{8,16},{16,8},{24,0},{1,25},{9,17},{17,9},{25,1},{2,26},{10... | collective-permute-start | bytes 172040 | tf_op jit(solution)/shard_map/ppermute | solution.py:795
  9.5 9.0 %collective-permute-start.12 = (bf16[9,64,128]{2,1,0:T(8,128)(2,1)}, bf16[9,64,128]{2,1,0:T(8,128)(2,1)S(1)}, u32[]{:S(2)}, u32[]{:S(2)}) collective-permute-start(bf16[9,64,128]{2,1,0:T(8,128)(2,1)} %pack.3), channel_id=1, source_target_pairs={{0,24},{8,16},{16,8},{24,0},{1,25},{9,17},{17,9},{25,1},{2,26},{10... | collective-permute-start | bytes 442376 | tf_op jit(solution)/shard_map/ppermute | solution.py:795
  13.3 11.9 %collective-permute-start.11 = (bf16[9,64,128]{2,1,0:T(8,128)(2,1)}, bf16[9,64,128]{2,1,0:T(8,128)(2,1)S(1)}, u32[]{:S(2)}, u32[]{:S(2)}) collective-permute-start(bf16[9,64,128]{2,1,0:T(8,128)(2,1)} %pack.3), channel_id=1, source_target_pairs={{0,16},{8,24},{16,0},{24,8},{1,17},{9,25},{17,1},{25,9},{2,18},{10... | collective-permute-start | bytes 442376 | tf_op jit(solution)/shard_map/ppermute | solution.py:795
  13.4 13.2 %collective-permute-start.10 = (bf16[9,64,128]{2,1,0:T(8,128)(2,1)}, bf16[9,64,128]{2,1,0:T(8,128)(2,1)S(1)}, u32[]{:S(2)}, u32[]{:S(2)}) collective-permute-start(bf16[9,64,128]{2,1,0:T(8,128)(2,1)} %pack.3), channel_id=1, source_target_pairs={{0,8},{8,0},{16,24},{24,16},{1,9},{9,1},{17,25},{25,17},{2,10},{10... | collective-permute-start | bytes 442376 | tf_op jit(solution)/shard_map/ppermute | solution.py:795
  14.1 11.1 %collective-permute-start.8 = (bf16[4,224,128]{2,1,0:T(8,128)(2,1)S(1)}, bf16[4,224,128]{2,1,0:T(8,128)(2,1)S(1)}, u32[]{:S(2)}, u32[]{:S(2)}) collective-permute-start(bf16[4,224,128]{2,1,0:T(8,128)(2,1)S(1)} %pad_maximum_fusion.1.refs_3_.refs_11_.refs_5_), channel_id=1, source_target_pairs={{0,6},{1,7},{2,4},{3,5},{4,2},{5,3},{6,0},{7,1},{8,14},{9,15},{10,... | collective-permute-start | bytes 688136 | tf_op jit(solution)/shard_map/ppermute | solution.py:795
  16.8 9.2 %collective-permute-start.6 = (bf16[4,224,128]{2,1,0:T(8,128)(2,1)S(1)}, bf16[4,224,128]{2,1,0:T(8,128)(2,1)S(1)}, u32[]{:S(2)}, u32[]{:S(2)}) collective-permute-start(bf16[4,224,128]{2,1,0:T(8,128)(2,1)S(1)} %pad_maximum_fusion.1.refs_3_.refs_11_.refs_5_), channel_id=1, source_target_pairs={{0,4},{1,5},{2,6},{3,7},{4,0},{5,1},{6,2},{7,3},{8,12},{9,13},{10,... | collective-permute-start | bytes 688136 | tf_op jit(solution)/shard_map/ppermute | solution.py:795
  18.5 7.7 %collective-permute-start.4 = (bf16[4,224,128]{2,1,0:T(8,128)(2,1)S(1)}, bf16[4,224,128]{2,1,0:T(8,128)(2,1)S(1)}, u32[]{:S(2)}, u32[]{:S(2)}) collective-permute-start(bf16[4,224,128]{2,1,0:T(8,128)(2,1)S(1)} %pad_maximum_fusion.1.refs_3_.refs_11_.refs_5_), channel_id=1, source_target_pairs={{0,2},{1,3},{2,0},{3,1},{4,6},{5,7},{6,4},{7,5},{8,10},{9,11},{10,... | collective-permute-start | bytes 688136 | tf_op jit(solution)/shard_map/ppermute | solution.py:795
  26.6 27.6 %collective-permute-start.16 = (bf16[4,9,64,128]{3,2,1,0:T(8,128)(2,1)S(1)}, bf16[4,9,64,128]{3,2,1,0:T(8,128)(2,1)S(1)}, u32[]{:S(2)}, u32[]{:S(2)}) collective-permute-start(bf16[4,9,64,128]{3,2,1,0:T(8,128)(2,1)S(1)} %pad_maximum_fusion.refs_5_), channel_id=1, source_target_pairs={{0,6},{1,7},{2,4},{3,5},{4,2},{5,3},{6,0},{7,1},{8,14},{9,15},{10,... | collective-permute-start | bytes 1769480 | tf_op jit(solution)/shard_map/ppermute | solution.py:795
  28.9 26.7 %collective-permute-start.15 = (bf16[4,9,64,128]{3,2,1,0:T(8,128)(2,1)S(1)}, bf16[4,9,64,128]{3,2,1,0:T(8,128)(2,1)S(1)}, u32[]{:S(2)}, u32[]{:S(2)}) collective-permute-start(bf16[4,9,64,128]{3,2,1,0:T(8,128)(2,1)S(1)} %pad_maximum_fusion.refs_5_), channel_id=1, source_target_pairs={{0,4},{1,5},{2,6},{3,7},{4,0},{5,1},{6,2},{7,3},{8,12},{9,13},{10,... | collective-permute-start | bytes 1769480 | tf_op jit(solution)/shard_map/ppermute | solution.py:795
  29.6 26.0 %collective-permute-start.14 = (bf16[4,9,64,128]{3,2,1,0:T(8,128)(2,1)S(1)}, bf16[4,9,64,128]{3,2,1,0:T(8,128)(2,1)S(1)}, u32[]{:S(2)}, u32[]{:S(2)}) collective-permute-start(bf16[4,9,64,128]{3,2,1,0:T(8,128)(2,1)S(1)} %pad_maximum_fusion.refs_5_), channel_id=1, source_target_pairs={{0,2},{1,3},{2,0},{3,1},{4,6},{5,7},{6,4},{7,5},{8,10},{9,11},{10,... | collective-permute-start | bytes 1769480 | tf_op jit(solution)/shard_map/ppermute | solution.py:795
  30.2 28.8 %collective-permute-start.13 = (bf16[4,9,64,128]{3,2,1,0:T(8,128)(2,1)S(1)}, bf16[4,9,64,128]{3,2,1,0:T(8,128)(2,1)S(1)}, u32[]{:S(2)}, u32[]{:S(2)}) collective-permute-start(bf16[4,9,64,128]{3,2,1,0:T(8,128)(2,1)S(1)} %pad_maximum_fusion.refs_5_), channel_id=1, source_target_pairs={{0,1},{1,0},{2,3},{3,2},{4,5},{5,4},{6,7},{7,6},{8,9},{9,8},{10,11... | collective-permute-start | bytes 1769480 | tf_op jit(solution)/shard_map/ppermute | solution.py:795
  102.1 28.2 %collective-permute-start.24 = (bf16[4,576,128]{2,1,0:T(8,128)(2,1)S(1)}, bf16[4,576,128]{2,1,0:T(8,128)(2,1)S(1)}, u32[]{:S(2)}, u32[]{:S(2)}) collective-permute-start(bf16[4,576,128]{2,1,0:T(8,128)(2,1)S(1)} %add_convert_fusion.3), channel_id=1, source_target_pairs={{0,2},{1,3},{2,0},{3,1},{4,6},{5,7},{6,4},{7,5},{8,10},{9,11},{10,... | collective-permute-start | bytes 1769480 | tf_op jit(solution)/shard_map/ppermute | solution.py:795
  103.7 28.0 %collective-permute-start.25 = (bf16[4,576,128]{2,1,0:T(8,128)(2,1)S(1)}, bf16[4,576,128]{2,1,0:T(8,128)(2,1)S(1)}, u32[]{:S(2)}, u32[]{:S(2)}) collective-permute-start(bf16[4,576,128]{2,1,0:T(8,128)(2,1)S(1)} %add_convert_fusion.2), channel_id=1, source_target_pairs={{0,4},{1,5},{2,6},{3,7},{4,0},{5,1},{6,2},{7,3},{8,12},{9,13},{10,... | collective-permute-start | bytes 1769480 | tf_op jit(solution)/shard_map/ppermute | solution.py:795
  104.9 26.8 %collective-permute-start.26 = (bf16[4,576,128]{2,1,0:T(8,128)(2,1)S(1)}, bf16[4,576,128]{2,1,0:T(8,128)(2,1)S(1)}, u32[]{:S(2)}, u32[]{:S(2)}) collective-permute-start(bf16[4,576,128]{2,1,0:T(8,128)(2,1)S(1)} %add_convert_fusion.1), channel_id=1, source_target_pairs={{0,6},{1,7},{2,4},{3,5},{4,2},{5,3},{6,0},{7,1},{8,14},{9,15},{10,... | collective-permute-start | bytes 1769480 | tf_op jit(solution)/shard_map/ppermute | solution.py:795
  131.8 8.8 %collective-permute-start.27 = (bf16[4,224,128]{2,1,0:T(8,128)(2,1)S(1)}, bf16[4,224,128]{2,1,0:T(8,128)(2,1)S(1)}, u32[]{:S(2)}, u32[]{:S(2)}) collective-permute-start(bf16[4,224,128]{2,1,0:T(8,128)(2,1)S(1)} %get-tuple-element.103), channel_id=1, source_target_pairs={{0,1},{1,0},{2,3},{3,2},{4,5},{5,4},{6,7},{7,6},{8,9},{9,8},{10,11... | collective-permute-start | bytes 688136 | tf_op jit(solution)/shard_map/ppermute | solution.py:795
  133.1 21.1 %collective-permute-start.36 = (bf16[576,128]{1,0:T(8,128)(2,1)S(1)}, bf16[576,128]{1,0:T(8,128)(2,1)S(1)}, u32[]{:S(2)}, u32[]{:S(2)}) collective-permute-start(bf16[576,128]{1,0:T(8,128)(2,1)S(1)} %slice_bitcast_fusion), channel_id=1, source_target_pairs={{0,24},{8,16},{16,8},{24,0},{1,25},{9,17},{17,9},{25,1},{2,26},{10... | collective-permute-start | bytes 442376 | tf_op jit(solution)/shard_map/ppermute | solution.py:795
  136.7 13.6 %collective-permute-start.31 = (bf16[4,224,128]{2,1,0:T(8,128)(2,1)S(1)}, bf16[4,224,128]{2,1,0:T(8,128)(2,1)S(1)}, u32[]{:S(2)}, u32[]{:S(2)}) collective-permute-start(bf16[4,224,128]{2,1,0:T(8,128)(2,1)S(1)} %add_convert_fusion.8), channel_id=1, source_target_pairs={{0,2},{1,3},{2,0},{3,1},{4,6},{5,7},{6,4},{7,5},{8,10},{9,11},{10,... | collective-permute-start | bytes 688136 | tf_op jit(solution)/shard_map/ppermute | solution.py:795
  137.8 12.9 %collective-permute-start.32 = (bf16[4,224,128]{2,1,0:T(8,128)(2,1)S(1)}, bf16[4,224,128]{2,1,0:T(8,128)(2,1)S(1)}, u32[]{:S(2)}, u32[]{:S(2)}) collective-permute-start(bf16[4,224,128]{2,1,0:T(8,128)(2,1)S(1)} %add_convert_fusion.7), channel_id=1, source_target_pairs={{0,4},{1,5},{2,6},{3,7},{4,0},{5,1},{6,2},{7,3},{8,12},{9,13},{10,... | collective-permute-start | bytes 688136 | tf_op jit(solution)/shard_map/ppermute | solution.py:795
  139.0 11.7 %collective-permute-start.33 = (bf16[4,224,128]{2,1,0:T(8,128)(2,1)S(1)}, bf16[4,224,128]{2,1,0:T(8,128)(2,1)S(1)}, u32[]{:S(2)}, u32[]{:S(2)}) collective-permute-start(bf16[4,224,128]{2,1,0:T(8,128)(2,1)S(1)} %add_convert_fusion.6), channel_id=1, source_target_pairs={{0,6},{1,7},{2,4},{3,5},{4,2},{5,3},{6,0},{7,1},{8,14},{9,15},{10,... | collective-permute-start | bytes 688136 | tf_op jit(solution)/shard_map/ppermute | solution.py:795
  140.7 18.0 %collective-permute-start.35 = (bf16[576,128]{1,0:T(8,128)(2,1)S(1)}, bf16[576,128]{1,0:T(8,128)(2,1)S(1)}, u32[]{:S(2)}, u32[]{:S(2)}) collective-permute-start(bf16[576,128]{1,0:T(8,128)(2,1)S(1)} %get-tuple-element.136), channel_id=1, source_target_pairs={{0,16},{8,24},{16,0},{24,8},{1,17},{9,25},{17,1},{25,9},{2,18},{10... | collective-permute-start | bytes 442376 | tf_op jit(solution)/shard_map/ppermute | solution.py:795
  150.4 9.4 %collective-permute-start.34 = (bf16[576,128]{1,0:T(8,128)(2,1)S(1)}, bf16[576,128]{1,0:T(8,128)(2,1)S(1)}, u32[]{:S(2)}, u32[]{:S(2)}) collective-permute-start(bf16[576,128]{1,0:T(8,128)(2,1)S(1)} %get-tuple-element.137), channel_id=1, source_target_pairs={{0,8},{8,0},{16,24},{24,16},{1,9},{9,1},{17,25},{25,17},{2,10},{10... | collective-permute-start | bytes 442376 | tf_op jit(solution)/shard_map/ppermute | solution.py:795
  150.9 8.9 %collective-permute-start.39 = (bf16[352,128]{1,0:T(8,128)(2,1)S(1)}, bf16[352,128]{1,0:T(8,128)(2,1)S(1)}, u32[]{:S(2)}, u32[]{:S(2)}) collective-permute-start(bf16[352,128]{1,0:T(8,128)(2,1)S(1)} %get-tuple-element.141), channel_id=1, source_target_pairs={{0,24},{8,16},{16,8},{24,0},{1,25},{9,17},{17,9},{25,1},{2,26},{10... | collective-permute-start | bytes 270344 | tf_op jit(solution)/shard_map/ppermute | solution.py:795
  153.2 8.1 %collective-permute-start.38 = (bf16[352,128]{1,0:T(8,128)(2,1)S(1)}, bf16[352,128]{1,0:T(8,128)(2,1)S(1)}, u32[]{:S(2)}, u32[]{:S(2)}) collective-permute-start(bf16[352,128]{1,0:T(8,128)(2,1)S(1)} %get-tuple-element.142), channel_id=1, source_target_pairs={{0,16},{8,24},{16,0},{24,8},{1,17},{9,25},{17,1},{25,9},{2,18},{10... | collective-permute-start | bytes 270344 | tf_op jit(solution)/shard_map/ppermute | solution.py:795
  154.2 7.2 %collective-permute-start.37 = (bf16[352,128]{1,0:T(8,128)(2,1)S(1)}, bf16[352,128]{1,0:T(8,128)(2,1)S(1)}, u32[]{:S(2)}, u32[]{:S(2)}) collective-permute-start(bf16[352,128]{1,0:T(8,128)(2,1)S(1)} %get-tuple-element.143), channel_id=1, source_target_pairs={{0,8},{8,0},{16,24},{24,16},{1,9},{9,1},{17,25},{25,17},{2,10},{10... | collective-permute-start | bytes 270344 | tf_op jit(solution)/shard_map/ppermute | solution.py:795
  (34 other events, 218.5 us)
